TPU v7x, 32 devices: a whole 2x2x4 slice. The times are simulated.
32 devices in a mesh: fsdp: 4 (over y, x), ctx: 8 (over z, core).
Axes of the slice: x: 2, y: 2, z: 4, core: 2. Of those that a mesh axis runs over, the one named last changes fastest.
Arguments:
- block_in: bfloat16 [4096, 1024], P(('fsdp', 'ctx')), may hold values from -6 to 6
- seq_lengths: int32 [4, 3], P('fsdp'), may hold values from 192 to 512, as said below
- norm_gain: bfloat16 [2, 1024], P(None, 'fsdp'), may hold values from 0.099609375 to 1.8984375
- in_proj: bfloat16 [2, 1024, 3352], P(None, 'fsdp'), may hold values from -0.1875 to 0.1875
- conv_weight: bfloat16 [2, 1792, 4], P(None, 'fsdp'), may hold values from -3 to 3
- conv_bias: bfloat16 [2, 1792], P(None, 'fsdp'), may hold values from -3 to 3
- dt_bias: bfloat16 [2, 24], P(None, 'fsdp'), may hold values from -3 to -1
- decay_log: bfloat16 [2, 24], P(None, 'fsdp'), may hold values from -10 to -1
- skip_gain: bfloat16 [2, 24], P(None, 'fsdp'), may hold values from 0.5 to 1.5
- mixer_gain: bfloat16 [2, 1536], P(None, 'fsdp'), may hold values from 0.099609375 to 1.8984375
- out_proj: bfloat16 [2, 1536, 1024], P(None, 'fsdp'), may hold values from -0.15625 to 0.15625
- query_proj: bfloat16 [2, 1024, 1024], P(None, 'fsdp'), may hold values from -0.1875 to 0.1875
- key_proj: bfloat16 [2, 1024, 256], P(None, 'fsdp'), may hold values from -0.1875 to 0.1875
- value_proj: bfloat16 [2, 1024, 256], P(None, 'fsdp'), may hold values from -0.1875 to 0.1875
- attn_proj: bfloat16 [2, 1024, 1024], P(None, 'fsdp'), may hold values from -1.5 to 1.5
- ffn_gain: bfloat16 [2, 1024], P(None, 'fsdp'), may hold values from 0.099609375 to 1.8984375
- gate_proj: bfloat16 [2, 1024, 2048], P(None, 'fsdp'), may hold values from -0.1875 to 0.1875
- up_proj: bfloat16 [2, 1024, 2048], P(None, 'fsdp'), may hold values from -0.1875 to 0.1875
- down_proj: bfloat16 [2, 2048, 1024], P(None, 'fsdp'), may hold values from -0.125 to 0.125
- out_grad: bfloat16 [4096, 1024], P(('fsdp', 'ctx')), may hold values from -6 to 6
Outputs:
- block_out: bfloat16 [4096, 1024], P(('fsdp', 'ctx'))
- in_grad: bfloat16 [4096, 1024], P(('fsdp', 'ctx'))
- grad_norm_gain: float32 [2, 1024], P(None, 'fsdp')
- grad_in_proj: float32 [2, 1024, 3352], P(None, 'fsdp')
- grad_conv_weight: float32 [2, 1792, 4], P(None, 'fsdp')
- grad_conv_bias: float32 [2, 1792], P(None, 'fsdp')
- grad_dt_bias: float32 [2, 24], P(None, 'fsdp')
- grad_decay_log: float32 [2, 24], P(None, 'fsdp')
- grad_skip_gain: float32 [2, 24], P(None, 'fsdp')
- grad_mixer_gain: float32 [2, 1536], P(None, 'fsdp')
- grad_out_proj: float32 [2, 1536, 1024], P(None, 'fsdp')
- grad_query_proj: float32 [2, 1024, 1024], P(None, 'fsdp')
- grad_key_proj: float32 [2, 1024, 256], P(None, 'fsdp')
- grad_value_proj: float32 [2, 1024, 256], P(None, 'fsdp')
- grad_attn_proj: float32 [2, 1024, 1024], P(None, 'fsdp')
- grad_ffn_gain: float32 [2, 1024], P(None, 'fsdp')
- grad_gate_proj: float32 [2, 1024, 2048], P(None, 'fsdp')
- grad_up_proj: float32 [2, 1024, 2048], P(None, 'fsdp')
- grad_down_proj: float32 [2, 2048, 1024], P(None, 'fsdp')
Inputs may be any that keep to these rules, and one draw needn't show every extreme that they name: `seq_lengths`: row f lists the lengths of the 3 sequences of fsdp index f in the order in which their pieces lie on every ctx device; each length is a multiple of the number of ctx devices, a row sums to 1024, and the longest of every row is exactly half of that.
All inputs are finite; a program needn't handle non-finite values.
Results may differ from a plain program's by a relative error of at most 0.039.
Values may be sent and summed in bfloat16 or wider, within the bound.
No kernel may reach another device: no remote copies, remote signals or barrier semaphores. Data moves between devices by JAX's collectives and lax.ppermute only.
A program may use at most 448 MiB of HBM per device.

v0:
```python
from functools import partial
import math

import jax
import jax.numpy as jnp
from jax import lax
from jax.sharding import PartitionSpec as P

QH = 8
KVH = 2
HD = 128
MH = 24
MP = 64
NS = 128
CONV = 4
LAYERS = 2
SEQS = 3
DSSM = 1536
CONVCH = 1792


EPSILON = 1e-05
ROPE_BASE = 100000000000.0
MASKED = -1e30
HIGHEST = lax.Precision.HIGHEST


def passed_along(shard, axis, by):
    size = lax.axis_size(axis)
    pairs = [(i, i + by) for i in range(size) if 0 <= i + by < size]
    return lax.ppermute(shard, axis, pairs)


def carried_in(shard, axis, combine, identity):
    size, index = (lax.axis_size(axis), lax.axis_index(axis))
    everything = jax.tree.map(lambda part: lax.all_gather(part, axis), shard)
    start = jax.tree.map(
        lambda part, zero: jnp.broadcast_to(jnp.asarray(zero, part.dtype), part.shape),
        shard,
        identity,
    )

    def step(k, before):
        reached = k < index
        new = combine(before, jax.tree.map(lambda part: part[k], everything))
        return jax.tree.map(lambda a, b: jnp.where(reached, a, b), new, before)

    return lax.fori_loop(0, size, step, start)


def carried_in_2(shard, axis, combine, identity):
    size, index = (lax.axis_size(axis), lax.axis_index(axis))
    everything = jax.tree.map(
        lambda part, kind: lax.all_gather(part.astype(kind), axis),
        shard,
        jax.tree.map(lambda a: jnp.bfloat16 if a.dtype == jnp.float32 else a.dtype, shard),
    )
    start = jax.tree.map(
        lambda part, zero: jnp.broadcast_to(jnp.asarray(zero, part.dtype), part.shape),
        shard,
        identity,
    )

    def step(k, before):
        at = size - 1 - k
        reached = at > index
        new = combine(
            before, jax.tree.map(lambda part, own: part[at].astype(own.dtype), everything, shard)
        )
        return jax.tree.map(lambda a, b: jnp.where(reached, a, b), new, before)

    return lax.fori_loop(0, size, step, start)


def round_value(values):
    rounded = lax.optimization_barrier(values.astype(jnp.bfloat16)).astype(jnp.float32)
    return values + lax.stop_gradient(rounded - values)


def round_grad(values):
    rounded = values.astype(jnp.bfloat16).astype(jnp.float32)
    return lax.stop_gradient(values) + (rounded - lax.stop_gradient(rounded))


def product(matrix_a, matrix_b):
    return jnp.dot(matrix_a, matrix_b, preferred_element_type=jnp.float32)


def rms_scale(values, gain_vec):
    return (
        values * lax.rsqrt(jnp.mean(values * values, axis=-1, keepdims=True) + EPSILON) * gain_vec
    )


def layout(pieces, device, local_rows):
    piece_ends = jnp.cumsum(pieces)
    piece_starts = piece_ends - pieces
    member = (local_rows[:, None] >= piece_starts[None, :]) & (
        local_rows[:, None] < piece_ends[None, :]
    )
    numbers = jnp.arange(SEQS, dtype=jnp.int32)
    sequence = jnp.sum(jnp.where(member, numbers[None, :], 0), axis=1)
    begin_row = jnp.sum(jnp.where(member, piece_starts[None, :], 0), axis=1)
    piece_len = jnp.sum(jnp.where(member, pieces[None, :], 0), axis=1)
    position = device * piece_len + local_rows - begin_row
    return (member, sequence, position, begin_row, piece_ends)


def rotate(vectors, position):
    half_dim = vectors.shape[-1] // 2
    frequency = jnp.exp(-math.log(ROPE_BASE) * jnp.arange(half_dim, dtype=jnp.float32) / half_dim)
    angles = position.astype(jnp.float32)[:, None] * frequency[None, :]
    cosine = jnp.cos(angles)[:, None, :]
    sine_val = jnp.sin(angles)[:, None, :]
    first_half = vectors[..., :half_dim]
    second_half = vectors[..., half_dim:]
    return jnp.concatenate(
        [
            first_half * cosine - second_half * sine_val,
            second_half * cosine + first_half * sine_val,
        ],
        axis=-1,
    )


def take_tails(projected, piece_ends):
    offsets = jnp.arange(CONV - 1, dtype=jnp.int32)
    tail_rows = piece_ends[:, None] - (CONV - 1) + offsets[None, :]
    return projected[:, DSSM : DSSM + CONVCH][tail_rows]


def piece_front(hidden, norm_gain, in_proj, query_proj, key_proj, value_proj, position, piece_ends):
    row_count = hidden.shape[0]
    normed = round_value(rms_scale(hidden, norm_gain))
    projected = round_grad(round_value(product(normed, in_proj)))
    queries = round_grad(
        round_value(
            rotate(product(normed, query_proj).reshape(row_count, QH, HD), position).reshape(
                row_count, QH * HD
            )
        )
    )
    keys_out = round_grad(
        round_value(
            rotate(product(normed, key_proj).reshape(row_count, KVH, HD), position).reshape(
                row_count, KVH * HD
            )
        )
    )
    values_out = round_grad(round_value(product(normed, value_proj)))
    return (projected, queries, keys_out, values_out, take_tails(projected, piece_ends))


def scan_block(
    projected,
    previous,
    conv_weight,
    conv_bias,
    dt_bias,
    decay_log,
    skip_gain,
    member,
    sequence,
    begin_row,
    piece_ends,
):
    row_count = projected.shape[0]
    row_ids = jnp.arange(row_count, dtype=jnp.int32)
    conv_in = projected[:, DSSM : DSSM + CONVCH]
    conv_sum = conv_bias[None, :] + conv_weight[:, CONV - 1][None, :] * conv_in
    for lag_rows in range(1, CONV):
        shifted = jnp.concatenate(
            [jnp.zeros((lag_rows, CONVCH), conv_in.dtype), conv_in[: row_count - lag_rows]], axis=0
        )
        before = begin_row - (row_ids - lag_rows)
        fetched = previous[sequence, jnp.clip(CONV - 1 - before, 0, CONV - 2)]
        conv_sum = conv_sum + conv_weight[:, CONV - 1 - lag_rows][None, :] * jnp.where(
            (before > 0)[:, None], fetched, shifted
        )
    conv_out = round_value(jax.nn.silu(conv_sum))
    inputs = conv_out[:, :DSSM].reshape(row_count, MH, MP)
    b_mat = conv_out[:, DSSM : DSSM + NS]
    c_mat = conv_out[:, DSSM + NS :]
    step_dt = jax.nn.softplus(projected[:, DSSM + CONVCH :] + dt_bias[None, :])
    log_decay = -step_dt * jnp.exp(decay_log)[None, :]
    running = jnp.cumsum(log_decay, axis=0)
    seg_cum = running - (running - log_decay)[begin_row]
    causal = (sequence[:, None] == sequence[None, :]) & (row_ids[:, None] >= row_ids[None, :])
    gap_log = jnp.where(causal[None], running.T[:, :, None] - running.T[:, None, :], MASKED)
    kernel = (
        jnp.exp(gap_log) * jnp.dot(c_mat, b_mat.T, precision=HIGHEST)[None] * step_dt.T[:, None, :]
    )
    y_part = (
        jnp.einsum("hij,jhp->ihp", kernel, inputs, precision=HIGHEST)
        + skip_gain[None, :, None] * inputs
    )
    seg_end = seg_cum[piece_ends - 1]
    decay_total = jnp.exp(seg_end)
    weight_end = jnp.exp(seg_end[sequence] - seg_cum) * step_dt
    member_f = member.astype(jnp.float32)
    end_state = jnp.einsum(
        "js,jh,jhp,jn->shpn", member_f, weight_end, inputs, b_mat, precision=HIGHEST
    )
    return (y_part, c_mat, seg_cum, decay_total, end_state)


def mixer_out(y_part, c_mat, seg_cum, state_in, projected, mixer_gain, out_proj, member):
    row_count = y_part.shape[0]
    member_f = member.astype(jnp.float32)
    carried = jnp.einsum("in,shpn->sihp", c_mat, state_in, precision=HIGHEST)
    carried = (
        jnp.einsum("is,sihp->ihp", member_f, carried, precision=HIGHEST)
        * jnp.exp(seg_cum)[:, :, None]
    )
    gated = (y_part + carried).reshape(row_count, DSSM) * jax.nn.silu(projected[:, :DSSM])
    return round_grad(product(round_value(rms_scale(gated, mixer_gain)), out_proj))


def piece_back(hidden, mamba_out, attended, attn_proj, ffn_gain, gate_proj, up_proj, down_proj):
    mid_sum = hidden + mamba_out + round_grad(product(attended, attn_proj))
    normed = round_value(rms_scale(mid_sum, ffn_gain))
    gate_val = round_grad(product(normed, gate_proj))
    up_val = round_grad(product(normed, up_proj))
    act_val = round_value(jax.nn.silu(gate_val) * up_val)
    return mid_sum + round_grad(product(act_val, down_proj))


def chain_states(earlier, later):
    return (earlier[0] * later[0], later[0][:, :, None, None] * earlier[1] + later[1])


def block_scores(q_heads, key_blk, begin_key, score_meta):
    pieces, sequence, position = score_meta
    row_count = q_heads.shape[0]
    count_keys = key_blk.shape[0]
    key_rows = begin_key + jnp.arange(count_keys, dtype=jnp.int32)
    _, key_seq, key_pos, _, _ = layout(pieces, key_rows // row_count, key_rows % row_count)
    allowed = (sequence[:, None] == key_seq[None, :]) & (key_pos[None, :] <= position[:, None])
    key_heads = key_blk.astype(jnp.float32).reshape(count_keys, KVH, HD)
    scores = jnp.einsum("qkgd,nkd->kgqn", q_heads, key_heads) * HD ** (-0.5)
    return (scores, allowed)


def attend_step(fold_carry, kv_piece, begin_key, q_heads, score_meta):
    top_score, total_w, summed = fold_carry
    key_blk, value_blk = kv_piece
    scores, allowed = block_scores(q_heads, key_blk, begin_key, score_meta)
    masked = jnp.where(allowed[None, None], scores, MASKED)
    new_top = jnp.maximum(top_score, jnp.max(masked, axis=-1))
    prob_blk = jnp.where(allowed[None, None], jnp.exp(masked - new_top[..., None]), 0.0)
    value_heads = value_blk.astype(jnp.float32).reshape(value_blk.shape[0], KVH, HD)
    total_w = jnp.sum(prob_blk, axis=-1)
    summed = jnp.einsum("kgqn,nkd->kgqd", prob_blk, value_heads)
    return (new_top, total_w, summed)


def attention_back(
    q_heads, keys_whole, values_whole, grad_att, attended_raw, log_total, score_meta
):
    row_count = q_heads.shape[0]
    group_size = QH // KVH
    grad_heads = grad_att.reshape(row_count, KVH, group_size, HD)
    delta_rows = jnp.einsum(
        "qkgd,qkgd->kgq", grad_heads, attended_raw.reshape(row_count, KVH, group_size, HD)
    )
    total_keys = keys_whole.shape[0]
    key_block = min(512, total_keys)
    block_starts = jnp.arange(total_keys // key_block, dtype=jnp.int32) * key_block

    def key_step(grad_q, scan_items):
        key_blk, value_blk, begin_key = scan_items
        scores, allowed = block_scores(q_heads, key_blk, begin_key, score_meta)
        prob_blk = jnp.where(allowed[None, None], jnp.exp(scores - log_total[..., None]), 0.0)
        key_heads = key_blk.astype(jnp.float32).reshape(key_block, KVH, HD)
        value_heads = value_blk.astype(jnp.float32).reshape(key_block, KVH, HD)
        grad_prob = jnp.einsum("qkgd,nkd->kgqn", grad_heads, value_heads)
        grad_score = round_value(prob_blk * (grad_prob - delta_rows[..., None])) * HD ** (-0.5)
        grad_q = grad_q + jnp.einsum("kgqn,nkd->qkgd", grad_score, key_heads)
        grad_key = jnp.einsum("kgqn,qkgd->nkd", grad_score, q_heads)
        grad_value = jnp.einsum("kgqn,qkgd->nkd", prob_blk, grad_heads)
        return (
            grad_q,
            (grad_key.reshape(key_block, KVH * HD), grad_value.reshape(key_block, KVH * HD)),
        )

    grad_q, (grad_keys, grad_values) = lax.scan(
        key_step,
        jnp.zeros_like(q_heads),
        (
            keys_whole.reshape(total_keys // key_block, key_block, KVH * HD),
            values_whole.reshape(total_keys // key_block, key_block, KVH * HD),
            block_starts,
        ),
    )
    own_keys, own_values = (
        lax.psum_scatter(
            grad_keys.reshape(total_keys, KVH * HD).astype(jnp.bfloat16),
            "ctx",
            scatter_dimension=0,
            tiled=True,
        ).astype(jnp.float32),
        lax.psum_scatter(
            grad_values.reshape(total_keys, KVH * HD).astype(jnp.bfloat16),
            "ctx",
            scatter_dimension=0,
            tiled=True,
        ).astype(jnp.float32),
    )
    return (grad_q.reshape(row_count, QH * HD), own_keys, own_values)


def gather_layer(shards, layer_idx):
    (
        norm_gain,
        in_proj,
        conv_weight,
        conv_bias,
        dt_bias,
        decay_log,
        skip_gain,
        mixer_gain,
        out_proj,
        query_proj,
        key_proj,
        value_proj,
        attn_proj,
        ffn_gain,
        gate_proj,
        up_proj,
        down_proj,
    ) = shards
    return (
        lax.all_gather(norm_gain[layer_idx], "fsdp", axis=0, tiled=True),
        lax.all_gather(in_proj[layer_idx], "fsdp", axis=0, tiled=True),
        lax.all_gather(conv_weight[layer_idx], "fsdp", axis=0, tiled=True),
        lax.all_gather(conv_bias[layer_idx], "fsdp", axis=0, tiled=True),
        lax.all_gather(dt_bias[layer_idx], "fsdp", axis=0, tiled=True),
        lax.all_gather(decay_log[layer_idx], "fsdp", axis=0, tiled=True),
        lax.all_gather(skip_gain[layer_idx], "fsdp", axis=0, tiled=True),
        lax.all_gather(mixer_gain[layer_idx], "fsdp", axis=0, tiled=True),
        lax.all_gather(out_proj[layer_idx], "fsdp", axis=0, tiled=True),
        lax.all_gather(query_proj[layer_idx], "fsdp", axis=0, tiled=True),
        lax.all_gather(key_proj[layer_idx], "fsdp", axis=0, tiled=True),
        lax.all_gather(value_proj[layer_idx], "fsdp", axis=0, tiled=True),
        lax.all_gather(attn_proj[layer_idx], "fsdp", axis=0, tiled=True),
        lax.all_gather(ffn_gain[layer_idx], "fsdp", axis=0, tiled=True),
        lax.all_gather(gate_proj[layer_idx], "fsdp", axis=0, tiled=True),
        lax.all_gather(up_proj[layer_idx], "fsdp", axis=0, tiled=True),
        lax.all_gather(down_proj[layer_idx], "fsdp", axis=0, tiled=True),
    )


def gather_again(shards, layer_idx):
    (
        norm_gain,
        in_proj,
        conv_weight,
        conv_bias,
        dt_bias,
        decay_log,
        skip_gain,
        mixer_gain,
        out_proj,
        query_proj,
        key_proj,
        value_proj,
        attn_proj,
        ffn_gain,
        gate_proj,
        up_proj,
        down_proj,
    ) = shards
    return (
        lax.all_gather(norm_gain[layer_idx], "fsdp", axis=0, tiled=True),
        lax.all_gather(in_proj[layer_idx], "fsdp", axis=0, tiled=True),
        lax.all_gather(conv_weight[layer_idx], "fsdp", axis=0, tiled=True),
        lax.all_gather(conv_bias[layer_idx], "fsdp", axis=0, tiled=True),
        lax.all_gather(dt_bias[layer_idx], "fsdp", axis=0, tiled=True),
        lax.all_gather(decay_log[layer_idx], "fsdp", axis=0, tiled=True),
        lax.all_gather(skip_gain[layer_idx], "fsdp", axis=0, tiled=True),
        lax.all_gather(mixer_gain[layer_idx], "fsdp", axis=0, tiled=True),
        lax.all_gather(out_proj[layer_idx], "fsdp", axis=0, tiled=True),
        lax.all_gather(query_proj[layer_idx], "fsdp", axis=0, tiled=True),
        lax.all_gather(key_proj[layer_idx], "fsdp", axis=0, tiled=True),
        lax.all_gather(value_proj[layer_idx], "fsdp", axis=0, tiled=True),
        lax.all_gather(attn_proj[layer_idx], "fsdp", axis=0, tiled=True),
        lax.all_gather(ffn_gain[layer_idx], "fsdp", axis=0, tiled=True),
        lax.all_gather(gate_proj[layer_idx], "fsdp", axis=0, tiled=True),
        lax.all_gather(up_proj[layer_idx], "fsdp", axis=0, tiled=True),
        lax.all_gather(down_proj[layer_idx], "fsdp", axis=0, tiled=True),
    )


def reduce_grads(weight_grads):
    (
        g_norm_gain,
        g_in_proj,
        g_conv_weight,
        g_conv_bias,
        g_dt_bias,
        g_decay_log,
        g_skip_gain,
        g_mixer_gain,
        g_out_proj,
        g_query_proj,
        g_key_proj,
        g_value_proj,
        g_attn_proj,
        g_ffn_gain,
        g_gate_proj,
        g_up_proj,
        g_down_proj,
    ) = weight_grads
    parted = (
        lax.psum_scatter(
            g_norm_gain.astype(jnp.bfloat16), "fsdp", scatter_dimension=0, tiled=True
        ).astype(jnp.float32),
        lax.psum_scatter(
            g_in_proj.astype(jnp.bfloat16), "fsdp", scatter_dimension=0, tiled=True
        ).astype(jnp.float32),
        lax.psum_scatter(
            g_conv_weight.astype(jnp.bfloat16), "fsdp", scatter_dimension=0, tiled=True
        ).astype(jnp.float32),
        lax.psum_scatter(
            g_conv_bias.astype(jnp.bfloat16), "fsdp", scatter_dimension=0, tiled=True
        ).astype(jnp.float32),
        lax.psum_scatter(
            g_dt_bias.astype(jnp.bfloat16), "fsdp", scatter_dimension=0, tiled=True
        ).astype(jnp.float32),
        lax.psum_scatter(
            g_decay_log.astype(jnp.bfloat16), "fsdp", scatter_dimension=0, tiled=True
        ).astype(jnp.float32),
        lax.psum_scatter(
            g_skip_gain.astype(jnp.bfloat16), "fsdp", scatter_dimension=0, tiled=True
        ).astype(jnp.float32),
        lax.psum_scatter(
            g_mixer_gain.astype(jnp.bfloat16), "fsdp", scatter_dimension=0, tiled=True
        ).astype(jnp.float32),
        lax.psum_scatter(
            g_out_proj.astype(jnp.bfloat16), "fsdp", scatter_dimension=0, tiled=True
        ).astype(jnp.float32),
        lax.psum_scatter(
            g_query_proj.astype(jnp.bfloat16), "fsdp", scatter_dimension=0, tiled=True
        ).astype(jnp.float32),
        lax.psum_scatter(
            g_key_proj.astype(jnp.bfloat16), "fsdp", scatter_dimension=0, tiled=True
        ).astype(jnp.float32),
        lax.psum_scatter(
            g_value_proj.astype(jnp.bfloat16), "fsdp", scatter_dimension=0, tiled=True
        ).astype(jnp.float32),
        lax.psum_scatter(
            g_attn_proj.astype(jnp.bfloat16), "fsdp", scatter_dimension=0, tiled=True
        ).astype(jnp.float32),
        lax.psum_scatter(
            g_ffn_gain.astype(jnp.bfloat16), "fsdp", scatter_dimension=0, tiled=True
        ).astype(jnp.float32),
        lax.psum_scatter(
            g_gate_proj.astype(jnp.bfloat16), "fsdp", scatter_dimension=0, tiled=True
        ).astype(jnp.float32),
        lax.psum_scatter(
            g_up_proj.astype(jnp.bfloat16), "fsdp", scatter_dimension=0, tiled=True
        ).astype(jnp.float32),
        lax.psum_scatter(
            g_down_proj.astype(jnp.bfloat16), "fsdp", scatter_dimension=0, tiled=True
        ).astype(jnp.float32),
    )
    return (
        lax.psum(parted[0].astype(jnp.bfloat16), "ctx").astype(jnp.float32),
        lax.psum(parted[1].astype(jnp.bfloat16), "ctx").astype(jnp.float32),
        lax.psum(parted[2].astype(jnp.bfloat16), "ctx").astype(jnp.float32),
        lax.psum(parted[3].astype(jnp.bfloat16), "ctx").astype(jnp.float32),
        lax.psum(parted[4].astype(jnp.bfloat16), "ctx").astype(jnp.float32),
        lax.psum(parted[5].astype(jnp.bfloat16), "ctx").astype(jnp.float32),
        lax.psum(parted[6].astype(jnp.bfloat16), "ctx").astype(jnp.float32),
        lax.psum(parted[7].astype(jnp.bfloat16), "ctx").astype(jnp.float32),
        lax.psum(parted[8].astype(jnp.bfloat16), "ctx").astype(jnp.float32),
        lax.psum(parted[9].astype(jnp.bfloat16), "ctx").astype(jnp.float32),
        lax.psum(parted[10].astype(jnp.bfloat16), "ctx").astype(jnp.float32),
        lax.psum(parted[11].astype(jnp.bfloat16), "ctx").astype(jnp.float32),
        lax.psum(parted[12].astype(jnp.bfloat16), "ctx").astype(jnp.float32),
        lax.psum(parted[13].astype(jnp.bfloat16), "ctx").astype(jnp.float32),
        lax.psum(parted[14].astype(jnp.bfloat16), "ctx").astype(jnp.float32),
        lax.psum(parted[15].astype(jnp.bfloat16), "ctx").astype(jnp.float32),
        lax.psum(parted[16].astype(jnp.bfloat16), "ctx").astype(jnp.float32),
    )


def layer_forward(hidden, gathered, layout_meta):
    pieces, sequence, position, member, begin_row, piece_ends = layout_meta
    (
        norm_gain,
        in_proj,
        conv_weight,
        conv_bias,
        dt_bias,
        decay_log,
        skip_gain,
        mixer_gain,
        out_proj,
        query_proj,
        key_proj,
        value_proj,
        attn_proj,
        ffn_gain,
        gate_proj,
        up_proj,
        down_proj,
    ) = tuple((weight_arr.astype(jnp.float32) for weight_arr in gathered))
    row_count = hidden.shape[0]
    group_size = QH // KVH
    projected, queries, keys_out, values_out, tails = piece_front(
        hidden,
        norm_gain,
        in_proj,
        query_proj,
        key_proj,
        value_proj,
        position=position,
        piece_ends=piece_ends,
    )
    previous = passed_along(tails.astype(jnp.bfloat16), "ctx", 1).astype(jnp.float32)
    y_part, c_mat, seg_cum, decay_total, end_state = scan_block(
        projected,
        previous,
        conv_weight,
        conv_bias,
        dt_bias,
        decay_log,
        skip_gain,
        member=member,
        sequence=sequence,
        begin_row=begin_row,
        piece_ends=piece_ends,
    )
    scanned = carried_in(
        (decay_total, end_state),
        "ctx",
        chain_states,
        (jnp.ones_like(decay_total), jnp.zeros_like(end_state)),
    )
    state_in = scanned[1]
    mamba_out = mixer_out(
        y_part, c_mat, seg_cum, state_in, projected, mixer_gain, out_proj, member=member
    )
    q_heads = queries.reshape(row_count, KVH, group_size, HD)
    key_send = keys_out.astype(jnp.bfloat16)
    value_send = values_out.astype(jnp.bfloat16)
    step_fn = partial(attend_step, q_heads=q_heads, score_meta=(pieces, sequence, position))
    fold_init = (
        jnp.full((KVH, group_size, row_count), MASKED, jnp.float32),
        jnp.zeros((KVH, group_size, row_count), jnp.float32),
        jnp.zeros((KVH, group_size, row_count, HD), jnp.float32),
    )
    keys_whole, values_whole = (key_send, value_send)
    top_score, total_w, summed = step_fn(
        fold_init,
        (
            lax.all_gather(key_send, "ctx", axis=0, tiled=True),
            lax.all_gather(value_send, "ctx", axis=0, tiled=True),
        ),
        jnp.int32(0),
    )
    attended_raw = (summed / total_w[..., None]).transpose(2, 0, 1, 3).reshape(row_count, QH * HD)
    log_total = top_score + jnp.log(total_w)
    layer_out = piece_back(
        hidden,
        mamba_out,
        round_value(attended_raw),
        attn_proj,
        ffn_gain,
        gate_proj,
        up_proj,
        down_proj,
    )
    return (
        layer_out,
        (
            previous,
            state_in,
            attended_raw,
            log_total,
            keys_whole,
            values_whole,
            projected,
            queries,
            key_send,
            value_send,
        ),
    )


def layer_backward(grad_out, hidden, gathered, kept, layout_meta):
    pieces, sequence, position, member, begin_row, piece_ends = layout_meta
    (
        norm_gain,
        in_proj,
        conv_weight,
        conv_bias,
        dt_bias,
        decay_log,
        skip_gain,
        mixer_gain,
        out_proj,
        query_proj,
        key_proj,
        value_proj,
        attn_proj,
        ffn_gain,
        gate_proj,
        up_proj,
        down_proj,
    ) = tuple((weight_arr.astype(jnp.float32) for weight_arr in gathered))
    (
        previous,
        state_in,
        attended_raw,
        log_total,
        keys_whole,
        values_whole,
        projected,
        queries,
        key_send,
        value_send,
    ) = kept
    row_count = hidden.shape[0]
    group_size = QH // KVH
    _, pull_front = jax.vjp(
        partial(piece_front, position=position, piece_ends=piece_ends),
        hidden,
        norm_gain,
        in_proj,
        query_proj,
        key_proj,
        value_proj,
    )
    mix_vals, pull_mix = jax.vjp(
        partial(
            scan_block, member=member, sequence=sequence, begin_row=begin_row, piece_ends=piece_ends
        ),
        projected,
        previous,
        conv_weight,
        conv_bias,
        dt_bias,
        decay_log,
        skip_gain,
    )
    y_part, c_mat, seg_cum, decay_total, end_state = mix_vals
    mamba_out, pull_mixer = jax.vjp(
        partial(mixer_out, member=member),
        y_part,
        c_mat,
        seg_cum,
        state_in,
        projected,
        mixer_gain,
        out_proj,
    )
    _, pull_back = jax.vjp(
        piece_back,
        hidden,
        mamba_out,
        round_value(attended_raw),
        attn_proj,
        ffn_gain,
        gate_proj,
        up_proj,
        down_proj,
    )
    (
        grad_hidden,
        grad_mamba,
        grad_att,
        g_attn_proj,
        g_ffn_gain,
        g_gate_proj,
        g_up_proj,
        g_down_proj,
    ) = pull_back(grad_out)
    keys_whole, values_whole = (
        lax.all_gather(key_send, "ctx", axis=0, tiled=True),
        lax.all_gather(value_send, "ctx", axis=0, tiled=True),
    )
    grad_queries, grad_keys, grad_values = attention_back(
        queries.reshape(row_count, KVH, group_size, HD),
        keys_whole,
        values_whole,
        round_value(grad_att),
        attended_raw,
        log_total,
        (pieces, sequence, position),
    )
    grad_y, grad_c, grad_seg, grad_state, grad_proj_out, g_mixer_gain, g_out_proj = pull_mixer(
        grad_mamba
    )
    back_scan = carried_in_2(
        (decay_total, grad_state),
        "ctx",
        chain_states,
        (jnp.ones_like(decay_total), jnp.zeros_like(grad_state)),
    )
    grad_end = back_scan[1]
    grad_decay = jnp.sum(grad_end * state_in, axis=(2, 3))
    grad_proj_mix, grad_prev, g_conv_weight, g_conv_bias, g_dt_bias, g_decay_log, g_skip_gain = (
        pull_mix((grad_y, grad_c, grad_seg, grad_decay, grad_end))
    )
    grad_tails = passed_along(grad_prev.astype(jnp.bfloat16), "ctx", -1).astype(grad_prev.dtype)
    grad_front, g_norm_gain, g_in_proj, g_query_proj, g_key_proj, g_value_proj = pull_front(
        (grad_proj_mix + grad_proj_out, grad_queries, grad_keys, grad_values, grad_tails)
    )
    return (
        grad_hidden + grad_front,
        (
            g_norm_gain,
            g_in_proj,
            g_conv_weight,
            g_conv_bias,
            g_dt_bias,
            g_decay_log,
            g_skip_gain,
            g_mixer_gain,
            g_out_proj,
            g_query_proj,
            g_key_proj,
            g_value_proj,
            g_attn_proj,
            g_ffn_gain,
            g_gate_proj,
            g_up_proj,
            g_down_proj,
        ),
    )


def per_device(
    block_in,
    seq_lengths,
    norm_gain,
    in_proj,
    conv_weight,
    conv_bias,
    dt_bias,
    decay_log,
    skip_gain,
    mixer_gain,
    out_proj,
    query_proj,
    key_proj,
    value_proj,
    attn_proj,
    ffn_gain,
    gate_proj,
    up_proj,
    down_proj,
    out_grad,
):
    shards = (
        norm_gain,
        in_proj,
        conv_weight,
        conv_bias,
        dt_bias,
        decay_log,
        skip_gain,
        mixer_gain,
        out_proj,
        query_proj,
        key_proj,
        value_proj,
        attn_proj,
        ffn_gain,
        gate_proj,
        up_proj,
        down_proj,
    )
    row_count = block_in.shape[0]
    pieces = seq_lengths[0] // lax.axis_size("ctx")
    local_rows = jnp.arange(row_count, dtype=jnp.int32)
    member, sequence, position, begin_row, piece_ends = layout(
        pieces, lax.axis_index("ctx"), local_rows
    )
    layout_meta = (pieces, sequence, position, member, begin_row, piece_ends)
    hidden = block_in.astype(jnp.float32)
    inputs_saved = []
    weights_saved = []
    kept_saved = []
    for layer_idx in range(LAYERS):
        gathered = gather_layer(shards, layer_idx)
        weights_saved.append(gathered)
        inputs_saved.append(hidden)
        hidden, kept = layer_forward(hidden, gathered, layout_meta)
        kept_saved.append(kept)
    block_out = hidden.astype(jnp.bfloat16)
    grad_hidden = out_grad.astype(jnp.float32)
    layer_grads = []
    for layer_idx in reversed(range(LAYERS)):
        gathered = gather_again(shards, layer_idx)
        grad_hidden, weight_grads = layer_backward(
            grad_hidden, inputs_saved[layer_idx], gathered, kept_saved[layer_idx], layout_meta
        )
        layer_grads.insert(0, reduce_grads(weight_grads))
    in_grad = grad_hidden.astype(jnp.bfloat16)
    stacked = tuple(
        (jnp.stack([grad_set[slot_idx] for grad_set in layer_grads]) for slot_idx in range(17))
    )
    return (block_out, in_grad) + stacked


def solution(mesh):
    placed = (
        P(("fsdp", "ctx"), None),
        P("fsdp", None),
        P(None, "fsdp"),
        P(None, "fsdp", None),
        P(None, "fsdp", None),
        P(None, "fsdp"),
        P(None, "fsdp"),
        P(None, "fsdp"),
        P(None, "fsdp"),
        P(None, "fsdp"),
        P(None, "fsdp", None),
        P(None, "fsdp", None),
        P(None, "fsdp", None),
        P(None, "fsdp", None),
        P(None, "fsdp", None),
        P(None, "fsdp"),
        P(None, "fsdp", None),
        P(None, "fsdp", None),
        P(None, "fsdp", None),
        P(("fsdp", "ctx"), None),
    )
    return jax.shard_map(
        per_device,
        mesh=mesh,
        in_specs=placed,
        out_specs=(
            P(("fsdp", "ctx"), None),
            P(("fsdp", "ctx"), None),
            P(None, "fsdp"),
            P(None, "fsdp", None),
            P(None, "fsdp", None),
            P(None, "fsdp"),
            P(None, "fsdp"),
            P(None, "fsdp"),
            P(None, "fsdp"),
            P(None, "fsdp"),
            P(None, "fsdp", None),
            P(None, "fsdp", None),
            P(None, "fsdp", None),
            P(None, "fsdp", None),
            P(None, "fsdp", None),
            P(None, "fsdp"),
            P(None, "fsdp", None),
            P(None, "fsdp", None),
            P(None, "fsdp", None),
        ),
        check_vma=False,
    )
```

profile of v0, /device:TPU:0, one launch (start us, length us, event | category | flops | bytes accessed | tf_op | source)
XLA Modules:
  0.0 2887.4 jit_solution(5721487352058602609)
XLA Ops:
  19.2 9.5 all-gather.2
  30.9 16.1 all-reduce.67
  52.4 20.2 all-gather.1
  76.5 19.0 all-gather.65.cloned.1.call-done
  163.6 10.1 all-gather.11
  182.4 25.0 all_gather.205
  210.5 10.4 all-gather.13
  223.0 20.4 all_gather.208
  264.3 12.1 all-gather.20
  295.0 18.1 all-gather.42
  316.3 23.7 while.94
  349.4 9.7 all-gather.69.cloned.1.call-done
  362.0 34.1 %all-gather.73.cloned.1.call-done = bf16[1,1024,1024]{2,1,0:T(8,128)(2,1)} async-done(((bf16[1,256,1024]{2,1,0:T(8,128)(2,1)}), bf16[1,1024,1024]{2,1,0:T(8,128)(2,1)}) %all-gather.73.cloned.1.call-update) | async-done | bytes 2097168 | tf_op jit(solution)/shard_map/all_gather | solution.py:345
  398.5 52.7 %all-gather.75.cloned.1.call-done = bf16[1,1024,2048]{2,1,0:T(8,128)(2,1)} async-done(((bf16[1,256,2048]{2,1,0:T(8,128)(2,1)}), bf16[1,1024,2048]{2,1,0:T(8,128)(2,1)}) %all-gather.75.cloned.1.call-update) | async-done | bytes 4194320 | tf_op jit(solution)/shard_map/all_gather | solution.py:347
  455.1 50.6 %all-gather.77.cloned.1.call-done = bf16[1,1024,2048]{2,1,0:T(8,128)(2,1)} async-done(((bf16[1,256,2048]{2,1,0:T(8,128)(2,1)}), bf16[1,1024,2048]{2,1,0:T(8,128)(2,1)}) %all-gather.77.cloned.1.call-update) | async-done | bytes 4194320 | tf_op jit(solution)/shard_map/all_gather | solution.py:348
  510.9 50.0 %all-gather.79.cloned.1.call-done = bf16[1,2048,1024]{2,1,0:T(8,128)(2,1)} async-done(((bf16[1,512,1024]{2,1,0:T(8,128)(2,1)}), bf16[1,2048,1024]{2,1,0:T(8,128)(2,1)}) %all-gather.79.cloned.1.call-update) | async-done | bytes 4194320 | tf_op jit(solution)/shard_map/all_gather | solution.py:349
  564.3 73.8 %all-gather.81.cloned.1.call-done = bf16[1,1024,3352]{1,2,0:T(8,128)(2,1)} async-done(((bf16[1,256,3352]{1,2,0:T(8,128)(2,1)}), bf16[1,1024,3352]{1,2,0:T(8,128)(2,1)}) %all-gather.81.cloned.1.call-update) | async-done | bytes 6864912 | tf_op jit(solution)/shard_map/all_gather | solution.py:334
  693.5 10.4 all-gather.30
  703.9 12.1 all-gather.32
  729.4 13.8 all-gather.43
  754.7 23.9 all_gather.227
  782.9 20.5 all_gather.230
  814.0 98.0 %all-gather.83.cloned.1.call-done = f32[24,24,64,128]{3,2,1,0:T(8,128)} async-done(((f32[3,24,64,128]{3,2,1,0:T(8,128)}), f32[24,24,64,128]{3,2,1,0:T(8,128)}) %all-gather.83.cloned.1.call-update) | async-done | bytes 18874384 | tf_op jit(solution)/shard_map/all_gather | solution.py:36
  912.0 23.9 while.95
  945.5 10.6 all-gather.85.cloned.1.call-done
  959.0 34.1 %all-gather.89.cloned.1.call-done = bf16[1,1024,1024]{2,1,0:T(8,128)(2,1)} async-done(((bf16[1,256,1024]{2,1,0:T(8,128)(2,1)}), bf16[1,1024,1024]{2,1,0:T(8,128)(2,1)}) %all-gather.89.cloned.1.call-update) | async-done | bytes 2097168 | tf_op jit(solution)/shard_map/all_gather | solution.py:345
  995.5 52.6 %all-gather.91.cloned.1.call-done = bf16[1,1024,2048]{2,1,0:T(8,128)(2,1)} async-done(((bf16[1,256,2048]{2,1,0:T(8,128)(2,1)}), bf16[1,1024,2048]{2,1,0:T(8,128)(2,1)}) %all-gather.91.cloned.1.call-update) | async-done | bytes 4194320 | tf_op jit(solution)/shard_map/all_gather | solution.py:347
  1051.2 52.0 %all-gather.93.cloned.1.call-done = bf16[1,1024,2048]{2,1,0:T(8,128)(2,1)} async-done(((bf16[1,256,2048]{2,1,0:T(8,128)(2,1)}), bf16[1,1024,2048]{2,1,0:T(8,128)(2,1)}) %all-gather.93.cloned.1.call-update) | async-done | bytes 4194320 | tf_op jit(solution)/shard_map/all_gather | solution.py:348
  1116.8 51.2 %while.96 = (s32[]{:T(128)}, f32[128,2,4,128]{0,3,2,1:T(8,128)}, bf16[2,512,256]{2,1,0:T(8,128)(2,1)}, bf16[2,512,256]{2,1,0:T(8,128)(2,1)}, bf16[2,512,256]{1,2...) while((s32[]{:T(128)}, f32[128,2,4,128]{0,3,2,1:T(8,128)}, ...), condition=%wide.region_31.33_spmd.clone, body=%wide.region_27.32_spmd.clone.sunk | while | flops 678917632 | bytes 24016652 | solution.py:286
  1185.6 12.7 all-gather.44
  1216.9 13.7 reduce-scatter.29.cloned.1.call-done
  1232.9 88.9 %all-gather.97.cloned.1.call-done = bf16[24,24,64,128]{3,2,1,0:T(8,128)(2,1)} async-done(((bf16[3,24,64,128]{3,2,1,0:T(8,128)(2,1)}), bf16[24,24,64,128]{3,2,1,0:T(8,128)(2,1)}) %all-gather.97.cloned.1.call-update) | async-done | bytes 9437200 | tf_op jit(solution)/shard_map/all_gather | solution.py:54
  1321.8 21.0 while.97
  1378.1 15.5 scatter_fusion.3
  1393.7 15.5 scatter_fusion.2
  1409.2 15.5 scatter_fusion.4
  1453.8 50.9 %while.98 = (s32[]{:T(128)}, f32[128,2,4,128]{0,3,2,1:T(8,128)}, bf16[2,512,256]{2,1,0:T(8,128)(2,1)}, bf16[2,512,256]{2,1,0:T(8,128)(2,1)}, bf16[2,512,256]{1,2...) while((s32[]{:T(128)}, f32[128,2,4,128]{0,3,2,1:T(8,128)}, ...), condition=%wide.region_60.62_spmd.clone, body=%wide.region_56.61_spmd.clone.sunk | while | flops 678917632 | bytes 24016652 | solution.py:286
  1545.0 23.3 reduce-scatter.33.cloned.1.call-done
  1601.6 9.0 all-gather.45
  1621.9 37.0 %all-gather.99.cloned.1.call-done = bf16[24,24,64,128]{3,2,1,0:T(8,128)(2,1)} async-done(((bf16[3,24,64,128]{3,2,1,0:T(8,128)(2,1)}), bf16[24,24,64,128]{3,2,1,0:T(8,128)(2,1)}) %all-gather.99.cloned.1.call-update) | async-done | bytes 9437200 | tf_op jit(solution)/shard_map/all_gather | solution.py:54
  1658.9 15.5 while.99
  1711.6 15.5 scatter_fusion.8
  1727.2 15.5 scatter_fusion.7
  1742.7 15.5 scatter_fusion.9
  1775.4 14.5 reduce-scatter.59.cloned.1.call-done
  1789.9 47.4 %reduce-scatter.43.cloned.1.call-done = bf16[384,1024]{1,0:T(8,128)(2,1)} async-done(((bf16[1536,1024]{1,0:T(8,128)(2,1)}), bf16[384,1024]{1,0:T(8,128)(2,1)}) %reduce-scatter.43.cloned.1.call-update) | async-done | bytes 786448 | tf_op jit(solution)/shard_map/reduce_scatter | solution.py:439
  1837.3 56.3 %reduce-scatter.67.cloned.1.call-done = bf16[256,2048]{1,0:T(8,128)(2,1)} async-done(((bf16[1024,2048]{1,0:T(8,128)(2,1)}), bf16[256,2048]{1,0:T(8,128)(2,1)}) %reduce-scatter.67.cloned.1.call-update) | async-done | bytes 1048592 | tf_op jit(solution)/shard_map/reduce_scatter | solution.py:460
  1893.6 56.5 %reduce-scatter.63.cloned.1.call-done = bf16[256,2048]{1,0:T(8,128)(2,1)} async-done(((bf16[1024,2048]{1,0:T(8,128)(2,1)}), bf16[256,2048]{1,0:T(8,128)(2,1)}) %reduce-scatter.63.cloned.1.call-update) | async-done | bytes 1048592 | tf_op jit(solution)/shard_map/reduce_scatter | solution.py:457
  1950.1 55.6 %reduce-scatter.71.cloned.1.call-done = bf16[512,1024]{1,0:T(8,128)(2,1)} async-done(((bf16[2048,1024]{1,0:T(8,128)(2,1)}), bf16[512,1024]{1,0:T(8,128)(2,1)}) %reduce-scatter.71.cloned.1.call-update) | async-done | bytes 1048592 | tf_op jit(solution)/shard_map/reduce_scatter | solution.py:463
  2005.7 28.4 reduce-scatter.49.cloned.1.call-done
  2034.1 27.6 reduce-scatter.53.cloned.1.call-done
  2061.7 38.9 %reduce-scatter.45.cloned.1.call-done = bf16[256,1024]{1,0:T(8,128)(2,1)} async-done(((bf16[1024,1024]{1,0:T(8,128)(2,1)}), bf16[256,1024]{1,0:T(8,128)(2,1)}) %reduce-scatter.45.cloned.1.call-update) | async-done | bytes 524304 | tf_op jit(solution)/shard_map/reduce_scatter | solution.py:442
  2100.6 38.2 %reduce-scatter.57.cloned.1.call-done = bf16[256,1024]{1,0:T(8,128)(2,1)} async-done(((bf16[1024,1024]{1,0:T(8,128)(2,1)}), bf16[256,1024]{1,0:T(8,128)(2,1)}) %reduce-scatter.57.cloned.1.call-update) | async-done | bytes 524304 | tf_op jit(solution)/shard_map/reduce_scatter | solution.py:451
  2138.8 47.3 %reduce-scatter.41.cloned.1.call-done = bf16[384,1024]{1,0:T(8,128)(2,1)} async-done(((bf16[1536,1024]{1,0:T(8,128)(2,1)}), bf16[384,1024]{1,0:T(8,128)(2,1)}) %reduce-scatter.41.cloned.1.call-update) | async-done | bytes 786448 | tf_op jit(solution)/shard_map/reduce_scatter | solution.py:439
  2186.1 55.8 %reduce-scatter.69.cloned.1.call-done = bf16[512,1024]{1,0:T(8,128)(2,1)} async-done(((bf16[2048,1024]{1,0:T(8,128)(2,1)}), bf16[512,1024]{1,0:T(8,128)(2,1)}) %reduce-scatter.69.cloned.1.call-update) | async-done | bytes 1048592 | tf_op jit(solution)/shard_map/reduce_scatter | solution.py:463
  2241.9 55.6 %reduce-scatter.65.cloned.1.call-done = bf16[256,2048]{1,0:T(8,128)(2,1)} async-done(((bf16[1024,2048]{1,0:T(8,128)(2,1)}), bf16[256,2048]{1,0:T(8,128)(2,1)}) %reduce-scatter.65.cloned.1.call-update) | async-done | bytes 1048592 | tf_op jit(solution)/shard_map/reduce_scatter | solution.py:460
  2297.4 56.5 %reduce-scatter.61.cloned.1.call-done = bf16[256,2048]{1,0:T(8,128)(2,1)} async-done(((bf16[1024,2048]{1,0:T(8,128)(2,1)}), bf16[256,2048]{1,0:T(8,128)(2,1)}) %reduce-scatter.61.cloned.1.call-update) | async-done | bytes 1048592 | tf_op jit(solution)/shard_map/reduce_scatter | solution.py:457
  2353.9 80.7 %reduce-scatter.39.cloned.1.call-done = bf16[256,3352]{0,1:T(8,128)(2,1)} async-done(((bf16[1024,3352]{0,1:T(8,128)(2,1)}), bf16[256,3352]{0,1:T(8,128)(2,1)}) %reduce-scatter.39.cloned.1.call-update) | async-done | bytes 1716240 | tf_op jit(solution)/shard_map/reduce_scatter | solution.py:418
  2434.6 80.3 %reduce-scatter.37.cloned.1.call-done = bf16[256,3352]{0,1:T(8,128)(2,1)} async-done(((bf16[1024,3352]{0,1:T(8,128)(2,1)}), bf16[256,3352]{0,1:T(8,128)(2,1)}) %reduce-scatter.37.cloned.1.call-update) | async-done | bytes 1716240 | tf_op jit(solution)/shard_map/reduce_scatter | solution.py:418
  2521.9 20.4 reduce-scatter.75.cloned.1.call-done
  2547.1 22.7 reduce-scatter.73.cloned.1.call-done
  2576.4 15.4 all-reduce.66
  2592.9 27.8 all-reduce.64
  2627.3 233.3 %all-reduce.70.cloned.1.call-done = (bf16[1,256,3352]{1,2,0:T(8,128)(2,1)}, bf16[1,256,3352]{1,2,0:T(8,128)(2,1)}, bf16[1,384,1024]{2,1,0:T(8,128)(2,1)}, bf16[1...) async-done(((bf16[1,256,3352]{1,2,0:T(8,128)(2,1)}, ...) | async-done | bytes 13918224 | tf_op jit(solution)/shard_map/psum | solution.py:469
  (1481 shorter events, 764.3 us)
Async XLA Ops:
  7.2 88.3 %all-gather.65.cloned.1.call-start = ((), (), s32[]{:S(2)}) async-start(), calls=%async_computation.46 | async-start | bytes 8581120 | tf_op jit(solution)/shard_map/all_gather | solution.py:334
  11.3 269.5 %all-gather.71.cloned.1.call-start = ((), (), s32[]{:S(2)}) async-start(), calls=%async_computation.49 | async-start | bytes 2621440 | tf_op jit(solution)/shard_map/all_gather | solution.py:342
  13.5 302.9 %all-gather.67.cloned.1.call-start = ((), (), s32[]{:S(2)}) async-start(), calls=%async_computation.47 | async-start | bytes 21233664 | tf_op jit(solution)/shard_map/all_gather | solution.py:36
  47.8 86.1 %copy-start.183 = (f32[128,3]{0,1:T(4,128)}, f32[128,3]{0,1:T(4,128)S(1)}, u32[]{:S(2)}) copy-start(f32[128,3]{0,1:T(4,128)S(1)} %fusion.484) | copy-start | bytes 4612
  104.3 190.0 %copy-start.3 = (f32[3,24]{1,0:T(4,128)}, f32[3,24]{1,0:T(4,128)S(1)}, u32[]{:S(2)}) copy-start(f32[3,24]{1,0:T(4,128)S(1)} %gather_fusion.5) | copy-start | bytes 868
  105.9 5.0 collective-permute-start
  133.7 209.8 %copy-start.43 = (f32[128,1536]{0,1:T(8,128)}, f32[128,1536]{0,1:T(8,128)S(1)}, u32[]{:S(2)}) copy-start(f32[128,1536]{0,1:T(8,128)S(1)} %slice.388) | copy-start | bytes 2359300
  137.4 221.7 %all-gather.69.cloned.1.call-start = ((), (), s32[]{:S(2)}) async-start(), calls=%async_computation.48 | async-start | bytes 3932160 | tf_op jit(solution)/shard_map/all_gather | solution.py:341
  138.8 257.3 %all-gather.73.cloned.1.call-start = ((), (), s32[]{:S(2)}) async-start(), calls=%async_computation.50 | async-start | bytes 2621440 | tf_op jit(solution)/shard_map/all_gather | solution.py:345
  141.2 309.9 %all-gather.75.cloned.1.call-start = ((), (), s32[]{:S(2)}) async-start(), calls=%async_computation.51 | async-start | bytes 5242880 | tf_op jit(solution)/shard_map/all_gather | solution.py:347
  142.8 362.9 %all-gather.77.cloned.1.call-start = ((), (), s32[]{:S(2)}) async-start(), calls=%async_computation.52 | async-start | bytes 5242880 | tf_op jit(solution)/shard_map/all_gather | solution.py:348
  146.1 414.7 %all-gather.79.cloned.1.call-start = ((), (), s32[]{:S(2)}) async-start(), calls=%async_computation.53 | async-start | bytes 5242880 | tf_op jit(solution)/shard_map/all_gather | solution.py:349
  147.7 490.4 %all-gather.81.cloned.1.call-start = ((), (), s32[]{:S(2)}) async-start(), calls=%async_computation.54 | async-start | bytes 8581120 | tf_op jit(solution)/shard_map/all_gather | solution.py:334
  148.4 575.7 %all-gather.95.cloned.1.call-start = ((), (), s32[]{:S(2)}) async-start(), calls=%async_computation.61 | async-start | bytes 5242880 | tf_op jit(solution)/shard_map/all_gather | solution.py:349
  149.0 594.8 %all-gather.87.cloned.1.call-start = ((), (), s32[]{:S(2)}) async-start(), calls=%async_computation.57 | async-start | bytes 2621440 | tf_op jit(solution)/shard_map/all_gather | solution.py:342
  149.8 762.3 %all-gather.83.cloned.1.call-start = ((), (), s32[]{:S(2)}) async-start(), calls=%async_computation.55 | async-start | bytes 21233664 | tf_op jit(solution)/shard_map/all_gather | solution.py:36
  398.3 162.6 %copy-start.8 = (f32[128,1024]{1,0:T(8,128)}, f32[128,1024]{1,0:T(8,128)S(1)}, u32[]{:S(2)}) copy-start(f32[128,1024]{1,0:T(8,128)S(1)} %get-tuple-element.1603) | copy-start | bytes 1572868
  398.3 107.4 %copy-start.278 = (f32[128]{0:T(128)}, f32[128]{0:T(128)S(1)}, u32[]{:S(2)}) copy-start(f32[128]{0:T(128)S(1)} %fusion.460) | copy-start | bytes 1540
  398.5 107.2 %copy-start.70 = (bf16[128,1024]{1,0:T(8,128)(2,1)}, bf16[128,1024]{1,0:T(8,128)(2,1)S(1)}, u32[]{:S(2)}) copy-start(bf16[128,1024]{1,0:T(8,128)(2,1)S(1)} %multiply_convert_fusion.6) | copy-start | bytes 786436
  563.9 79.1 %copy-start.31 = (f32[128,1024]{1,0:T(8,128)}, f32[128,1024]{1,0:T(8,128)S(1)}, u32[]{:S(2)}) copy-start(f32[128,1024]{1,0:T(8,128)S(1)} %get-tuple-element.1606) | copy-start | bytes 1572868
  564.3 218.4 %copy-start.27 = (bf16[128,1024]{1,0:T(8,128)(2,1)}, bf16[128,1024]{1,0:T(8,128)(2,1)S(1)}, u32[]{:S(2)}) copy-start(bf16[128,1024]{1,0:T(8,128)(2,1)S(1)} %subtract_add_fusion.21) | copy-start | bytes 786436
  649.0 5.4 collective-permute-start.1
  680.5 275.5 %all-gather.85.cloned.1.call-start = ((), (), s32[]{:S(2)}) async-start(), calls=%async_computation.56 | async-start | bytes 3932160 | tf_op jit(solution)/shard_map/all_gather | solution.py:341
  681.3 311.8 %all-gather.89.cloned.1.call-start = ((), (), s32[]{:S(2)}) async-start(), calls=%async_computation.58 | async-start | bytes 2621440 | tf_op jit(solution)/shard_map/all_gather | solution.py:345
  681.9 366.3 %all-gather.91.cloned.1.call-start = ((), (), s32[]{:S(2)}) async-start(), calls=%async_computation.59 | async-start | bytes 5242880 | tf_op jit(solution)/shard_map/all_gather | solution.py:347
  682.5 420.7 %all-gather.93.cloned.1.call-start = ((), (), s32[]{:S(2)}) async-start(), calls=%async_computation.60 | async-start | bytes 5242880 | tf_op jit(solution)/shard_map/all_gather | solution.py:348
  683.0 530.2 %reduce-scatter.31.cloned.1.call-start = ((), (), s32[]{:S(2)}) async-start(), calls=%async_computation.25 | async-start | bytes 589824 | tf_op jit(solution)/shard_map/reduce_scatter | solution.py:296
  724.1 388.8 %copy-start.160 = (f32[1,1024]{1,0:T(1,128)}, f32[1,1024]{1,0:T(1,128)S(1)}, u32[]{:S(2)}) copy-start(f32[1,1024]{1,0:T(1,128)S(1)} %convert_element_type.1151) | copy-start | bytes 12292
  811.9 181.3 %copy-start.128 = (bf16[128,1024]{0,1:T(8,128)(2,1)}, bf16[128,1024]{0,1:T(8,128)(2,1)S(1)}, u32[]{:S(2)}) copy-start(bf16[128,1024]{0,1:T(8,128)(2,1)S(1)} %subtract_add_fusion.19) | copy-start | bytes 786436
  814.0 125.4 %copy-start.201 = (f32[128,128]{1,0:T(8,128)}, f32[128,128]{1,0:T(8,128)S(1)}, u32[]{:S(2)}) copy-start(f32[128,128]{1,0:T(8,128)S(1)} %fusion.414) | copy-start | bytes 196612
  945.2 227.5 %copy-start.307 = (f32[128]{0:T(128)}, f32[128]{0:T(128)S(1)}, u32[]{:S(2)}) copy-start(f32[128]{0:T(128)S(1)} %fusion.462) | copy-start | bytes 1540
  995.3 117.6 %copy-start.5 = (f32[128,1024]{1,0:T(8,128)}, f32[128,1024]{1,0:T(8,128)S(1)}, u32[]{:S(2)}) copy-start(f32[128,1024]{1,0:T(8,128)S(1)} %get-tuple-element.1614) | copy-start | bytes 1572868
  995.3 117.5 %copy-start.265 = (f32[128]{0:T(128)}, f32[128]{0:T(128)S(1)}, u32[]{:S(2)}) copy-start(f32[128]{0:T(128)S(1)} %fusion.463) | copy-start | bytes 1540
  995.5 107.7 %copy-start.72 = (bf16[128,1024]{1,0:T(8,128)(2,1)}, bf16[128,1024]{1,0:T(8,128)(2,1)S(1)}, u32[]{:S(2)}) copy-start(bf16[128,1024]{1,0:T(8,128)(2,1)S(1)} %multiply_convert_fusion.4) | copy-start | bytes 786436
  995.5 107.7 %copy-start.156 = (f32[128,2048]{1,0:T(8,128)S(1)}, f32[128,2048]{1,0:T(8,128)}, u32[]{:S(2)}) copy-start(f32[128,2048]{1,0:T(8,128)} %fusion.48) | copy-start | bytes 3145732
  1168.1 62.5 %reduce-scatter.29.cloned.1.call-start = ((), (), s32[]{:S(2)}) async-start(), calls=%async_computation.24 | async-start | bytes 589824 | tf_op jit(solution)/shard_map/reduce_scatter | solution.py:302
  1168.7 153.1 %all-gather.97.cloned.1.call-start = ((), (), s32[]{:S(2)}) async-start(), calls=%async_computation.62 | async-start | bytes 10616832 | tf_op jit(solution)/shard_map/all_gather | solution.py:54
  1181.1 360.9 %reduce-scatter.35.cloned.1.call-start = ((), (), s32[]{:S(2)}) async-start(), calls=%async_computation.27 | async-start | bytes 589824 | tf_op jit(solution)/shard_map/reduce_scatter | solution.py:296
  1214.7 107.1 %copy-start.174 = (bf16[128,2,128]{2,1,0:T(2,128)(2,1)}, bf16[128,2,128]{2,1,0:T(2,128)(2,1)S(1)}, u32[]{:S(2)}) copy-start(bf16[128,2,128]{2,1,0:T(2,128)(2,1)S(1)} %pad_add_fusion.3) | copy-start | bytes 196612
  1424.8 5.7 collective-permute-start.2
  1504.8 63.5 %reduce-scatter.33.cloned.1.call-start = ((), (), s32[]{:S(2)}) async-start(), calls=%async_computation.26 | async-start | bytes 589824 | tf_op jit(solution)/shard_map/reduce_scatter | solution.py:302
  1505.6 153.4 %all-gather.99.cloned.1.call-start = ((), (), s32[]{:S(2)}) async-start(), calls=%async_computation.63 | async-start | bytes 10616832 | tf_op jit(solution)/shard_map/all_gather | solution.py:54
  1517.6 257.7 %reduce-scatter.51.cloned.1.call-start = ((), (), s32[]{:S(2)}) async-start(), calls=%async_computation.35 | async-start | bytes 655360 | tf_op jit(solution)/shard_map/reduce_scatter | solution.py:445
  1518.8 256.5 %reduce-scatter.55.cloned.1.call-start = ((), (), s32[]{:S(2)}) async-start(), calls=%async_computation.37 | async-start | bytes 655360 | tf_op jit(solution)/shard_map/reduce_scatter | solution.py:448
  1520.1 255.3 %reduce-scatter.47.cloned.1.call-start = ((), (), s32[]{:S(2)}) async-start(), calls=%async_computation.33 | async-start | bytes 2621440 | tf_op jit(solution)/shard_map/reduce_scatter | solution.py:442
  1522.3 267.7 %reduce-scatter.59.cloned.1.call-start = ((), (), s32[]{:S(2)}) async-start(), calls=%async_computation.39 | async-start | bytes 2621440 | tf_op jit(solution)/shard_map/reduce_scatter | solution.py:451
  1524.4 312.9 %reduce-scatter.43.cloned.1.call-start = ((), (), s32[]{:S(2)}) async-start(), calls=%async_computation.31 | async-start | bytes 3932160 | tf_op jit(solution)/shard_map/reduce_scatter | solution.py:439
  1527.3 366.3 %reduce-scatter.67.cloned.1.call-start = ((), (), s32[]{:S(2)}) async-start(), calls=%async_computation.43 | async-start | bytes 5242880 | tf_op jit(solution)/shard_map/reduce_scatter | solution.py:460
  1531.9 418.2 %reduce-scatter.63.cloned.1.call-start = ((), (), s32[]{:S(2)}) async-start(), calls=%async_computation.41 | async-start | bytes 5242880 | tf_op jit(solution)/shard_map/reduce_scatter | solution.py:457
  1536.3 469.3 %reduce-scatter.71.cloned.1.call-start = ((), (), s32[]{:S(2)}) async-start(), calls=%async_computation.45 | async-start | bytes 5242880 | tf_op jit(solution)/shard_map/reduce_scatter | solution.py:463
  1541.9 492.2 %reduce-scatter.49.cloned.1.call-start = ((), (), s32[]{:S(2)}) async-start(), calls=%async_computation.34 | async-start | bytes 655360 | tf_op jit(solution)/shard_map/reduce_scatter | solution.py:445
  1544.8 517.0 %reduce-scatter.53.cloned.1.call-start = ((), (), s32[]{:S(2)}) async-start(), calls=%async_computation.36 | async-start | bytes 655360 | tf_op jit(solution)/shard_map/reduce_scatter | solution.py:448
  1570.4 530.2 %reduce-scatter.45.cloned.1.call-start = ((), (), s32[]{:S(2)}) async-start(), calls=%async_computation.32 | async-start | bytes 2621440 | tf_op jit(solution)/shard_map/reduce_scatter | solution.py:442
  1575.2 563.5 %reduce-scatter.57.cloned.1.call-start = ((), (), s32[]{:S(2)}) async-start(), calls=%async_computation.38 | async-start | bytes 2621440 | tf_op jit(solution)/shard_map/reduce_scatter | solution.py:451
  1578.4 607.6 %reduce-scatter.41.cloned.1.call-start = ((), (), s32[]{:S(2)}) async-start(), calls=%async_computation.30 | async-start | bytes 3932160 | tf_op jit(solution)/shard_map/reduce_scatter | solution.py:439
  1581.2 660.6 %reduce-scatter.69.cloned.1.call-start = ((), (), s32[]{:S(2)}) async-start(), calls=%async_computation.44 | async-start | bytes 5242880 | tf_op jit(solution)/shard_map/reduce_scatter | solution.py:463
  1586.0 711.5 %reduce-scatter.65.cloned.1.call-start = ((), (), s32[]{:S(2)}) async-start(), calls=%async_computation.42 | async-start | bytes 5242880 | tf_op jit(solution)/shard_map/reduce_scatter | solution.py:460
  1590.6 763.4 %reduce-scatter.61.cloned.1.call-start = ((), (), s32[]{:S(2)}) async-start(), calls=%async_computation.40 | async-start | bytes 5242880 | tf_op jit(solution)/shard_map/reduce_scatter | solution.py:457
  1595.0 839.6 %reduce-scatter.39.cloned.1.call-start = ((), (), s32[]{:S(2)}) async-start(), calls=%async_computation.29 | async-start | bytes 8581120 | tf_op jit(solution)/shard_map/reduce_scatter | solution.py:418
  1601.0 913.9 %reduce-scatter.37.cloned.1.call-start = ((), (), s32[]{:S(2)}) async-start(), calls=%async_computation.28 | async-start | bytes 8581120 | tf_op jit(solution)/shard_map/reduce_scatter | solution.py:418
  1758.3 5.7 collective-permute-start.3
  1772.0 770.3 %reduce-scatter.75.cloned.1.call-start = ((), (), s32[]{:S(2)}) async-start(), calls=%async_computation.65 | async-start | bytes 573440
  1773.9 795.9 %reduce-scatter.73.cloned.1.call-start = ((), (), s32[]{:S(2)}) async-start(), calls=%async_computation.64 | async-start | bytes 573440
  1775.1 1085.5 %all-reduce.70.cloned.1.call-start = ((), (), s32[]{:S(2)}) async-start(), calls=%async_computation.66 | async-start | bytes 27836416 | tf_op jit(solution)/shard_map/psum | solution.py:469
  (371 other events, 3469.5 us)
Sparse Core Ops, SparseCore 0:
  11.4 84.0 all-gather.64
  97.4 35.5 all-gather.70
  137.5 177.6 all-gather.66
  316.8 42.1 all-gather.68
  360.8 35.3 all-gather.72
  398.4 52.6 all-gather.74
  453.0 52.6 all-gather.76
  508.1 52.6 all-gather.78
  563.3 74.7 all-gather.80
  640.3 52.7 all-gather.94
  695.6 37.6 all-gather.86
  735.3 176.6 all-gather.82
  913.9 42.1 all-gather.84
  957.8 35.3 all-gather.88
  995.4 52.6 all-gather.90
  1050.4 52.6 all-gather.92
  1168.2 30.9 reduce-scatter.30
  1201.4 29.0 reduce-scatter.28
  1232.8 88.9 all-gather.96
  1504.9 31.3 reduce-scatter.34
  1539.2 29.0 reduce-scatter.32
  1569.9 88.9 all-gather.98
  1661.7 23.3 reduce-scatter.50
  1688.0 24.7 reduce-scatter.54
  1716.4 35.1 reduce-scatter.46
  1754.7 35.2 reduce-scatter.58
  1793.4 43.9 reduce-scatter.42
  1840.9 52.6 reduce-scatter.66
  1897.4 52.6 reduce-scatter.62
  1952.9 52.6 reduce-scatter.70
  2009.3 24.7 reduce-scatter.48
  2036.9 24.7 reduce-scatter.52
  2065.4 35.1 reduce-scatter.44
  2103.6 35.1 reduce-scatter.56
  2142.1 43.9 reduce-scatter.40
  2189.1 52.6 reduce-scatter.68
  2244.7 52.6 reduce-scatter.64
  2301.2 52.6 reduce-scatter.60
  2357.4 77.1 reduce-scatter.38
  2437.7 77.1 reduce-scatter.36
  2517.7 24.5 reduce-scatter.74
  2545.2 24.5 reduce-scatter.72
  2573.5 287.0 all-reduce.69
where the time goes:
time: 2900 us; the launch traced here: 2890 us
  waiting for transfers between devices  1720 us (59%)
  blocking collectives  327 us (11%)
  other arithmetic  322 us (11%)
  matrix products  279 us (10%)
  local copies, waits for them, and re-layouts  201 us (7%)
    psum x1, waiting for transfers between devices, reduce_grads(): lax.psum(parted[1].astype(jnp.bfloat16), 'ctx').astype(jnp.float32)  233 us
    reduce_scatter x2, waiting for transfers between devices, reduce_grads(): lax.psum_scatter(g_in_proj.astype(jnp.bfloat16), 'fsdp', scatter_dimensio...  161 us
    dot_general x54, matrix products, product(): return jnp.dot(matrix_a, matrix_b, preferred_element_type=jnp.float32)  148 us
    all_gather x2, waiting for transfers between devices, carried_in_2(): lax.all_gather(part.astype(kind), axis)  126 us
    reduce_scatter x2, waiting for transfers between devices, reduce_grads(): lax.psum_scatter(g_gate_proj.astype(jnp.bfloat16), 'fsdp', scatter_dimens...  113 us
    reduce_scatter x2, waiting for transfers between devices, reduce_grads(): lax.psum_scatter(g_up_proj.astype(jnp.bfloat16), 'fsdp', scatter_dimensio...  112 us
    reduce_scatter x2, waiting for transfers between devices, reduce_grads(): lax.psum_scatter(g_down_proj.astype(jnp.bfloat16), 'fsdp', scatter_dimens...  111 us
    all_gather x2, waiting for transfers between devices, gather_layer(): lax.all_gather(gate_proj[layer_idx], 'fsdp', axis=0, tiled=True)  105 us
  transfers between devices with their start and end apart: 47, of which 34 were waited for; matrix products, arithmetic and copies ran while one was open for 18% of the time, Pallas kernels for 0%

commit v1 on v0

v1 whole, which is shorter than its diff:
```python
import math

import jax
import jax.numpy as jnp
from jax import lax
from jax.sharding import Mesh, PartitionSpec as P

QH = 8
KVH = 2
HD = 128
MH = 24
MP = 64
NS = 128
CONV = 4
LAYERS = 2
SEQS = 3
DSSM = 1536
CONVCH = 1792
TP = 8
ZZ = 4
PAR = 2
HEADS = MH // TP
XW = HEADS * MP
CW = XW + 2 * NS
CHUNK = 128

EPSILON = 1e-05
ROPE_BASE = 100000000000.0
MASKED = -1e30
BF = jnp.bfloat16
F32 = jnp.float32
TPA = ("zz", "par")


def dot(a, b):
    return jnp.dot(a, b, preferred_element_type=F32)


def dot_nt(a, b):
    return lax.dot_general(a, b, (((1,), (1,)), ((), ())), preferred_element_type=F32)


def dot_tn(a, b):
    return lax.dot_general(a, b, (((0,), (0,)), ((), ())), preferred_element_type=F32)


def rotate(vectors, cosine, sine):
    half = HD // 2
    a = vectors[:, :half]
    b = vectors[:, half:]
    return jnp.concatenate([a * cosine - b * sine, b * cosine + a * sine], axis=-1)


def one_hot(index, count):
    return (index[:, None] == jnp.arange(count, dtype=jnp.int32)[None, :]).astype(BF)


def inv_rms(values):
    return lax.rsqrt(jnp.mean(values * values, axis=-1, keepdims=True) + EPSILON)


def rms_back(grad_y, values, inv, gain):
    scaled = values * inv
    gg = grad_y * gain
    grad_v = (gg - scaled * jnp.mean(gg * scaled, axis=-1, keepdims=True)) * inv
    grad_g = jnp.sum(grad_y * scaled, axis=0)
    return grad_v, grad_g


def ssd_local(conv_in, dt_raw, conv_weight, conv_bias, dt_bias, decay_log, skip_gain, seg, pos):
    rows = conv_in.shape[0]
    conv_sum = conv_bias[None, :] + conv_weight[CONV - 1][None, :] * conv_in
    for lag in range(1, CONV):
        shifted = jnp.concatenate(
            [jnp.zeros((lag, CW), conv_in.dtype), conv_in[: rows - lag]], axis=0
        )
        conv_sum = conv_sum + conv_weight[CONV - 1 - lag][None, :] * jnp.where(
            (pos >= lag)[:, None], shifted, 0.0
        )
    conv_out = jax.nn.silu(conv_sum)
    rounded = lax.optimization_barrier(conv_out.astype(BF)).astype(F32)
    conv_out = conv_out + lax.stop_gradient(rounded - conv_out)
    chunks = rows // CHUNK
    xs = conv_out[:, :XW].reshape(chunks, CHUNK, HEADS, MP)
    bm = conv_out[:, XW : XW + NS].reshape(chunks, CHUNK, NS)
    cm = conv_out[:, XW + NS :].reshape(chunks, CHUNK, NS)
    dt = jax.nn.softplus(dt_raw + dt_bias[None, :]).reshape(chunks, CHUNK, HEADS)
    la = -dt * jnp.exp(decay_log)
    cum = jnp.cumsum(la, axis=1)
    sg = seg.reshape(chunks, CHUNK)
    causal = (sg[:, :, None] == sg[:, None, :]) & jnp.tril(jnp.ones((CHUNK, CHUNK), bool))[None]
    cum_t = cum.transpose(0, 2, 1)
    dt_t = dt.transpose(0, 2, 1)
    gap = jnp.where(causal[:, None], cum_t[:, :, :, None] - cum_t[:, :, None, :], MASKED)
    cb = jnp.einsum("cin,cjn->cij", cm, bm)
    kern = jnp.exp(gap) * cb[:, None] * dt_t[:, :, None, :]
    y = jnp.einsum("chij,cjhp->cihp", kern, xs)
    last = cum[:, -1, :]
    wend = (
        jnp.exp(last[:, None, :] - cum) * dt * (sg == sg[:, -1:]).astype(F32)[:, :, None]
    )
    ends = jnp.einsum("cjh,cjhp,cjn->chpn", wend, xs, bm)
    running = jnp.cumsum(last, axis=0)
    before = running - last
    ids = jnp.arange(chunks)
    seg_last = sg[:, -1]
    prev_seg = jnp.concatenate([jnp.full((1,), -1, seg_last.dtype), seg_last[:-1]])
    flows = (ids[:, None] > ids[None, :]) & (prev_seg[:, None] == seg_last[None, :])
    carry = jnp.exp(jnp.where(flows[:, :, None], before[:, None, :] - running[None, :, :], MASKED))
    state_in = jnp.einsum("cdh,dhpn->chpn", carry, ends)
    win = jnp.exp(cum) * (sg == prev_seg[:, None]).astype(F32)[:, :, None]
    y = y + jnp.einsum("cin,chpn->cihp", cm, state_in) * win[..., None]
    y = y + skip_gain[None, None, :, None] * xs
    return y.reshape(rows, XW)


def attn_block(q, k, seg_q, pos_q, seg, pos):
    scores = dot_nt(q, k) * HD ** (-0.5)
    allowed = (seg_q[:, None] == seg[None, :]) & (pos[None, :] <= pos_q[:, None])
    return jnp.where(allowed, scores, MASKED)


def in_blocks(step, carry, arrays):
    rows = arrays[0].shape[0]
    size = min(rows, 1024 * 1024 // rows)
    if size == rows:
        return step(carry, arrays)
    split = tuple(a.reshape((rows // size, size) + a.shape[1:]) for a in arrays)
    carry, outs = lax.scan(step, carry, split)
    return carry, jax.tree.map(lambda o: o.reshape((rows,) + o.shape[2:]), outs)


def attn_forward(q, k, v, seg, pos):
    def step(carry, block):
        q_b, seg_b, pos_b = block
        scores = attn_block(q_b, k, seg_b, pos_b, seg, pos)
        top = jnp.max(scores, axis=-1, keepdims=True)
        prob = jnp.exp(scores - top)
        total = jnp.sum(prob, axis=-1, keepdims=True)
        return carry, (dot(prob.astype(BF), v) / total, top + jnp.log(total))

    return in_blocks(step, 0.0, (q, seg, pos))[1]


def attn_backward(q, k, v, grad, delta, logs, seg, pos):
    def step(carry, block):
        q_b, grad_b, delta_b, logs_b, seg_b, pos_b = block
        prob = jnp.exp(attn_block(q_b, k, seg_b, pos_b, seg, pos) - logs_b)
        gs = (prob * (dot_nt(grad_b, v) - delta_b)).astype(BF)
        gk = carry[0] + dot_tn(gs, q_b) * HD ** (-0.5)
        gv = carry[1] + dot_tn(prob.astype(BF), grad_b)
        return (gk, gv), dot(gs, k) * HD ** (-0.5)

    zero = jnp.zeros(k.shape, F32)
    (gk, gv), gq = in_blocks(step, (zero, zero), (q, grad, delta, logs, seg, pos))
    return gq, gk, gv


def layer_forward(h, w, meta):
    seg, pos, cosine, sine = meta
    inv1 = inv_rms(h)
    normed = (h * inv1 * w["norm_gain"]).astype(BF)
    pr = dot(normed, w["w1"])
    proj = pr[:, :768].astype(BF)
    q = rotate(pr[:, 768:896], cosine, sine).astype(BF)
    k = rotate(pr[:, 896:1024], cosine, sine).astype(BF)
    v = pr[:, 1024:1152].astype(BF)
    z = proj[:, :XW].astype(F32)
    conv_in = proj[:, XW : XW + CW].astype(F32)
    dt_raw = proj[:, XW + CW : XW + CW + HEADS].astype(F32)

    def run(ci, dr, cw, cb, db, dl, sk):
        return ssd_local(ci, dr, cw, cb, db, dl, sk, seg, pos)

    ssd, pull = jax.vjp(
        run,
        conv_in,
        dt_raw,
        w["conv_weight"],
        w["conv_bias"],
        w["dt_bias"],
        w["decay_log"],
        w["skip_gain"],
    )
    gated = ssd * jax.nn.silu(z)
    square = lax.psum(jnp.sum(gated * gated, axis=-1), TPA)
    attended, logs = attn_forward(q, k, v, seg, pos)
    inv_g = lax.rsqrt(square / DSSM + EPSILON)[:, None]
    mixer = (gated * inv_g * w["mixer_gain"]).astype(BF)
    att_low = attended.astype(BF)
    mixed = jnp.concatenate([mixer, att_low], axis=1)
    mid = h + lax.psum(dot(mixed, w["wr"][: XW + HD]).astype(BF), TPA).astype(F32)
    inv2 = inv_rms(mid)
    normed2 = (mid * inv2 * w["ffn_gain"]).astype(BF)
    gu = dot(normed2, w["w2"])
    ff = gu.shape[1] // 2
    act = (jax.nn.silu(gu[:, :ff]) * gu[:, ff:]).astype(BF)
    kept = dict(
        h=h, inv1=inv1, normed=normed, z=z, ssd=ssd, gated=gated, pull=pull, inv_g=inv_g,
        q=q, k=k, v=v, attended=attended, logs=logs, mixed=mixed, mid=mid, inv2=inv2,
        normed2=normed2, gu=gu, act=act,
    )
    return mid, act, kept


def layer_backward(gout, w, kept, meta):
    seg, pos, cosine, sine = meta
    g_down = gout.astype(BF)
    g_act = dot_nt(g_down, w["wr"][XW + HD :])
    d_down = dot_tn(kept["act"], g_down)
    ff = kept["gu"].shape[1] // 2
    gate, up = kept["gu"][:, :ff], kept["gu"][:, ff:]
    sig = jax.nn.sigmoid(gate)
    g_gate = g_act * up * sig * (1.0 + gate * (1.0 - sig))
    g_up = g_act * gate * sig
    g_gu = jnp.concatenate([g_gate.astype(BF), g_up.astype(BF)], axis=1)
    g_n2 = lax.psum(dot_nt(g_gu, w["w2"]).astype(BF), TPA).astype(F32)
    d_w2 = dot_tn(kept["normed2"], g_gu)
    g_mid, d_ffn_gain = rms_back(g_n2, kept["mid"], kept["inv2"], w["ffn_gain"])
    g_mid = gout + g_mid
    g_low = g_mid.astype(BF)
    g_mixed = dot_nt(g_low, w["wr"][: XW + HD])
    d_wr = dot_tn(kept["mixed"], g_low)
    g_mix = g_mixed[:, :XW]
    scaled = kept["gated"] * kept["inv_g"]
    gg = g_mix * w["mixer_gain"]
    d_mixer_gain = jnp.sum(g_mix * scaled, axis=0)
    mean = lax.psum(jnp.sum(gg * scaled, axis=-1), TPA)[:, None] / DSSM
    g_att = g_mixed[:, XW:].astype(BF)
    delta = jnp.sum(g_att.astype(F32) * kept["attended"], axis=-1, keepdims=True)
    gq, gk, gv = attn_backward(
        kept["q"], kept["k"], kept["v"], g_att, delta, kept["logs"], seg, pos
    )
    gq = rotate(gq.astype(BF).astype(F32), cosine, -sine).astype(BF)
    gk = rotate(gk.astype(BF).astype(F32), cosine, -sine).astype(BF)
    g_gated = (gg - scaled * mean) * kept["inv_g"]
    z = kept["z"]
    sz = jax.nn.sigmoid(z)
    g_ssd = g_gated * z * sz
    g_z = g_gated * kept["ssd"] * sz * (1.0 + z * (1.0 - sz))
    g_conv, g_dt, d_cw, d_cb, d_db, d_dl, d_sk = kept["pull"](g_ssd)
    rows = gout.shape[0]
    g_pr = jnp.concatenate(
        [
            g_z.astype(BF),
            g_conv.astype(BF),
            g_dt.astype(BF),
            jnp.zeros((rows, 128 - HEADS), BF),
            gq,
            gk,
            gv.astype(BF),
        ],
        axis=1,
    )
    g_n1 = lax.psum(dot_nt(g_pr, w["w1"]).astype(BF), TPA).astype(F32)
    d_w1 = dot_tn(kept["normed"], g_pr)
    g_h, d_norm_gain = rms_back(g_n1, kept["h"], kept["inv1"], w["norm_gain"])
    small = (d_norm_gain, d_cw, d_cb, d_db, d_dl, d_sk, d_mixer_gain, d_ffn_gain)
    return g_mid + g_h, (d_w1, d_w2, d_wr, d_down), small


def per_device(
    block_in,
    seq_lengths,
    norm_gain,
    in_proj,
    conv_weight,
    conv_bias,
    dt_bias,
    decay_log,
    skip_gain,
    mixer_gain,
    out_proj,
    query_proj,
    key_proj,
    value_proj,
    attn_proj,
    ffn_gain,
    gate_proj,
    up_proj,
    down_proj,
    out_grad,
):
    fs = lax.axis_size("fsdp")
    reps = lax.axis_size("rep")
    ctx = reps * TP
    own_rows, width = block_in.shape
    rows = ctx * own_rows
    f = lax.axis_index("fsdp")
    rep = lax.axis_index("rep")
    t = lax.axis_index(TPA)
    every = ("rep",) + TPA

    lengths = seq_lengths[0]
    ends = jnp.cumsum(lengths)
    starts = ends - lengths
    line = jnp.arange(rows, dtype=jnp.int32)
    seg = jnp.sum((line[:, None] >= ends[None, :]).astype(jnp.int32), axis=1)
    pos = line - jnp.sum(jnp.where(seg[:, None] == jnp.arange(SEQS)[None, :], starts[None, :], 0), axis=1)
    pieces = lengths // ctx
    p_ends = jnp.cumsum(pieces)
    p_starts = p_ends - pieces
    local = line % own_rows
    piece = line // own_rows
    l_seg = jnp.sum((local[:, None] >= p_ends[None, :]).astype(jnp.int32), axis=1)
    pick = l_seg[:, None] == jnp.arange(SEQS)[None, :]
    place = (
        jnp.sum(jnp.where(pick, starts[None, :] - p_starts[None, :] + piece[:, None] * pieces[None, :], 0), axis=1)
        + local
    )
    half = HD // 2
    frequency = jnp.exp(-math.log(ROPE_BASE) * jnp.arange(half, dtype=F32) / half)
    angles = pos.astype(F32)[:, None] * frequency[None, :]
    meta = (seg, pos, jnp.cos(angles), jnp.sin(angles))

    to_seq = one_hot(place, rows).T
    x_all = lax.all_gather(block_in, every, axis=0, tiled=True)

    def columns(layer):
        pieces_1 = [
            lax.dynamic_slice_in_dim(in_proj[layer], XW * t, XW, 1),
            lax.dynamic_slice_in_dim(in_proj[layer], DSSM + XW * t, XW, 1),
            in_proj[layer][:, 2 * DSSM : DSSM + CONVCH],
            lax.dynamic_slice_in_dim(in_proj[layer], DSSM + CONVCH + HEADS * t, HEADS, 1),
            jnp.zeros((in_proj.shape[1], 128 - HEADS), BF),
            lax.dynamic_slice_in_dim(query_proj[layer], HD * t, HD, 1),
            lax.dynamic_slice_in_dim(key_proj[layer], HD * (t * KVH // TP), HD, 1),
            lax.dynamic_slice_in_dim(value_proj[layer], HD * (t * KVH // TP), HD, 1),
        ]
        ff = gate_proj.shape[2] // TP
        pieces_2 = [
            lax.dynamic_slice_in_dim(gate_proj[layer], ff * t, ff, 1),
            lax.dynamic_slice_in_dim(up_proj[layer], ff * t, ff, 1),
        ]
        return jnp.concatenate(pieces_1, 1), jnp.concatenate(pieces_2, 1)

    par = t % PAR
    ff = gate_proj.shape[2] // TP

    def row_pieces(layer):
        return jnp.concatenate(
            [
                lax.dynamic_slice_in_dim(out_proj[layer], XW * par, XW, 0),
                lax.dynamic_slice_in_dim(attn_proj[layer], HD * par, HD, 0),
                lax.dynamic_slice_in_dim(down_proj[layer], ff * par, ff, 0),
            ],
            0,
        )

    forth = []
    for s in range(fs):
        for r in range(reps):
            for c in range(TP):
                src = (s * reps + r) * TP + c
                dst = ((c // PAR) * reps + r) * TP + PAR * s + c % PAR
                forth.append((src, dst))
    back = [(b, a) for a, b in forth]
    axes = ("fsdp",) + every

    smalls = jnp.concatenate(
        [
            norm_gain,
            conv_weight.transpose(0, 2, 1).reshape(LAYERS, -1),
            conv_bias,
            dt_bias,
            decay_log,
            skip_gain,
            mixer_gain,
            ffn_gain,
        ],
        axis=1,
    )
    small_all = lax.all_gather(smalls, "fsdp", axis=0)
    w1_own, w2_own = zip(*[columns(layer) for layer in range(LAYERS)])
    w1 = [None, None]
    w2 = [None, None]
    wr = [None, None]
    for layer in range(LAYERS):
        w1[layer] = lax.all_gather(w1_own[layer], "fsdp", axis=0, tiled=True)
        wr[layer] = lax.ppermute(row_pieces(layer), axes, forth)
        w2[layer] = lax.all_gather(w2_own[layer], "fsdp", axis=0, tiled=True)
    g_all = lax.all_gather(out_grad, every, axis=0, tiled=True)

    sizes = [
        norm_gain.shape[1],
        CONV * conv_weight.shape[1],
        conv_bias.shape[1],
        dt_bias.shape[1],
        decay_log.shape[1],
        skip_gain.shape[1],
        mixer_gain.shape[1],
        ffn_gain.shape[1],
    ]
    offsets = [sum(sizes[:i]) for i in range(len(sizes) + 1)]

    def own_conv(full):
        return jnp.concatenate(
            [lax.dynamic_slice_in_dim(full, XW * t, XW, full.ndim - 1), full[..., DSSM:]], -1
        )

    weights = []
    for layer in range(LAYERS):
        part = [
            small_all[:, layer, offsets[i] : offsets[i + 1]].astype(F32) for i in range(len(sizes))
        ]
        cw = part[1].reshape(fs, CONV, -1).transpose(1, 0, 2).reshape(CONV, CONVCH)
        full = [p.reshape(-1) for p in part]
        weights.append(
            dict(
                w1=w1[layer],
                w2=w2[layer],
                wr=wr[layer],
                norm_gain=full[0],
                conv_weight=own_conv(cw),
                conv_bias=own_conv(full[2]),
                dt_bias=lax.dynamic_slice_in_dim(full[3], HEADS * t, HEADS, 0),
                decay_log=lax.dynamic_slice_in_dim(full[4], HEADS * t, HEADS, 0),
                skip_gain=lax.dynamic_slice_in_dim(full[5], HEADS * t, HEADS, 0),
                mixer_gain=lax.dynamic_slice_in_dim(full[6], XW * t, XW, 0),
                ffn_gain=full[7],
            )
        )

    h = dot(to_seq, x_all)
    saved = []
    for layer in range(LAYERS):
        mid, act, kept = layer_forward(h, weights[layer], meta)
        saved.append(kept)
        if layer < LAYERS - 1:
            h = mid + lax.psum(dot(act, weights[layer]["wr"][XW + HD :]).astype(BF), TPA).astype(F32)

    own_place = lax.dynamic_slice_in_dim(place, (rep * TP + t) * own_rows, own_rows, 0)
    own_hot = one_hot(own_place, rows)
    rep_place = lax.dynamic_slice_in_dim(place, rep * TP * own_rows, TP * own_rows, 0)
    act_rep = dot(one_hot(rep_place, rows), act).astype(BF)
    down_own = lax.psum_scatter(
        dot(act_rep, weights[-1]["wr"][XW + HD :]).astype(BF), TPA, scatter_dimension=0, tiled=True
    )
    mid_own = jnp.dot(
        own_hot.astype(F32), mid, precision=lax.Precision.HIGHEST, preferred_element_type=F32
    )
    block_out = (mid_own + down_own.astype(F32)).astype(BF)

    gout = dot(to_seq, g_all)
    big = [None, None]
    small = [None, None]
    for layer in reversed(range(LAYERS)):
        gout, grads, small_grads = layer_backward(gout, weights[layer], saved[layer], meta)
        d_w1, d_w2, d_wr, d_down = grads
        col_2 = lax.psum_scatter(d_w2.astype(BF), "fsdp", scatter_dimension=0, tiled=True)
        d_rows = jnp.concatenate([d_wr.astype(BF), d_down.astype(BF)], 0)
        d_rows = lax.ppermute(d_rows, axes, back)
        d_rows = lax.psum_scatter(d_rows, "zz", scatter_dimension=0, tiled=True)
        col_1 = lax.psum_scatter(d_w1.astype(BF), "fsdp", scatter_dimension=0, tiled=True)
        big[layer] = (
            lax.all_gather(col_1, TPA, axis=0),
            lax.all_gather(col_2, TPA, axis=0),
            lax.all_gather(d_rows, TPA, axis=0),
        )
        small[layer] = small_grads
    in_grad = dot(own_hot, gout.astype(BF)).astype(BF)

    first = (t == 0).astype(F32)

    def spread_conv(vec):
        zero = jnp.zeros(vec.shape[:-1] + (DSSM,), F32)
        at = (0,) * (vec.ndim - 1) + (XW * t,)
        return jnp.concatenate(
            [lax.dynamic_update_slice(zero, vec[..., :XW], at), vec[..., XW:]], -1
        )

    def spread(vec, count):
        return lax.dynamic_update_slice(jnp.zeros((count,), F32), vec, (vec.shape[0] * t,))

    flat = []
    for layer in range(LAYERS):
        g_n, g_cw, g_cb, g_db, g_dl, g_sk, g_mg, g_fg = small[layer]
        flat += [
            g_n * first,
            spread_conv(g_cw).T.reshape(-1),
            spread_conv(g_cb),
            spread(g_db, MH),
            spread(g_dl, MH),
            spread(g_sk, MH),
            spread(g_mg, DSSM),
            g_fg * first,
        ]
    summed = lax.psum(jnp.concatenate(flat), ("fsdp",) + TPA)
    full_sizes = [fs * s for s in sizes] * LAYERS
    outs_small = [[] for _ in sizes]
    at = 0
    for i, size in enumerate(full_sizes):
        own = size // fs
        outs_small[i % len(sizes)].append(lax.dynamic_slice_in_dim(summed, at + own * f, own, 0))
        at += size
    (o_norm, o_cw, o_cb, o_db, o_dl, o_sk, o_mg, o_fg) = [jnp.stack(o) for o in outs_small]
    o_cw = o_cw.reshape(LAYERS, -1, CONV)

    def joined(parts):
        return parts.transpose(1, 0, 2).reshape(parts.shape[1], -1)

    o_in, o_q, o_k, o_v, o_gate, o_up, o_out, o_attn, o_down = [[] for _ in range(9)]
    for layer in range(LAYERS):
        c1, c2, rw = big[layer]
        c1 = c1.astype(F32)
        c2 = c2.astype(F32)
        bc = jnp.sum(c1[:, :, 2 * XW : XW + CW], axis=0)
        o_in.append(
            jnp.concatenate(
                [
                    joined(c1[:, :, :XW]),
                    joined(c1[:, :, XW : 2 * XW]),
                    bc,
                    joined(c1[:, :, XW + CW : XW + CW + HEADS]),
                ],
                1,
            )
        )
        o_q.append(joined(c1[:, :, 768:896]))
        group = TP // KVH
        o_k.append(joined(jnp.sum(c1[:, :, 896:1024].reshape(KVH, group, -1, HD), axis=1)))
        o_v.append(joined(jnp.sum(c1[:, :, 1024:1152].reshape(KVH, group, -1, HD), axis=1)))
        o_gate.append(joined(c2[:, :, :ff]))
        o_up.append(joined(c2[:, :, ff:]))
        rw = rw.astype(F32).reshape(ZZ, PAR, -1, width).transpose(1, 0, 2, 3)
        rw = rw.reshape(PAR, -1, width)
        o_out.append(rw[:, :XW].reshape(-1, width))
        o_attn.append(rw[:, XW : XW + HD].reshape(-1, width))
        o_down.append(rw[:, XW + HD :].reshape(-1, width))

    return (
        block_out,
        in_grad,
        o_norm,
        jnp.stack(o_in),
        o_cw,
        o_cb,
        o_db,
        o_dl,
        o_sk,
        o_mg,
        jnp.stack(o_out),
        jnp.stack(o_q),
        jnp.stack(o_k),
        jnp.stack(o_v),
        jnp.stack(o_attn),
        o_fg,
        jnp.stack(o_gate),
        jnp.stack(o_up),
        jnp.stack(o_down),
    )


def solution(mesh):
    fs = mesh.shape["fsdp"]
    inner = Mesh(
        mesh.devices.reshape(fs, mesh.shape["ctx"] // TP, ZZ, PAR), ("fsdp", "rep", "zz", "par")
    )
    tokens = P(("fsdp", "rep", "zz", "par"), None)
    vec = P(None, "fsdp")
    mat = P(None, "fsdp", None)
    kinds = (
        vec, mat, mat, vec, vec, vec, vec, vec, mat, mat, mat, mat, mat, vec, mat, mat, mat
    )
    return jax.shard_map(
        per_device,
        mesh=inner,
        in_specs=(tokens, P("fsdp", None)) + kinds + (tokens,),
        out_specs=(tokens, tokens) + kinds,
        check_vma=False,
    )
```

time: 2900 us -> 1960 us (0.68)
  waiting for transfers between devices: 1720 us -> 1180 us
  blocking collectives: 327 us -> 67.8 us
  other arithmetic: 322 us -> 210 us
  matrix products: 279 us -> 177 us
  local copies, waits for them, and re-layouts: 201 us -> 258 us
    reduce_scatter x22 -> x7, waiting for transfers between devices: 777 us -> 244 us  [the longest x2 80.5 us: per_device(): lax.psum_scatter(d_w1.astype(BF), 'fsdp', scatter_dimension=0, tiled=True)]
    psum x1 -> x8, waiting for transfers between devices: 233 us -> 637 us  [the longest x2 186 us: layer_backward(): g_n1 = lax.psum(dot_nt(g_pr, w['w1']).astype(BF), TPA).astype(F32)]
    all_gather x18 -> x12, waiting for transfers between devices: 663 us -> 302 us  [the longest x2 68.6 us: per_device(): lax.all_gather(col_1, TPA, axis=0)]
    all_gather x20 -> x1, blocking collectives: 267 us -> 6.83 us  [per_device(): small_all = lax.all_gather(smalls, 'fsdp', axis=0)]
    scatter-add x14 -> x0, other arithmetic: 103 us -> none  [the longest x6 93 us: scan_block(): fetched = previous[sequence, jnp.clip(CONV - 1 - before, 0, CONV - 2)]]
    dot_general x102 -> x70, matrix products: 279 us -> 177 us  [the longest x15 67.1 us: dot(): return jnp.dot(a, b, preferred_element_type=F32)]
    select_n x49 -> x10, other arithmetic: 81.1 us -> 7.59 us  [the longest x6 6.16 us: ssd_local(): jnp.where((pos >= lag)[:, None], shifted, 0.0)]
    unnamed x45 -> x27, waiting for transfers between devices: 49 us -> 1.11 us
  transfers between devices with their start and end apart: 47 -> 31, of which waited for: 34 -> 26; matrix products, arithmetic and copies ran while one was open for 18% -> 17% of each run, Pallas kernels for 0% -> 0%
where the time goes in v1:
time: 1960 us; the launch traced here: 1940 us
  waiting for transfers between devices  1180 us (60%)
  local copies, waits for them, and re-layouts  258 us (13%)
  other arithmetic  210 us (11%)
  matrix products  177 us (9%)
  blocking collectives  67.8 us (3%)
  starting transfers between devices  25.1 us (1%)
    psum x2, waiting for transfers between devices, layer_backward(): g_n1 = lax.psum(dot_nt(g_pr, w['w1']).astype(BF), TPA).astype(F32)  186 us
    psum x1, waiting for transfers between devices, per_device(): summed = lax.psum(jnp.concatenate(flat), ('fsdp',) + TPA)  124 us
    psum x2, waiting for transfers between devices, layer_backward(): g_n2 = lax.psum(dot_nt(g_gu, w['w2']).astype(BF), TPA).astype(F32)  118 us
    psum x2, waiting for transfers between devices, layer_forward(): lax.psum(dot(mixed, w['wr'][:XW + HD]).astype(BF), TPA).astype(F32)  111 us
    psum x1, waiting for transfers between devices, per_device(): lax.psum(dot(act, weights[layer]['wr'][XW + HD:]).astype(BF), TPA)  98.7 us
    reduce_scatter x2, waiting for transfers between devices, per_device(): lax.psum_scatter(d_w1.astype(BF), 'fsdp', scatter_dimension=0, tiled=True)  80.5 us
    reduce_scatter x2, waiting for transfers between devices, per_device(): lax.psum_scatter(d_w2.astype(BF), 'fsdp', scatter_dimension=0, tiled=True)  71.8 us
    all_gather x2, waiting for transfers between devices, per_device(): lax.all_gather(col_1, TPA, axis=0)  68.6 us
  transfers between devices with their start and end apart: 31, of which 26 were waited for; matrix products, arithmetic and copies ran while one was open for 17% of the time, Pallas kernels for 0%

profile of v1, /device:TPU:0, one launch (start us, length us, event | category | flops | bytes accessed | tf_op | source)
XLA Modules:
  0.0 1942.2 jit_solution(17561582725169451346)
XLA Ops:
  14.3 10.4 collective-permute-start
  38.6 7.5 concatenate.124
  46.5 6.8 all-gather.7
  63.4 36.3 %all-gather.21.cloned.1.call-done = bf16[1024,1024]{1,0:T(8,128)(2,1)} async-done(((bf16[128,1024]{1,0:T(8,128)(2,1)}), bf16[1024,1024]{1,0:T(8,128)(2,1)}) %all-gather.21.cloned.1.call-update) | async-done | bytes 2097168 | tf_op jit(solution)/shard_map/all_gather | solution.py:317
  99.6 6.2 multiply_reduce_fusion.3
  105.9 35.1 %all-gather.23.cloned.1.call-done = bf16[1024,1152]{0,1:T(8,128)(2,1)} async-done(((bf16[256,1152]{0,1:T(8,128)(2,1)}), bf16[1024,1152]{0,1:T(8,128)(2,1)}) %all-gather.23.cloned.1.call-update) | async-done | bytes 2359312 | tf_op jit(solution)/shard_map/all_gather | solution.py:379
  141.0 8.3 fusion.452
  153.8 4.3 fusion.295
  183.0 16.4 psum.84
  210.3 56.3 %all-reduce.37.cloned.1.call-done = bf16[1024,1024]{0,1:T(8,128)(2,1)} async-done(((bf16[1024,1024]{0,1:T(8,128)(2,1)}), bf16[1024,1024]{0,1:T(8,128)(2,1)}) %all-reduce.37.cloned.1.call-update) | async-done | bytes 2097168 | tf_op jit(solution)/shard_map/psum | solution.py:192
  266.6 6.0 multiply_reduce_fusion.2
  272.5 22.6 %all-gather.25.cloned.1.call-done = bf16[1024,512]{1,0:T(8,128)(2,1)} async-done(((bf16[256,512]{1,0:T(8,128)(2,1)}), bf16[1024,512]{1,0:T(8,128)(2,1)}) %all-gather.25.cloned.1.call-update) | async-done | bytes 1048592 | tf_op jit(solution)/shard_map/all_gather | solution.py:381
  309.6 8.4 concatenate.136
  320.4 10.4 collective-permute-start.1
  332.7 98.7 %all-reduce.39.cloned.1.call-done = bf16[1024,1024]{0,1:T(8,128)(2,1)} async-done(((bf16[1024,1024]{0,1:T(8,128)(2,1)}), bf16[1024,1024]{0,1:T(8,128)(2,1)}) %all-reduce.39.cloned.1.call-update) | async-done | bytes 2097168 | tf_op jit(solution)/shard_map/psum | solution.py:430
  431.5 6.0 multiply_reduce_fusion.1
  437.4 33.2 %all-gather.27.cloned.1.call-done = bf16[1024,1152]{0,1:T(8,128)(2,1)} async-done(((bf16[256,1152]{0,1:T(8,128)(2,1)}), bf16[1024,1152]{0,1:T(8,128)(2,1)}) %all-gather.27.cloned.1.call-update) | async-done | bytes 2359312 | tf_op jit(solution)/shard_map/all_gather | solution.py:379
  470.7 8.3 fusion.456
  490.4 4.3 fusion.296
  539.8 17.0 psum.87
  566.4 6.2 fusion.25
  572.6 54.2 %all-reduce.41.cloned.1.call-done = bf16[1024,1024]{0,1:T(8,128)(2,1)} async-done(((bf16[1024,1024]{0,1:T(8,128)(2,1)}), bf16[1024,1024]{0,1:T(8,128)(2,1)}) %all-reduce.41.cloned.1.call-update) | async-done | bytes 2097168 | tf_op jit(solution)/shard_map/psum | solution.py:192
  626.8 6.0 multiply_reduce_fusion
  633.5 22.1 %all-gather.29.cloned.1.call-done = bf16[1024,512]{1,0:T(8,128)(2,1)} async-done(((bf16[256,512]{1,0:T(8,128)(2,1)}), bf16[1024,512]{1,0:T(8,128)(2,1)}) %all-gather.29.cloned.1.call-update) | async-done | bytes 1048592 | tf_op jit(solution)/shard_map/all_gather | solution.py:381
  670.5 5.5 copy.943
  677.3 54.0 %all-reduce.43.cloned.1.call-done = bf16[1024,1024]{0,1:T(8,128)(2,1)} async-done(((bf16[1024,1024]{0,1:T(8,128)(2,1)}), bf16[1024,1024]{0,1:T(8,128)(2,1)}) %all-reduce.43.cloned.1.call-update) | async-done | bytes 2097168 | tf_op jit(solution)/shard_map/psum | solution.py:217
  731.3 4.9 fusion.21
  755.6 14.0 psum.90
  769.6 4.8 multiply_reduce_fusion.17
  823.1 5.9 fusion.426
  835.5 5.3 concatenate.146
  840.8 6.6 convolution_convert_fusion.3
  847.7 63.0 %all-reduce.45.cloned.1.call-done = bf16[1024,1024]{0,1:T(8,128)(2,1)} async-done(((bf16[1024,1024]{0,1:T(8,128)(2,1)}), bf16[1024,1024]{0,1:T(8,128)(2,1)}) %all-reduce.45.cloned.1.call-update) | async-done | bytes 2097168 | tf_op jit(solution)/shard_map/psum | solution.py:255
  910.7 4.9 fusion.22
  925.7 64.1 %all-reduce.47.cloned.1.call-done = bf16[1024,1024]{0,1:T(8,128)(2,1)} async-done(((bf16[1024,1024]{0,1:T(8,128)(2,1)}), bf16[1024,1024]{0,1:T(8,128)(2,1)}) %all-reduce.47.cloned.1.call-update) | async-done | bytes 2097168 | tf_op jit(solution)/shard_map/psum | solution.py:217
  989.8 4.9 fusion.23
  1007.2 13.6 psum.93
  1043.9 23.3 %fusion.461 = f32[8,128,3]{2,0,1:T(8,128)S(1)} fusion(f32[8,128,3]{2,0,1:T(8,128)S(1)} %copy.1011), kind=kOutput, calls=%fused_computation.783 | output fusion | flops 390144 | bytes 24576 | tf_op jit(solution)/shard_map/transpose(jvp(jit(cumsum)))/reduce_window_sum | solution.py:89
  1073.5 5.7 fusion.427
  1096.3 5.4 concatenate.148
  1101.7 6.6 convolution_convert_fusion.2
  1109.5 4.5 convolution_convert_fusion.10
  1114.1 4.6 convolution_convert_fusion.11
  1133.1 6.5 convolution_convert_fusion
  1141.3 6.5 convolution_convert_fusion.1
  1148.9 4.6 convolution_convert_fusion.8
  1159.5 123.3 %all-reduce.49.cloned.1.call-done = bf16[1024,1024]{0,1:T(8,128)(2,1)} async-done(((bf16[1024,1024]{0,1:T(8,128)(2,1)}), bf16[1024,1024]{0,1:T(8,128)(2,1)}) %all-reduce.49.cloned.1.call-update) | async-done | bytes 2097168 | tf_op jit(solution)/shard_map/psum | solution.py:255
  1287.8 41.2 %reduce-scatter.20.cloned.1.call-done = bf16[256,512]{1,0:T(8,128)(2,1)} async-done(((bf16[1024,512]{1,0:T(8,128)(2,1)}), bf16[256,512]{1,0:T(8,128)(2,1)}) %reduce-scatter.20.cloned.1.call-update) | async-done | bytes 262160 | tf_op jit(solution)/shard_map/reduce_scatter | solution.py:450
  1329.0 30.7 %reduce-scatter.18.cloned.1.call-done = bf16[256,512]{1,0:T(8,128)(2,1)} async-done(((bf16[1024,512]{1,0:T(8,128)(2,1)}), bf16[256,512]{1,0:T(8,128)(2,1)}) %reduce-scatter.18.cloned.1.call-update) | async-done | bytes 262160 | tf_op jit(solution)/shard_map/reduce_scatter | solution.py:450
  1359.7 31.9 %reduce-scatter.16.cloned.1.call-done = bf16[144,1024]{1,0:T(8,128)(2,1)} async-done(((bf16[576,1024]{1,0:T(8,128)(2,1)}), bf16[144,1024]{1,0:T(8,128)(2,1)}) %reduce-scatter.16.cloned.1.call-update) | async-done | bytes 294928 | tf_op jit(solution)/shard_map/reduce_scatter | solution.py:453
  1391.7 30.6 %reduce-scatter.14.cloned.1.call-done = bf16[144,1024]{1,0:T(8,128)(2,1)} async-done(((bf16[576,1024]{1,0:T(8,128)(2,1)}), bf16[144,1024]{1,0:T(8,128)(2,1)}) %reduce-scatter.14.cloned.1.call-update) | async-done | bytes 294928 | tf_op jit(solution)/shard_map/reduce_scatter | solution.py:453
  1422.4 39.5 %reduce-scatter.12.cloned.1.call-done = bf16[256,1152]{1,0:T(8,128)(2,1)} async-done(((bf16[1024,1152]{1,0:T(8,128)(2,1)}), bf16[256,1152]{1,0:T(8,128)(2,1)}) %reduce-scatter.12.cloned.1.call-update) | async-done | bytes 589840 | tf_op jit(solution)/shard_map/reduce_scatter | solution.py:454
  1462.0 41.0 %reduce-scatter.10.cloned.1.call-done = bf16[256,1152]{1,0:T(8,128)(2,1)} async-done(((bf16[1024,1152]{1,0:T(8,128)(2,1)}), bf16[256,1152]{1,0:T(8,128)(2,1)}) %reduce-scatter.10.cloned.1.call-update) | async-done | bytes 589840 | tf_op jit(solution)/shard_map/reduce_scatter | solution.py:454
  1503.1 4.8 fusion.249
  1512.2 29.2 %reduce-scatter.8.cloned.1.call-done = bf16[128,1024]{1,0:T(8,128)(2,1)} async-done(((bf16[1024,1024]{1,0:T(8,128)(2,1)}), bf16[128,1024]{1,0:T(8,128)(2,1)}) %reduce-scatter.8.cloned.1.call-update) | async-done | bytes 262160 | tf_op jit(solution)/shard_map/reduce_scatter | solution.py:436
  1543.2 123.7 %all-reduce.51.cloned.1.call-done = f32[25232]{0:T(1024)} async-done(((f32[25232]{0:T(1024)}), f32[25232]{0:T(1024)}) %all-reduce.51.cloned.1.call-update) | async-done | bytes 100944 | tf_op jit(solution)/shard_map/psum | solution.py:488
  1676.5 22.1 %all-gather.43.cloned.1.call-done = bf16[2048,512]{1,0:T(8,128)(2,1)} async-done(((bf16[256,512]{1,0:T(8,128)(2,1)}), bf16[2048,512]{1,0:T(8,128)(2,1)}) %all-gather.43.cloned.1.call-update) | async-done | bytes 2097168 | tf_op jit(solution)/shard_map/all_gather | solution.py:457
  1709.7 19.0 all-gather.41.cloned.1.call-done
  1739.8 4.9 pad_maximum_fusion.2
  1747.0 14.4 all-gather.39.cloned.1.call-done
  1765.2 28.6 %all-gather.37.cloned.1.call-done = bf16[1152,1024]{1,0:T(8,128)(2,1)} async-done(((bf16[144,1024]{1,0:T(8,128)(2,1)}), bf16[1152,1024]{1,0:T(8,128)(2,1)}) %all-gather.37.cloned.1.call-update) | async-done | bytes 2359312 | tf_op jit(solution)/shard_map/all_gather | solution.py:458
  1802.9 43.2 %all-gather.35.cloned.1.call-done = bf16[2048,1152]{1,0:T(8,128)(2,1)} async-done(((bf16[256,1152]{1,0:T(8,128)(2,1)}), bf16[2048,1152]{1,0:T(8,128)(2,1)}) %all-gather.35.cloned.1.call-update) | async-done | bytes 4718608 | tf_op jit(solution)/shard_map/all_gather | solution.py:456
  1857.8 4.6 slice_bitcast_fusion.5
  1872.9 25.3 %all-gather.33.cloned.1.call-done = bf16[2048,1152]{1,0:T(8,128)(2,1)} async-done(((bf16[256,1152]{1,0:T(8,128)(2,1)}), bf16[2048,1152]{1,0:T(8,128)(2,1)}) %all-gather.33.cloned.1.call-update) | async-done | bytes 4718608 | tf_op jit(solution)/shard_map/all_gather | solution.py:456
  (1156 shorter events, 455.1 us)
Async XLA Ops:
  7.2 92.4 %all-gather.21.cloned.1.call-start = ((), (), s32[]{:S(2)}) async-start(), calls=%async_computation.7 | async-start | bytes 2359296 | tf_op jit(solution)/shard_map/all_gather | solution.py:317
  7.9 133.0 %all-gather.23.cloned.1.call-start = ((), (), s32[]{:S(2)}) async-start(), calls=%async_computation.8 | async-start | bytes 2949120 | tf_op jit(solution)/shard_map/all_gather | solution.py:379
  14.3 185.4 %collective-permute-start = (bf16[576,1024]{1,0:T(8,128)(2,1)}, bf16[576,1024]{1,0:T(8,128)(2,1)}, u32[]{:S(2)}, u32[]{:S(2)}) collective-permute-start(bf16[576,1024]{1,0:T(8,128)(2,1)} %pad_maximum_fusion.7), channel_id=1, source_target_pairs={{0,0},{1,1},{2,8},{3,9},{4,16},{5,17},{6,24},{7,25},{8,2},{9,3},{1... | collective-permute-start | bytes 3538952 | tf_op jit(solution)/shard_map/ppermute | solution.py:380
  46.2 220.4 %all-reduce.37.cloned.1.call-start = ((), (), s32[]{:S(2)}) async-start(), calls=%async_computation.9 | async-start | bytes 4194304 | tf_op jit(solution)/shard_map/psum | solution.py:192
  56.8 49.0 %copy-start.171 = (f32[4,1792]{1,0:T(4,128)}, f32[4,1792]{1,0:T(4,128)S(1)}, u32[]{:S(2)}) copy-start(f32[4,1792]{1,0:T(4,128)S(1)} %reshape.892) | copy-start | bytes 86020
  57.1 115.5 %copy-start.140 = (s32[1024]{0:T(1024)}, s32[1024]{0:T(1024)S(1)}, u32[]{:S(2)}) copy-start(s32[1024]{0:T(1024)S(1)} %convert_reduce_fusion) | copy-start | bytes 12292
  57.3 48.6 %copy-start.275 = (f32[24]{0:T(128)}, f32[24]{0:T(128)S(1)}, u32[]{:S(2)}) copy-start(f32[24]{0:T(128)S(1)} %reshape.886) | copy-start | bytes 292
  57.4 48.5 %copy-start.277 = (f32[24]{0:T(128)}, f32[24]{0:T(128)S(1)}, u32[]{:S(2)}) copy-start(f32[24]{0:T(128)S(1)} %reshape.895) | copy-start | bytes 292
  57.7 92.0 %copy-start.289 = (f32[3]{0:T(128)}, f32[3]{0:T(128)S(1)}, u32[]{:S(2)}) copy-start(f32[3]{0:T(128)S(1)} %dynamic_slice.213) | copy-start | bytes 40
  59.0 92.1 %copy-start.272 = (f32[3]{0:T(128)}, f32[3]{0:T(128)S(1)}, u32[]{:S(2)}) copy-start(f32[3]{0:T(128)S(1)} %get-tuple-element.348) | copy-start | bytes 40
  60.7 93.0 %copy-start.212 = (f32[1,448]{1,0:T(1,128)}, f32[1,448]{1,0:T(1,128)S(1)}, u32[]{:S(2)}) copy-start(f32[1,448]{1,0:T(1,128)S(1)} %get-tuple-element.295) | copy-start | bytes 5380
  60.7 93.0 %copy-start.214 = (f32[1,448]{1,0:T(1,128)}, f32[1,448]{1,0:T(1,128)S(1)}, u32[]{:S(2)}) copy-start(f32[1,448]{1,0:T(1,128)S(1)} %get-tuple-element.296) | copy-start | bytes 5380
  60.7 93.0 %copy-start.216 = (f32[1,448]{1,0:T(1,128)}, f32[1,448]{1,0:T(1,128)S(1)}, u32[]{:S(2)}) copy-start(f32[1,448]{1,0:T(1,128)S(1)} %get-tuple-element.297) | copy-start | bytes 5380
  60.7 93.0 %copy-start.218 = (f32[1,448]{1,0:T(1,128)}, f32[1,448]{1,0:T(1,128)S(1)}, u32[]{:S(2)}) copy-start(f32[1,448]{1,0:T(1,128)S(1)} %get-tuple-element.298) | copy-start | bytes 5380
  61.1 109.5 %copy-start.203 = (pred[8,8]{1,0:T(8,128)(4,1)}, pred[8,8]{1,0:T(8,128)(4,1)S(1)}, u32[]{:S(2)}) copy-start(pred[8,8]{1,0:T(8,128)(4,1)S(1)} %fusion.374) | copy-start | bytes 196
  61.1 92.6 %copy-start.172 = (pred[1024]{0:T(1024)(128)(4,1)}, pred[1024]{0:T(1024)(128)(4,1)S(1)}, u32[]{:S(2)}) copy-start(pred[1024]{0:T(1024)(128)(4,1)S(1)} %get-tuple-element.309) | copy-start | bytes 3076
  61.1 92.6 %copy-start.175 = (pred[1024]{0:T(1024)(128)(4,1)}, pred[1024]{0:T(1024)(128)(4,1)S(1)}, u32[]{:S(2)}) copy-start(pred[1024]{0:T(1024)(128)(4,1)S(1)} %get-tuple-element.310) | copy-start | bytes 3076
  61.1 92.6 %copy-start.178 = (pred[1024]{0:T(1024)(128)(4,1)}, pred[1024]{0:T(1024)(128)(4,1)S(1)}, u32[]{:S(2)}) copy-start(pred[1024]{0:T(1024)(128)(4,1)S(1)} %get-tuple-element.311) | copy-start | bytes 3076
  61.2 44.7 %copy-start.285 = (s32[1024]{0:T(1024)}, s32[1024]{0:T(1024)S(1)}, u32[]{:S(2)}) copy-start(s32[1024]{0:T(1024)S(1)} %fusion.389) | copy-start | bytes 12292
  61.8 109.5 %copy-start.155 = (f32[1024]{0:T(1024)}, f32[1024]{0:T(1024)S(1)}, u32[]{:S(2)}) copy-start(f32[1024]{0:T(1024)S(1)} %get-tuple-element.312) | copy-start | bytes 12292
  61.9 101.1 %copy-start.159 = (f32[8,128]{1,0:T(8,128)}, f32[8,128]{1,0:T(8,128)S(1)}, u32[]{:S(2)}) copy-start(f32[8,128]{1,0:T(8,128)S(1)} %get-tuple-element.307) | copy-start | bytes 12292
  62.5 78.4 %copy-start.183 = (f32[4,1,256]{2,1,0:T(1,128)}, f32[4,1,256]{2,1,0:T(1,128)S(1)}, u32[]{:S(2)}) copy-start(f32[4,1,256]{2,1,0:T(1,128)S(1)} %get-tuple-element.285) | copy-start | bytes 12292
  62.5 232.6 %copy-start.194 = (f32[4,1,256]{2,1,0:T(1,128)}, f32[4,1,256]{2,1,0:T(1,128)S(1)}, u32[]{:S(2)}) copy-start(f32[4,1,256]{2,1,0:T(1,128)S(1)} %get-tuple-element.286) | copy-start | bytes 12292
  62.5 408.1 %copy-start.192 = (f32[4,1,256]{2,1,0:T(1,128)}, f32[4,1,256]{2,1,0:T(1,128)S(1)}, u32[]{:S(2)}) copy-start(f32[4,1,256]{2,1,0:T(1,128)S(1)} %get-tuple-element.284) | copy-start | bytes 12292
  105.9 43.4 %copy-start.181 = (f32[1024]{0:T(1024)}, f32[1024]{0:T(1024)S(1)}, u32[]{:S(2)}) copy-start(f32[1024]{0:T(1024)S(1)} %add_rsqrt_fusion.5) | copy-start | bytes 12292
  204.3 90.9 %all-gather.25.cloned.1.call-start = ((), (), s32[]{:S(2)}) async-start(), calls=%async_computation.10 | async-start | bytes 1310720 | tf_op jit(solution)/shard_map/all_gather | solution.py:381
  209.8 221.6 %all-reduce.39.cloned.1.call-start = ((), (), s32[]{:S(2)}) async-start(), calls=%async_computation.11 | async-start | bytes 4194304 | tf_op jit(solution)/shard_map/psum | solution.py:430
  272.5 26.5 %copy-start.186 = (f32[1024]{0:T(1024)}, f32[1024]{0:T(1024)S(1)}, u32[]{:S(2)}) copy-start(f32[1024]{0:T(1024)S(1)} %add_rsqrt_fusion.3) | copy-start | bytes 12292
  304.7 166.0 %all-gather.27.cloned.1.call-start = ((), (), s32[]{:S(2)}) async-start(), calls=%async_computation.12 | async-start | bytes 2949120 | tf_op jit(solution)/shard_map/all_gather | solution.py:379
  318.0 248.3 %all-gather.31.cloned.1.call-start = ((), (), s32[]{:S(2)}) async-start(), calls=%async_computation.16 | async-start | bytes 2359296 | tf_op jit(solution)/shard_map/all_gather | solution.py:382
  320.4 239.2 %collective-permute-start.1 = (bf16[576,1024]{1,0:T(8,128)(2,1)}, bf16[576,1024]{1,0:T(8,128)(2,1)}, u32[]{:S(2)}, u32[]{:S(2)}) collective-permute-start(bf16[576,1024]{1,0:T(8,128)(2,1)} %pad_maximum_fusion.8), channel_id=1, source_target_pairs={{0,0},{1,1},{2,8},{3,9},{4,16},{5,17},{6,24},{7,25},{8,2},{9,3},{1... | collective-permute-start | bytes 3538952 | tf_op jit(solution)/shard_map/ppermute | solution.py:380
  330.8 296.1 %all-reduce.41.cloned.1.call-start = ((), (), s32[]{:S(2)}) async-start(), calls=%async_computation.13 | async-start | bytes 4194304 | tf_op jit(solution)/shard_map/psum | solution.py:192
  331.1 148.2 %copy-start.291 = (f32[3]{0:T(128)}, f32[3]{0:T(128)S(1)}, u32[]{:S(2)}) copy-start(f32[3]{0:T(128)S(1)} %dynamic_slice.241) | copy-start | bytes 40
  332.6 157.7 %copy-start.220 = (f32[1,448]{1,0:T(1,128)}, f32[1,448]{1,0:T(1,128)S(1)}, u32[]{:S(2)}) copy-start(f32[1,448]{1,0:T(1,128)S(1)} %get-tuple-element.291) | copy-start | bytes 5380
  332.6 157.7 %copy-start.222 = (f32[1,448]{1,0:T(1,128)}, f32[1,448]{1,0:T(1,128)S(1)}, u32[]{:S(2)}) copy-start(f32[1,448]{1,0:T(1,128)S(1)} %get-tuple-element.292) | copy-start | bytes 5380
  332.6 157.7 %copy-start.224 = (f32[1,448]{1,0:T(1,128)}, f32[1,448]{1,0:T(1,128)S(1)}, u32[]{:S(2)}) copy-start(f32[1,448]{1,0:T(1,128)S(1)} %get-tuple-element.293) | copy-start | bytes 5380
  332.6 157.7 %copy-start.226 = (f32[1,448]{1,0:T(1,128)}, f32[1,448]{1,0:T(1,128)S(1)}, u32[]{:S(2)}) copy-start(f32[1,448]{1,0:T(1,128)S(1)} %get-tuple-element.294) | copy-start | bytes 5380
  437.4 41.5 %copy-start.188 = (f32[1024]{0:T(1024)}, f32[1024]{0:T(1024)S(1)}, u32[]{:S(2)}) copy-start(f32[1024]{0:T(1024)S(1)} %add_rsqrt_fusion.2) | copy-start | bytes 12292
  564.3 91.3 %all-gather.29.cloned.1.call-start = ((), (), s32[]{:S(2)}) async-start(), calls=%async_computation.14 | async-start | bytes 1310720 | tf_op jit(solution)/shard_map/all_gather | solution.py:381
  566.1 165.2 %all-reduce.43.cloned.1.call-start = ((), (), s32[]{:S(2)}) async-start(), calls=%async_computation.17 | async-start | bytes 4194304 | tf_op jit(solution)/shard_map/psum | solution.py:217
  666.3 244.4 %all-reduce.45.cloned.1.call-start = ((), (), s32[]{:S(2)}) async-start(), calls=%async_computation.18 | async-start | bytes 4194304 | tf_op jit(solution)/shard_map/psum | solution.py:255
  847.4 63.3 %copy-start.189 = (f32[1024]{0:T(1024)S(1)}, f32[1024]{0:T(1024)}, u32[]{:S(2)}) copy-start(f32[1024]{0:T(1024)} %copy-done.188) | copy-start | bytes 12292
  847.4 63.3 %copy-start.193 = (f32[4,1,256]{2,1,0:T(1,128)S(1)}, f32[4,1,256]{2,1,0:T(1,128)}, u32[]{:S(2)}) copy-start(f32[4,1,256]{2,1,0:T(1,128)} %copy-done.192) | copy-start | bytes 12292
  847.4 142.3 %all-reduce.47.cloned.1.call-start = ((), (), s32[]{:S(2)}) async-start(), calls=%async_computation.19 | async-start | bytes 4194304 | tf_op jit(solution)/shard_map/psum | solution.py:217
  925.0 64.8 %copy-start.187 = (f32[1024]{0:T(1024)S(1)}, f32[1024]{0:T(1024)}, u32[]{:S(2)}) copy-start(f32[1024]{0:T(1024)} %copy-done.186) | copy-start | bytes 12292
  925.0 64.8 %copy-start.195 = (f32[4,1,256]{2,1,0:T(1,128)S(1)}, f32[4,1,256]{2,1,0:T(1,128)}, u32[]{:S(2)}) copy-start(f32[4,1,256]{2,1,0:T(1,128)} %copy-done.194) | copy-start | bytes 12292
  925.0 357.7 %all-reduce.49.cloned.1.call-start = ((), (), s32[]{:S(2)}) async-start(), calls=%async_computation.20 | async-start | bytes 4194304 | tf_op jit(solution)/shard_map/psum | solution.py:255
  1108.4 220.6 %reduce-scatter.20.cloned.1.call-start = ((), (), s32[]{:S(2)}) async-start(), calls=%async_computation.27 | async-start | bytes 1310720 | tf_op jit(solution)/shard_map/reduce_scatter | solution.py:450
  1114.0 245.6 %reduce-scatter.18.cloned.1.call-start = ((), (), s32[]{:S(2)}) async-start(), calls=%async_computation.26 | async-start | bytes 1310720 | tf_op jit(solution)/shard_map/reduce_scatter | solution.py:450
  1118.8 272.9 %reduce-scatter.16.cloned.1.call-start = ((), (), s32[]{:S(2)}) async-start(), calls=%async_computation.25 | async-start | bytes 1474560 | tf_op jit(solution)/shard_map/reduce_scatter | solution.py:453
  1123.9 0.9 collective-permute-start.3
  1125.9 296.4 %reduce-scatter.14.cloned.1.call-start = ((), (), s32[]{:S(2)}) async-start(), calls=%async_computation.24 | async-start | bytes 1474560 | tf_op jit(solution)/shard_map/reduce_scatter | solution.py:453
  1131.1 0.9 collective-permute-start.2
  1133.0 328.9 %reduce-scatter.12.cloned.1.call-start = ((), (), s32[]{:S(2)}) async-start(), calls=%async_computation.23 | async-start | bytes 2949120 | tf_op jit(solution)/shard_map/reduce_scatter | solution.py:454
  1139.7 363.3 %reduce-scatter.10.cloned.1.call-start = ((), (), s32[]{:S(2)}) async-start(), calls=%async_computation.22 | async-start | bytes 2949120 | tf_op jit(solution)/shard_map/reduce_scatter | solution.py:454
  1147.9 393.6 %reduce-scatter.8.cloned.1.call-start = ((), (), s32[]{:S(2)}) async-start(), calls=%async_computation.15 | async-start | bytes 2359296 | tf_op jit(solution)/shard_map/reduce_scatter | solution.py:436
  1153.7 513.2 %all-reduce.51.cloned.1.call-start = ((), (), s32[]{:S(2)}) async-start(), calls=%async_computation.21 | async-start | bytes 204800 | tf_op jit(solution)/shard_map/psum | solution.py:488
  1287.7 410.8 %all-gather.43.cloned.1.call-start = ((), (), s32[]{:S(2)}) async-start(), calls=%async_computation.33 | async-start | bytes 2359296 | tf_op jit(solution)/shard_map/all_gather | solution.py:457
  1328.9 399.8 %all-gather.41.cloned.1.call-start = ((), (), s32[]{:S(2)}) async-start(), calls=%async_computation.32 | async-start | bytes 2359296 | tf_op jit(solution)/shard_map/all_gather | solution.py:457
  1359.7 401.7 %all-gather.39.cloned.1.call-start = ((), (), s32[]{:S(2)}) async-start(), calls=%async_computation.31 | async-start | bytes 2654208 | tf_op jit(solution)/shard_map/all_gather | solution.py:458
  1391.7 402.1 %all-gather.37.cloned.1.call-start = ((), (), s32[]{:S(2)}) async-start(), calls=%async_computation.30 | async-start | bytes 2654208 | tf_op jit(solution)/shard_map/all_gather | solution.py:458
  1422.3 85.6 %copy-start.37 = (bf16[1024,1024]{0,1:T(8,128)(2,1)S(1)}, bf16[1024,1024]{0,1:T(8,128)(2,1)}, u32[]{:S(2)}) copy-start(bf16[1024,1024]{0,1:T(8,128)(2,1)} %all-reduce.49.cloned.1.call-done) | copy-start | bytes 6291460
  1422.3 423.8 %all-gather.35.cloned.1.call-start = ((), (), s32[]{:S(2)}) async-start(), calls=%async_computation.29 | async-start | bytes 5308416 | tf_op jit(solution)/shard_map/all_gather | solution.py:456
  1461.9 436.3 %all-gather.33.cloned.1.call-start = ((), (), s32[]{:S(2)}) async-start(), calls=%async_computation.28 | async-start | bytes 5308416 | tf_op jit(solution)/shard_map/all_gather | solution.py:456
  (289 other events, 1119.2 us)
Sparse Core Ops, SparseCore 0:
  9.6 89.9 all-gather.20
  102.0 38.8 all-gather.22
  204.4 62.1 all-reduce.36
  268.8 26.2 all-gather.24
  304.8 126.6 all-reduce.38
  433.7 36.8 all-gather.26
  472.3 29.0 all-gather.30
  564.4 62.3 all-reduce.40
  629.2 26.2 all-gather.28
  666.4 64.8 all-reduce.42
  847.6 63.0 all-reduce.44
  925.2 64.5 all-reduce.46
  1108.5 174.2 all-reduce.48
  1285.5 43.3 reduce-scatter.19
  1331.9 27.7 reduce-scatter.17
  1362.4 29.1 reduce-scatter.15
  1394.4 27.8 reduce-scatter.13
  1425.8 36.0 reduce-scatter.11
  1465.5 37.3 reduce-scatter.9
  1505.7 35.7 reduce-scatter.7
  1547.6 119.2 all-reduce.50
  1668.5 29.9 all-gather.42
  1700.1 28.5 all-gather.40
  1730.2 31.1 all-gather.38
  1763.0 30.7 all-gather.36
  1795.3 50.8 all-gather.34
  1847.6 50.5 all-gather.32

commit v2 on v1

--- a/solution.py
+++ b/solution.py
@@ -53,6 +53,50 @@
 
 def one_hot(index, count):
     return (index[:, None] == jnp.arange(count, dtype=jnp.int32)[None, :]).astype(BF)
+
+
+def swapped(shard, axis, by):
+    size = lax.axis_size(axis)
+    return lax.ppermute(shard, axis, [(i, i ^ by) for i in range(size)])
+
+
+def tp_sum(values):
+    values = values + swapped(values, "par", 1)
+    others = [swapped(values, "zz", by) for by in range(1, ZZ)]
+    for other in others:
+        values = values + other
+    return values
+
+
+def gathered_rows(shard, axis):
+    size, own = lax.axis_size(axis), lax.axis_index(axis)
+    rows = shard.shape[0]
+    whole = jnp.zeros((size * rows,) + shard.shape[1:], shard.dtype)
+    others = [swapped(shard, axis, by) for by in range(1, size)]
+    for by, block in enumerate([shard] + others):
+        whole = lax.dynamic_update_slice_in_dim(whole, block, (own ^ by) * rows, 0)
+    return whole
+
+
+def scattered_rows(whole, axis):
+    size, own = lax.axis_size(axis), lax.axis_index(axis)
+    rows = whole.shape[0] // size
+    blocks = [
+        lax.dynamic_slice_in_dim(whole, (own ^ by) * rows, rows, 0) for by in range(size)
+    ]
+    total = blocks[0].astype(F32)
+    for by in range(1, size):
+        total = total + swapped(blocks[by], axis, by).astype(F32)
+    return total
+
+
+def group_tokens(shard):
+    line = [shard] + [swapped(shard, "zz", by) for by in range(1, ZZ)]
+    line = jnp.concatenate(line, 0)
+    both = jnp.concatenate([line, swapped(line, "par", 1)], 0)
+    if lax.axis_size("rep") > 1:
+        both = lax.all_gather(both, "rep", axis=0, tiled=True)
+    return both
 
 
 def inv_rms(values):
@@ -183,7 +227,7 @@
         w["skip_gain"],
     )
     gated = ssd * jax.nn.silu(z)
-    square = lax.psum(jnp.sum(gated * gated, axis=-1), TPA)
+    square = tp_sum(jnp.sum(gated * gated, axis=-1))
     attended, logs = attn_forward(q, k, v, seg, pos)
     inv_g = lax.rsqrt(square / DSSM + EPSILON)[:, None]
     mixer = (gated * inv_g * w["mixer_gain"]).astype(BF)
@@ -203,7 +247,7 @@
     return mid, act, kept
 
 
-def layer_backward(gout, w, kept, meta):
+def layer_backward(gout, w, kept, meta, reduce_rows, pending):
     seg, pos, cosine, sine = meta
     g_down = gout.astype(BF)
     g_act = dot_nt(g_down, w["wr"][XW + HD :])
@@ -221,11 +265,14 @@
     g_low = g_mid.astype(BF)
     g_mixed = dot_nt(g_low, w["wr"][: XW + HD])
     d_wr = dot_tn(kept["mixed"], g_low)
+    early = reduce_rows(d_w2, d_wr, d_down)
+    if pending is None:
+        pending = early()
     g_mix = g_mixed[:, :XW]
     scaled = kept["gated"] * kept["inv_g"]
     gg = g_mix * w["mixer_gain"]
     d_mixer_gain = jnp.sum(g_mix * scaled, axis=0)
-    mean = lax.psum(jnp.sum(gg * scaled, axis=-1), TPA)[:, None] / DSSM
+    mean = tp_sum(jnp.sum(gg * scaled, axis=-1))[:, None] / DSSM
     g_att = g_mixed[:, XW:].astype(BF)
     delta = jnp.sum(g_att.astype(F32) * kept["attended"], axis=-1, keepdims=True)
     gq, gk, gv = attn_backward(
@@ -252,11 +299,12 @@
         ],
         axis=1,
     )
+    g_pr, pending = lax.optimization_barrier((g_pr, pending))
     g_n1 = lax.psum(dot_nt(g_pr, w["w1"]).astype(BF), TPA).astype(F32)
     d_w1 = dot_tn(kept["normed"], g_pr)
     g_h, d_norm_gain = rms_back(g_n1, kept["h"], kept["inv1"], w["norm_gain"])
     small = (d_norm_gain, d_cw, d_cb, d_db, d_dl, d_sk, d_mixer_gain, d_ffn_gain)
-    return g_mid + g_h, (d_w1, d_w2, d_wr, d_down), small
+    return g_mid + g_h, d_w1, early, pending, small
 
 
 def per_device(
@@ -308,13 +356,19 @@
         jnp.sum(jnp.where(pick, starts[None, :] - p_starts[None, :] + piece[:, None] * pieces[None, :], 0), axis=1)
         + local
     )
+    zz = lax.axis_index("zz")
+    slot = jnp.arange(ctx, dtype=jnp.int32)
+    near = (zz ^ (slot % ZZ)) * PAR + (lax.axis_index("par") ^ (slot // ZZ % PAR))
+    order = (slot // TP * TP + near)[:, None] * own_rows
+    order = (order + jnp.arange(own_rows, dtype=jnp.int32)[None, :]).reshape(-1)
+    place_rel = place[order]
     half = HD // 2
     frequency = jnp.exp(-math.log(ROPE_BASE) * jnp.arange(half, dtype=F32) / half)
     angles = pos.astype(F32)[:, None] * frequency[None, :]
     meta = (seg, pos, jnp.cos(angles), jnp.sin(angles))
 
-    to_seq = one_hot(place, rows).T
-    x_all = lax.all_gather(block_in, every, axis=0, tiled=True)
+    to_seq = one_hot(place_rel, rows).T
+    x_all = group_tokens(block_in)
 
     def columns(layer):
         pieces_1 = [
@@ -376,10 +430,10 @@
     w2 = [None, None]
     wr = [None, None]
     for layer in range(LAYERS):
-        w1[layer] = lax.all_gather(w1_own[layer], "fsdp", axis=0, tiled=True)
+        w1[layer] = gathered_rows(w1_own[layer], "fsdp")
         wr[layer] = lax.ppermute(row_pieces(layer), axes, forth)
-        w2[layer] = lax.all_gather(w2_own[layer], "fsdp", axis=0, tiled=True)
-    g_all = lax.all_gather(out_grad, every, axis=0, tiled=True)
+        w2[layer] = gathered_rows(w2_own[layer], "fsdp")
+    g_all = group_tokens(out_grad)
 
     sizes = [
         norm_gain.shape[1],
@@ -443,56 +497,72 @@
 
     gout = dot(to_seq, g_all)
     big = [None, None]
-    small = [None, None]
+
+    def reduce_rows(d_w2, d_wr, d_down):
+        d_rows = jnp.concatenate([d_wr.astype(BF), d_down.astype(BF)], 0)
+        d_rows = scattered_rows(lax.ppermute(d_rows, axes, back), "zz").astype(BF)
+        part = jnp.concatenate(
+            [
+                scattered_rows(d_w2.astype(BF), "fsdp").astype(BF),
+                d_rows.reshape(d_w2.shape[0] // fs, -1),
+            ],
+            1,
+        )
+        return lambda: lax.all_gather(part, TPA, axis=0)
+
+    def reduce_columns(d_w1, small_grads):
+        g_n, g_cw, g_cb, g_db, g_dl, g_sk, g_mg, g_fg = small_grads
+        small = jnp.concatenate(
+            [g_n, g_cw.reshape(-1), g_cb, g_db, g_dl, g_sk, g_mg, g_fg]
+        )
+        others = [swapped(small, "fsdp", by) for by in range(1, fs)]
+        for other in others:
+            small = small + other
+        part = scattered_rows(d_w1.astype(BF), "fsdp").astype(BF)
+        held = jnp.zeros((part.shape[0] * 64,), BF)
+        held = lax.dynamic_update_slice(held, small.astype(BF), (0,)).reshape(-1, 64)
+        part = jnp.concatenate([part[:, :704], held, part[:, 768:]], 1)
+        return lax.all_gather(part, TPA, axis=0)
+
+    pending = None
     for layer in reversed(range(LAYERS)):
-        gout, grads, small_grads = layer_backward(gout, weights[layer], saved[layer], meta)
-        d_w1, d_w2, d_wr, d_down = grads
-        col_2 = lax.psum_scatter(d_w2.astype(BF), "fsdp", scatter_dimension=0, tiled=True)
-        d_rows = jnp.concatenate([d_wr.astype(BF), d_down.astype(BF)], 0)
-        d_rows = lax.ppermute(d_rows, axes, back)
-        d_rows = lax.psum_scatter(d_rows, "zz", scatter_dimension=0, tiled=True)
-        col_1 = lax.psum_scatter(d_w1.astype(BF), "fsdp", scatter_dimension=0, tiled=True)
-        big[layer] = (
-            lax.all_gather(col_1, TPA, axis=0),
-            lax.all_gather(col_2, TPA, axis=0),
-            lax.all_gather(d_rows, TPA, axis=0),
-        )
-        small[layer] = small_grads
+        gout, d_w1, early, pending, small_grads = layer_backward(
+            gout, weights[layer], saved[layer], meta, reduce_rows, pending
+        )
+        if layer == LAYERS - 1:
+            first_part = pending
+            pending = reduce_columns(d_w1, small_grads)
+        else:
+            big[layer + 1] = (first_part, pending)
+            big[layer] = (early(), reduce_columns(d_w1, small_grads))
     in_grad = dot(own_hot, gout.astype(BF)).astype(BF)
 
-    first = (t == 0).astype(F32)
-
-    def spread_conv(vec):
-        zero = jnp.zeros(vec.shape[:-1] + (DSSM,), F32)
-        at = (0,) * (vec.ndim - 1) + (XW * t,)
+    own_sizes = [width, CONV * CW, CW, HEADS, HEADS, HEADS, XW, width]
+    own_at = [sum(own_sizes[:i]) for i in range(len(own_sizes) + 1)]
+    outs_small = [[] for _ in sizes]
+
+    def conv_full(parts):
+        parts = parts.astype(F32)
         return jnp.concatenate(
-            [lax.dynamic_update_slice(zero, vec[..., :XW], at), vec[..., XW:]], -1
-        )
-
-    def spread(vec, count):
-        return lax.dynamic_update_slice(jnp.zeros((count,), F32), vec, (vec.shape[0] * t,))
-
-    flat = []
+            [
+                jnp.moveaxis(parts[..., :XW], 0, -2).reshape(parts.shape[1:-1] + (DSSM,)),
+                jnp.sum(parts[..., XW:], axis=0),
+            ],
+            -1,
+        )
+
     for layer in range(LAYERS):
-        g_n, g_cw, g_cb, g_db, g_dl, g_sk, g_mg, g_fg = small[layer]
-        flat += [
-            g_n * first,
-            spread_conv(g_cw).T.reshape(-1),
-            spread_conv(g_cb),
-            spread(g_db, MH),
-            spread(g_dl, MH),
-            spread(g_sk, MH),
-            spread(g_mg, DSSM),
-            g_fg * first,
+        held = big[layer][1][:, :, 704:768].reshape(TP, -1)
+        parts = [held[:, own_at[i] : own_at[i + 1]] for i in range(len(own_sizes))]
+        full = [
+            parts[0][0].astype(F32),
+            conv_full(parts[1].reshape(TP, CONV, CW)).T.reshape(-1),
+            conv_full(parts[2]),
         ]
-    summed = lax.psum(jnp.concatenate(flat), ("fsdp",) + TPA)
-    full_sizes = [fs * s for s in sizes] * LAYERS
-    outs_small = [[] for _ in sizes]
-    at = 0
-    for i, size in enumerate(full_sizes):
-        own = size // fs
-        outs_small[i % len(sizes)].append(lax.dynamic_slice_in_dim(summed, at + own * f, own, 0))
-        at += size
+        full += [p.astype(F32).reshape(-1) for p in parts[3:7]] + [parts[7][0].astype(F32)]
+        for i, vec in enumerate(full):
+            own = vec.shape[0] // fs
+            outs_small[i].append(lax.dynamic_slice_in_dim(vec, own * f, own, 0))
     (o_norm, o_cw, o_cb, o_db, o_dl, o_sk, o_mg, o_fg) = [jnp.stack(o) for o in outs_small]
     o_cw = o_cw.reshape(LAYERS, -1, CONV)
 
@@ -501,7 +571,8 @@
 
     o_in, o_q, o_k, o_v, o_gate, o_up, o_out, o_attn, o_down = [[] for _ in range(9)]
     for layer in range(LAYERS):
-        c1, c2, rw = big[layer]
+        c2, c1 = big[layer]
+        rw = c2[:, :, 2 * ff :].reshape(TP, -1, width)
         c1 = c1.astype(F32)
         c2 = c2.astype(F32)
         bc = jnp.sum(c1[:, :, 2 * XW : XW + CW], axis=0)
@@ -521,7 +592,7 @@
         o_k.append(joined(jnp.sum(c1[:, :, 896:1024].reshape(KVH, group, -1, HD), axis=1)))
         o_v.append(joined(jnp.sum(c1[:, :, 1024:1152].reshape(KVH, group, -1, HD), axis=1)))
         o_gate.append(joined(c2[:, :, :ff]))
-        o_up.append(joined(c2[:, :, ff:]))
+        o_up.append(joined(c2[:, :, ff : 2 * ff]))
         rw = rw.astype(F32).reshape(ZZ, PAR, -1, width).transpose(1, 0, 2, 3)
         rw = rw.reshape(PAR, -1, width)
         o_out.append(rw[:, :XW].reshape(-1, width))

time: 1960 us -> 1570 us (0.80)
  waiting for transfers between devices: 1180 us -> 454 us
  starting transfers between devices: 25.1 us -> 277 us
  local copies, waits for them, and re-layouts: 258 us -> 373 us
  blocking collectives: 67.8 us -> 8.38 us
  other arithmetic: 210 us -> 258 us
  matrix products: 177 us -> 155 us
    all_gather x12 -> x4, waiting for transfers between devices: 302 us -> 0.01 us  [the longest x2 0.01 us: reduce_rows(): return lambda: lax.all_gather(part, TPA, axis=0)]
    ppermute x2 -> x62, starting transfers between devices: 1.74 us -> 255 us  [the longest x60 243 us: swapped(): return lax.ppermute(shard, axis, [(i, i ^ by) for i in range(size)])]
    reduce_scatter x6 -> x0, waiting for transfers between devices: 215 us -> none  [the longest x2 80.5 us: per_device(): lax.psum_scatter(d_w1.astype(BF), 'fsdp', scatter_dimension=0, tiled=True)]
    psum x2, waiting for transfers between devices: 186 us -> 52.9 us  [layer_backward(): g_n1 = lax.psum(dot_nt(g_pr, w['w1']).astype(BF), TPA).astype(F32)]
    psum x1 -> x0, waiting for transfers between devices: 124 us -> none  [per_device(): summed = lax.psum(jnp.concatenate(flat), ('fsdp',) + TPA)]
    ppermute x2 -> x62, waiting for transfers between devices: 0.01 us -> 113 us  [the longest x60 113 us: swapped(): return lax.ppermute(shard, axis, [(i, i ^ by) for i in range(size)])]
    psum x4 -> x0, blocking collectives: 61 us -> none  [the longest x2 33.4 us: layer_forward(): square = lax.psum(jnp.sum(gated * gated, axis=-1), TPA)]
    reduce_scatter x1, waiting for transfers between devices: 29.2 us -> 0.02 us  [per_device(): lax.psum_scatter(dot(act_rep, weights[-1]['wr'][XW + HD:]).astype(BF), TP...]
  transfers between devices with their start and end apart: 31 -> 76, of which waited for: 26 -> 18; matrix products, arithmetic and copies ran while one was open for 17% -> 41% of each run, Pallas kernels for 0% -> 0%
where the time goes in v2:
time: 1570 us; the launch traced here: 1540 us
  waiting for transfers between devices  454 us (29%)
  local copies, waits for them, and re-layouts  373 us (24%)
  starting transfers between devices  277 us (18%)
  other arithmetic  258 us (16%)
  matrix products  155 us (10%)
  between operations  18.7 us (1%)
    ppermute x60, starting transfers between devices, swapped(): return lax.ppermute(shard, axis, [(i, i ^ by) for i in range(size)])  243 us
    ppermute x60, waiting for transfers between devices, swapped(): return lax.ppermute(shard, axis, [(i, i ^ by) for i in range(size)])  113 us
    psum x2, waiting for transfers between devices, layer_forward(): lax.psum(dot(mixed, w['wr'][:XW + HD]).astype(BF), TPA).astype(F32)  105 us
    psum x2, waiting for transfers between devices, layer_backward(): g_n2 = lax.psum(dot_nt(g_gu, w['w2']).astype(BF), TPA).astype(F32)  98.7 us
    psum x1, waiting for transfers between devices, per_device(): lax.psum(dot(act, weights[layer]['wr'][XW + HD:]).astype(BF), TPA)  83.6 us
    unnamed x682, local copies, waits for them, and re-layouts  66.3 us
    psum x2, waiting for transfers between devices, layer_backward(): g_n1 = lax.psum(dot_nt(g_pr, w['w1']).astype(BF), TPA).astype(F32)  52.9 us
    dot_general x15, matrix products, dot(): return jnp.dot(a, b, preferred_element_type=F32)  52 us
  transfers between devices with their start and end apart: 76, of which 18 were waited for; matrix products, arithmetic and copies ran while one was open for 41% of the time, Pallas kernels for 0%

profile of v2, /device:TPU:0, one launch (start us, length us, event | category | flops | bytes accessed | tf_op | source)
XLA Modules:
  0.0 1543.1 jit_solution(3648930454969774872)
XLA Ops:
  10.6 4.2 slice_bitcast_fusion.6
  26.1 5.5 concatenate.161
  44.3 8.4 all-gather.5
  108.0 9.0 gather_fusion
  118.3 11.7 concatenate.173
  138.7 10.4 collective-permute-start.11
  151.4 22.6 %collective-permute-done.6 = bf16[256,1152]{0,1:T(8,128)(2,1)S(1)} collective-permute-done((bf16[256,1152]{0,1:T(8,128)(2,1)S(1)}, bf16[256,1152]{0,1:T(8,128)(2,1)S(1)}, u32[]{:S(2)}, u32[]{:S(2)}) %collective-permute-start.6) | collective-permute-done | bytes 589856 | tf_op jit(solution)/shard_map/ppermute | solution.py:60
  177.0 5.3 fusion.467
  186.9 4.1 fusion.295
  215.4 5.6 collective-permute-start.10
  224.4 23.7 %collective-permute-start.16 = (bf16[256,1152]{0,1:T(8,128)(2,1)}, bf16[256,1152]{0,1:T(8,128)(2,1)}, u32[]{:S(2)}, u32[]{:S(2)}) collective-permute-start(bf16[256,1152]{0,1:T(8,128)(2,1)} %concatenate.173), channel_id=1, source_target_pairs={{0,16},{8,24},{16,0},{24,8},{1,17},{9,25},{17,1},{25,9},{2,18},{10... | collective-permute-start | bytes 1769480 | tf_op jit(solution)/shard_map/ppermute | solution.py:60
  266.0 6.9 collective-permute-done.13
  279.4 62.9 %all-reduce.38.cloned.1.call-done = bf16[1024,1024]{0,1:T(8,128)(2,1)} async-done(((bf16[1024,1024]{0,1:T(8,128)(2,1)}), bf16[1024,1024]{0,1:T(8,128)(2,1)}) %all-reduce.38.cloned.1.call-update) | async-done | bytes 2097168 | tf_op jit(solution)/shard_map/psum | solution.py:236
  358.0 10.4 collective-permute-start.22
  372.6 28.3 %collective-permute-done.17 = bf16[256,1152]{0,1:T(8,128)(2,1)S(1)} collective-permute-done((bf16[256,1152]{0,1:T(8,128)(2,1)}, bf16[256,1152]{0,1:T(8,128)(2,1)S(1)}, u32[]{:S(2)}, u32[]{:S(2)}) %collective-permute-start.17) | collective-permute-done | bytes 589856 | tf_op jit(solution)/shard_map/ppermute | solution.py:60
  401.0 83.6 %all-reduce.40.cloned.1.call-done = bf16[1024,1024]{0,1:T(8,128)(2,1)} async-done(((bf16[1024,1024]{0,1:T(8,128)(2,1)}), bf16[1024,1024]{0,1:T(8,128)(2,1)}) %all-reduce.40.cloned.1.call-update) | async-done | bytes 2097168 | tf_op jit(solution)/shard_map/psum | solution.py:484
  488.3 5.5 fusion.470
  496.6 23.3 %fusion.473 = f32[8,128,3]{2,0,1:T(8,128)S(1)} fusion(f32[8,128,3]{2,0,1:T(8,128)S(1)} %copy.760), kind=kOutput, calls=%fused_computation.881 | output fusion | flops 390144 | bytes 24576 | tf_op jit(solution)/shard_map/jvp(jit(cumsum))/reduce_window_sum | solution.py:133
  520.2 4.1 fusion.296
  574.0 3.9 convolution_convert_fusion.4
  588.1 6.0 fusion.25
  594.2 5.6 copy.785
  599.7 42.2 %all-reduce.42.cloned.1.call-done = bf16[1024,1024]{0,1:T(8,128)(2,1)} async-done(((bf16[1024,1024]{0,1:T(8,128)(2,1)}), bf16[1024,1024]{0,1:T(8,128)(2,1)}) %all-reduce.42.cloned.1.call-update) | async-done | bytes 2097168 | tf_op jit(solution)/shard_map/psum | solution.py:236
  658.9 4.0 convolution_convert_fusion.11
  669.7 52.4 %all-reduce.44.cloned.1.call-done = bf16[1024,1024]{0,1:T(8,128)(2,1)} async-done(((bf16[1024,1024]{0,1:T(8,128)(2,1)}), bf16[1024,1024]{0,1:T(8,128)(2,1)}) %all-reduce.44.cloned.1.call-update) | async-done | bytes 2097168 | tf_op jit(solution)/shard_map/psum | solution.py:261
  722.2 4.9 fusion.21
  733.5 10.8 collective-permute-start.37
  758.5 4.6 multiply_convert_fusion.1
  764.3 50.0 %collective-permute-start.38 = (bf16[144,1024]{1,0:T(8,128)(2,1)S(1)}, bf16[144,1024]{1,0:T(8,128)(2,1)S(1)}, u32[]{:S(2)}, u32[]{:S(2)}) collective-permute-start(bf16[144,1024]{1,0:T(8,128)(2,1)S(1)} %get-tuple-element.203), channel_id=1, source_target_pairs={{0,2},{2,0},{4,6},{6,4},{1,3},{3,1},{5,7},{7,5},{8,10},{10,8},{12,... | collective-permute-start | bytes 884744 | tf_op jit(solution)/shard_map/ppermute | solution.py:60
  821.8 13.6 collective-permute-done.39
  845.9 6.8 collective-permute-start.31
  863.7 4.5 multiply_reduce_fusion.19
  878.0 3.8 fusion.162
  902.1 4.3 fusion.441
  909.8 4.8 concatenate.185
  914.6 6.8 convolution_convert_fusion.3
  922.0 5.1 convolution_convert_fusion.1
  932.8 52.9 %all-reduce.46.cloned.1.call-done = bf16[1024,1024]{0,1:T(8,128)(2,1)} async-done(((bf16[1024,1024]{0,1:T(8,128)(2,1)}), bf16[1024,1024]{0,1:T(8,128)(2,1)}) %all-reduce.46.cloned.1.call-update) | async-done | bytes 2097168 | tf_op jit(solution)/shard_map/psum | solution.py:303
  985.7 4.9 fusion.22
  1019.7 46.3 %all-reduce.48.cloned.1.call-done = bf16[1024,1024]{0,1:T(8,128)(2,1)} async-done(((bf16[1024,1024]{0,1:T(8,128)(2,1)}), bf16[1024,1024]{0,1:T(8,128)(2,1)}) %all-reduce.48.cloned.1.call-update) | async-done | bytes 2097168 | tf_op jit(solution)/shard_map/psum | solution.py:261
  1066.0 4.9 fusion.23
  1099.1 4.2 multiply_reduce_fusion.17
  1131.2 4.3 fusion.440
  1139.1 4.7 concatenate.189
  1143.8 6.6 convolution_convert_fusion.2
  1151.5 4.6 convolution_convert_fusion.8
  1172.0 86.8 %collective-permute-start.61 = (bf16[144,1024]{1,0:T(8,128)(2,1)}, bf16[144,1024]{1,0:T(8,128)(2,1)}, u32[]{:S(2)}, u32[]{:S(2)}) collective-permute-start(bf16[144,1024]{1,0:T(8,128)(2,1)} %get-tuple-element.200), channel_id=1, source_target_pairs={{0,2},{2,0},{4,6},{6,4},{1,3},{3,1},{5,7},{7,5},{8,10},{10,8},{12,... | collective-permute-start | bytes 884744 | tf_op jit(solution)/shard_map/ppermute | solution.py:60
  1264.0 17.8 %collective-permute-done.61 = bf16[144,1024]{1,0:T(8,128)(2,1)} collective-permute-done((bf16[144,1024]{1,0:T(8,128)(2,1)}, bf16[144,1024]{1,0:T(8,128)(2,1)}, u32[]{:S(2)}, u32[]{:S(2)}) %collective-permute-start.61) | collective-permute-done | bytes 294944 | tf_op jit(solution)/shard_map/ppermute | solution.py:60
  1281.8 5.7 collective-permute-done.62
  1292.9 5.1 convolution_convert_fusion
  1311.0 4.8 fusion.24
  1320.8 8.9 collective-permute-done.52
  1334.5 4.8 fusion.249
  1341.0 6.9 convert_element_type.729
  1350.6 6.4 reshape.1128
  1364.1 4.0 slice_bitcast_fusion
  1376.5 6.8 copy.867
  1383.3 6.8 convert_element_type.704
  1413.3 6.8 convert_element_type.728
  1422.8 6.4 reshape.1126
  1436.4 4.0 slice_bitcast_fusion.1
  1445.6 4.1 copy.883
  1471.0 6.6 copy.866
  1477.7 6.7 convert_element_type.703
  (1326 shorter events, 621.9 us)
Async XLA Ops:
  7.2 335.0 %all-reduce.38.cloned.1.call-start = ((), (), s32[]{:S(2)}) async-start(), calls=%async_computation.1 | async-start | bytes 4194304 | tf_op jit(solution)/shard_map/psum | solution.py:236
  31.6 107.2 %collective-permute-start.4 = (bf16[256,1152]{0,1:T(8,128)(2,1)S(1)}, bf16[256,1152]{0,1:T(8,128)(2,1)}, u32[]{:S(2)}, u32[]{:S(2)}) collective-permute-start(bf16[256,1152]{0,1:T(8,128)(2,1)S(1)} %concatenate.161), channel_id=1, source_target_pairs={{0,8},{8,0},{16,24},{24,16},{1,9},{9,1},{17,25},{25,17},{2,10},{10... | collective-permute-start | bytes 1769480 | tf_op jit(solution)/shard_map/ppermute | solution.py:60
  34.5 115.8 %collective-permute-start.5 = (bf16[256,1152]{0,1:T(8,128)(2,1)S(1)}, bf16[256,1152]{0,1:T(8,128)(2,1)}, u32[]{:S(2)}, u32[]{:S(2)}) collective-permute-start(bf16[256,1152]{0,1:T(8,128)(2,1)S(1)} %concatenate.161), channel_id=1, source_target_pairs={{0,16},{8,24},{16,0},{24,8},{1,17},{9,25},{17,1},{25,9},{2,18},{10... | collective-permute-start | bytes 1769480 | tf_op jit(solution)/shard_map/ppermute | solution.py:60
  36.0 96.4 %collective-permute-start = (bf16[128,1024]{1,0:T(8,128)(2,1)}, bf16[128,1024]{1,0:T(8,128)(2,1)}, u32[]{:S(2)}, u32[]{:S(2)}) collective-permute-start(bf16[128,1024]{1,0:T(8,128)(2,1)} %param.21), channel_id=1, source_target_pairs={{0,2},{2,0},{4,6},{6,4},{1,3},{3,1},{5,7},{7,5},{8,10},{10,8},{12,... | collective-permute-start | bytes 786440 | tf_op jit(solution)/shard_map/ppermute | solution.py:60
  37.6 96.4 %collective-permute-start.1 = (bf16[128,1024]{1,0:T(8,128)(2,1)}, bf16[128,1024]{1,0:T(8,128)(2,1)}, u32[]{:S(2)}, u32[]{:S(2)}) collective-permute-start(bf16[128,1024]{1,0:T(8,128)(2,1)} %param.21), channel_id=1, source_target_pairs={{0,4},{2,6},{4,0},{6,2},{1,5},{3,7},{5,1},{7,3},{8,12},{10,14},{12... | collective-permute-start | bytes 786440 | tf_op jit(solution)/shard_map/ppermute | solution.py:60
  40.2 94.3 %collective-permute-start.2 = (bf16[128,1024]{1,0:T(8,128)(2,1)}, bf16[128,1024]{1,0:T(8,128)(2,1)}, u32[]{:S(2)}, u32[]{:S(2)}) collective-permute-start(bf16[128,1024]{1,0:T(8,128)(2,1)} %param.21), channel_id=1, source_target_pairs={{0,6},{2,4},{4,2},{6,0},{1,7},{3,5},{5,3},{7,1},{8,14},{10,12},{12... | collective-permute-start | bytes 786440 | tf_op jit(solution)/shard_map/ppermute | solution.py:60
  132.4 41.6 %collective-permute-start.6 = (bf16[256,1152]{0,1:T(8,128)(2,1)S(1)}, bf16[256,1152]{0,1:T(8,128)(2,1)S(1)}, u32[]{:S(2)}, u32[]{:S(2)}) collective-permute-start(bf16[256,1152]{0,1:T(8,128)(2,1)S(1)} %concatenate.161), channel_id=1, source_target_pairs={{0,24},{8,16},{16,8},{24,0},{1,25},{9,17},{17,9},{25,1},{2,26},{10... | collective-permute-start | bytes 1769480 | tf_op jit(solution)/shard_map/ppermute | solution.py:60
  134.0 236.3 %collective-permute-start.15 = (bf16[256,1152]{0,1:T(8,128)(2,1)}, bf16[256,1152]{0,1:T(8,128)(2,1)}, u32[]{:S(2)}, u32[]{:S(2)}) collective-permute-start(bf16[256,1152]{0,1:T(8,128)(2,1)} %concatenate.173), channel_id=1, source_target_pairs={{0,8},{8,0},{16,24},{24,16},{1,9},{9,1},{17,25},{25,17},{2,10},{10... | collective-permute-start | bytes 1769480 | tf_op jit(solution)/shard_map/ppermute | solution.py:60
  135.7 38.4 %collective-permute-start.3 = (bf16[512,1024]{1,0:T(8,128)(2,1)S(1)}, bf16[512,1024]{1,0:T(8,128)(2,1)S(1)}, u32[]{:S(2)}, u32[]{:S(2)}) collective-permute-start(bf16[512,1024]{1,0:T(8,128)(2,1)S(1)} %pad_maximum_fusion.11), channel_id=1, source_target_pairs={{0,1},{1,0},{2,3},{3,2},{4,5},{5,4},{6,7},{7,6},{8,9},{9,8},{10,11... | collective-permute-start | bytes 3145736 | tf_op jit(solution)/shard_map/ppermute | solution.py:60
  138.7 111.8 %collective-permute-start.11 = (bf16[576,1024]{1,0:T(8,128)(2,1)}, bf16[576,1024]{1,0:T(8,128)(2,1)}, u32[]{:S(2)}, u32[]{:S(2)}) collective-permute-start(bf16[576,1024]{1,0:T(8,128)(2,1)} %pad_maximum_fusion.7), channel_id=1, source_target_pairs={{0,0},{1,1},{2,8},{3,9},{4,16},{5,17},{6,24},{7,25},{8,2},{9,3},{1... | collective-permute-start | bytes 3538952 | tf_op jit(solution)/shard_map/ppermute | solution.py:434
  221.0 27.1 %collective-permute-start.8 = (f32[1024]{0:T(1024)S(1)}, f32[1024]{0:T(1024)S(1)}, u32[]{:S(2)}, u32[]{:S(2)}) collective-permute-start(f32[1024]{0:T(1024)S(1)} %add.733), channel_id=1, source_target_pairs={{0,2},{2,0},{4,6},{6,4},{1,3},{3,1},{5,7},{7,5},{8,10},{10,8},{12,... | collective-permute-start | bytes 12296 | tf_op jit(solution)/shard_map/ppermute | solution.py:60
  221.0 27.3 %collective-permute-start.9 = (f32[1024]{0:T(1024)S(1)}, f32[1024]{0:T(1024)S(1)}, u32[]{:S(2)}, u32[]{:S(2)}) collective-permute-start(f32[1024]{0:T(1024)S(1)} %add.733), channel_id=1, source_target_pairs={{0,4},{2,6},{4,0},{6,2},{1,5},{3,7},{5,1},{7,3},{8,12},{10,14},{12... | collective-permute-start | bytes 12296 | tf_op jit(solution)/shard_map/ppermute | solution.py:60
  224.4 147.0 %collective-permute-start.16 = (bf16[256,1152]{0,1:T(8,128)(2,1)}, bf16[256,1152]{0,1:T(8,128)(2,1)}, u32[]{:S(2)}, u32[]{:S(2)}) collective-permute-start(bf16[256,1152]{0,1:T(8,128)(2,1)} %concatenate.173), channel_id=1, source_target_pairs={{0,16},{8,24},{16,0},{24,8},{1,17},{9,25},{17,1},{25,9},{2,18},{10... | collective-permute-start | bytes 1769480 | tf_op jit(solution)/shard_map/ppermute | solution.py:60
  248.1 15.1 collective-permute-start.12
  248.3 24.5 %collective-permute-start.13 = (bf16[256,512]{1,0:T(8,128)(2,1)}, bf16[256,512]{1,0:T(8,128)(2,1)S(1)}, u32[]{:S(2)}, u32[]{:S(2)}) collective-permute-start(bf16[256,512]{1,0:T(8,128)(2,1)} %get-tuple-element.248), channel_id=1, source_target_pairs={{0,16},{8,24},{16,0},{24,8},{1,17},{9,25},{17,1},{25,9},{2,18},{10... | collective-permute-start | bytes 786440 | tf_op jit(solution)/shard_map/ppermute | solution.py:60
  250.5 24.6 %collective-permute-start.14 = (bf16[256,512]{1,0:T(8,128)(2,1)}, bf16[256,512]{1,0:T(8,128)(2,1)}, u32[]{:S(2)}, u32[]{:S(2)}) collective-permute-start(bf16[256,512]{1,0:T(8,128)(2,1)} %get-tuple-element.248), channel_id=1, source_target_pairs={{0,24},{8,16},{16,8},{24,0},{1,25},{9,17},{17,9},{25,1},{2,26},{10... | collective-permute-start | bytes 786440 | tf_op jit(solution)/shard_map/ppermute | solution.py:60
  255.8 228.8 %all-reduce.40.cloned.1.call-start = ((), (), s32[]{:S(2)}) async-start(), calls=%async_computation.2 | async-start | bytes 4194304 | tf_op jit(solution)/shard_map/psum | solution.py:484
  263.2 91.6 %collective-permute-start.26 = (bf16[128,1024]{1,0:T(8,128)(2,1)S(1)}, bf16[128,1024]{1,0:T(8,128)(2,1)S(1)}, u32[]{:S(2)}, u32[]{:S(2)}) collective-permute-start(bf16[128,1024]{1,0:T(8,128)(2,1)S(1)} %copy-done.136), channel_id=1, source_target_pairs={{0,2},{2,0},{4,6},{6,4},{1,3},{3,1},{5,7},{7,5},{8,10},{10,8},{12,... | collective-permute-start | bytes 786440 | tf_op jit(solution)/shard_map/ppermute | solution.py:60
  272.8 85.2 %collective-permute-start.27 = (bf16[128,1024]{1,0:T(8,128)(2,1)S(1)}, bf16[128,1024]{1,0:T(8,128)(2,1)S(1)}, u32[]{:S(2)}, u32[]{:S(2)}) collective-permute-start(bf16[128,1024]{1,0:T(8,128)(2,1)S(1)} %copy-done.136), channel_id=1, source_target_pairs={{0,4},{2,6},{4,0},{6,2},{1,5},{3,7},{5,1},{7,3},{8,12},{10,14},{12... | collective-permute-start | bytes 786440 | tf_op jit(solution)/shard_map/ppermute | solution.py:60
  275.1 93.2 %collective-permute-start.28 = (bf16[128,1024]{1,0:T(8,128)(2,1)S(1)}, bf16[128,1024]{1,0:T(8,128)(2,1)S(1)}, u32[]{:S(2)}, u32[]{:S(2)}) collective-permute-start(bf16[128,1024]{1,0:T(8,128)(2,1)S(1)} %copy-done.136), channel_id=1, source_target_pairs={{0,6},{2,4},{4,2},{6,0},{1,7},{3,5},{5,3},{7,1},{8,14},{10,12},{12... | collective-permute-start | bytes 786440 | tf_op jit(solution)/shard_map/ppermute | solution.py:60
  354.8 287.1 %all-reduce.42.cloned.1.call-start = ((), (), s32[]{:S(2)}) async-start(), calls=%async_computation.3 | async-start | bytes 4194304 | tf_op jit(solution)/shard_map/psum | solution.py:236
  354.8 46.1 %collective-permute-start.17 = (bf16[256,1152]{0,1:T(8,128)(2,1)}, bf16[256,1152]{0,1:T(8,128)(2,1)S(1)}, u32[]{:S(2)}, u32[]{:S(2)}) collective-permute-start(bf16[256,1152]{0,1:T(8,128)(2,1)} %concatenate.173), channel_id=1, source_target_pairs={{0,24},{8,16},{16,8},{24,0},{1,25},{9,17},{17,9},{25,1},{2,26},{10... | collective-permute-start | bytes 1769480 | tf_op jit(solution)/shard_map/ppermute | solution.py:60
  358.0 215.2 %collective-permute-start.22 = (bf16[576,1024]{1,0:T(8,128)(2,1)}, bf16[576,1024]{1,0:T(8,128)(2,1)}, u32[]{:S(2)}, u32[]{:S(2)}) collective-permute-start(bf16[576,1024]{1,0:T(8,128)(2,1)} %pad_maximum_fusion.8), channel_id=1, source_target_pairs={{0,0},{1,1},{2,8},{3,9},{4,16},{5,17},{6,24},{7,25},{8,2},{9,3},{1... | collective-permute-start | bytes 3538952 | tf_op jit(solution)/shard_map/ppermute | solution.py:434
  368.4 211.3 %collective-permute-start.23 = (bf16[256,512]{1,0:T(8,128)(2,1)}, bf16[256,512]{1,0:T(8,128)(2,1)}, u32[]{:S(2)}, u32[]{:S(2)}) collective-permute-start(bf16[256,512]{1,0:T(8,128)(2,1)} %get-tuple-element.242), channel_id=1, source_target_pairs={{0,8},{8,0},{16,24},{24,16},{1,9},{9,1},{17,25},{25,17},{2,10},{10... | collective-permute-start | bytes 786440 | tf_op jit(solution)/shard_map/ppermute | solution.py:60
  542.9 16.2 %collective-permute-start.18 = (f32[1024]{0:T(1024)}, f32[1024]{0:T(1024)}, u32[]{:S(2)}, u32[]{:S(2)}) collective-permute-start(f32[1024]{0:T(1024)} %get-tuple-element.135), channel_id=1, source_target_pairs={{0,1},{1,0},{2,3},{3,2},{4,5},{5,4},{6,7},{7,6},{8,9},{9,8},{10,11... | collective-permute-start | bytes 12296 | tf_op jit(solution)/shard_map/ppermute | solution.py:60
  568.7 13.8 collective-permute-start.24
  570.2 14.0 collective-permute-start.25
  571.6 14.2 collective-permute-start.29
  577.9 144.2 %all-reduce.44.cloned.1.call-start = ((), (), s32[]{:S(2)}) async-start(), calls=%async_computation.5 | async-start | bytes 4194304 | tf_op jit(solution)/shard_map/psum | solution.py:261
  657.5 257.1 %all-gather.11.cloned.1.call-start = ((), (), s32[]{:S(2)}) async-start(), calls=%async_computation.9 | async-start | bytes 5308416 | tf_op jit(solution)/shard_map/all_gather | solution.py:511
  664.7 79.6 %collective-permute-start.34 = (bf16[256,512]{0,1:T(8,128)(2,1)}, bf16[256,512]{0,1:T(8,128)(2,1)}, u32[]{:S(2)}, u32[]{:S(2)}) collective-permute-start(bf16[256,512]{0,1:T(8,128)(2,1)} %get-tuple-element.209), channel_id=1, source_target_pairs={{0,8},{8,0},{16,24},{24,16},{1,9},{9,1},{17,25},{25,17},{2,10},{10... | collective-permute-start | bytes 786440 | tf_op jit(solution)/shard_map/ppermute | solution.py:60
  666.2 78.2 %collective-permute-start.35 = (bf16[256,512]{0,1:T(8,128)(2,1)}, bf16[256,512]{0,1:T(8,128)(2,1)}, u32[]{:S(2)}, u32[]{:S(2)}) collective-permute-start(bf16[256,512]{0,1:T(8,128)(2,1)} %get-tuple-element.211), channel_id=1, source_target_pairs={{0,16},{8,24},{16,0},{24,8},{1,17},{9,25},{17,1},{25,9},{2,18},{10... | collective-permute-start | bytes 786440 | tf_op jit(solution)/shard_map/ppermute | solution.py:60
  667.7 76.7 %collective-permute-start.36 = (bf16[256,512]{0,1:T(8,128)(2,1)}, bf16[256,512]{0,1:T(8,128)(2,1)}, u32[]{:S(2)}, u32[]{:S(2)}) collective-permute-start(bf16[256,512]{0,1:T(8,128)(2,1)} %get-tuple-element.210), channel_id=1, source_target_pairs={{0,24},{8,16},{16,8},{24,0},{1,25},{9,17},{17,9},{25,1},{2,26},{10... | collective-permute-start | bytes 786440 | tf_op jit(solution)/shard_map/ppermute | solution.py:60
  733.5 29.5 %collective-permute-start.37 = (bf16[576,1024]{1,0:T(8,128)(2,1)}, bf16[576,1024]{1,0:T(8,128)(2,1)}, u32[]{:S(2)}, u32[]{:S(2)}) collective-permute-start(bf16[576,1024]{1,0:T(8,128)(2,1)} %pad_maximum_fusion.9), channel_id=1, source_target_pairs={{0,0},{1,1},{8,2},{9,3},{16,4},{17,5},{24,6},{25,7},{2,8},{3,9},{1... | collective-permute-start | bytes 3538952 | tf_op jit(solution)/shard_map/ppermute | solution.py:503
  758.3 86.3 %collective-permute-start.30 = (f32[1024]{0:T(1024)}, f32[1024]{0:T(1024)}, u32[]{:S(2)}, u32[]{:S(2)}) collective-permute-start(f32[1024]{0:T(1024)} %get-tuple-element.98), channel_id=1, source_target_pairs={{0,1},{1,0},{2,3},{3,2},{4,5},{5,4},{6,7},{7,6},{8,9},{9,8},{10,11... | collective-permute-start | bytes 12296 | tf_op jit(solution)/shard_map/ppermute | solution.py:60
  764.3 57.5 %collective-permute-start.38 = (bf16[144,1024]{1,0:T(8,128)(2,1)S(1)}, bf16[144,1024]{1,0:T(8,128)(2,1)S(1)}, u32[]{:S(2)}, u32[]{:S(2)}) collective-permute-start(bf16[144,1024]{1,0:T(8,128)(2,1)S(1)} %get-tuple-element.203), channel_id=1, source_target_pairs={{0,2},{2,0},{4,6},{6,4},{1,3},{3,1},{5,7},{7,5},{8,10},{10,8},{12,... | collective-permute-start | bytes 884744 | tf_op jit(solution)/shard_map/ppermute | solution.py:60
  814.3 21.1 %collective-permute-start.39 = (bf16[144,1024]{1,0:T(8,128)(2,1)S(1)}, bf16[144,1024]{1,0:T(8,128)(2,1)S(1)}, u32[]{:S(2)}, u32[]{:S(2)}) collective-permute-start(bf16[144,1024]{1,0:T(8,128)(2,1)S(1)} %get-tuple-element.205), channel_id=1, source_target_pairs={{0,4},{2,6},{4,0},{6,2},{1,5},{3,7},{5,1},{7,3},{8,12},{10,14},{12... | collective-permute-start | bytes 884744 | tf_op jit(solution)/shard_map/ppermute | solution.py:60
  814.3 21.1 %collective-permute-start.40 = (bf16[144,1024]{1,0:T(8,128)(2,1)S(1)}, bf16[144,1024]{1,0:T(8,128)(2,1)S(1)}, u32[]{:S(2)}, u32[]{:S(2)}) collective-permute-start(bf16[144,1024]{1,0:T(8,128)(2,1)S(1)} %get-tuple-element.204), channel_id=1, source_target_pairs={{0,6},{2,4},{4,2},{6,0},{1,7},{3,5},{5,3},{7,1},{8,14},{10,12},{12... | collective-permute-start | bytes 884744 | tf_op jit(solution)/shard_map/ppermute | solution.py:60
  841.3 144.4 %all-reduce.46.cloned.1.call-start = ((), (), s32[]{:S(2)}) async-start(), calls=%async_computation.6 | async-start | bytes 4194304 | tf_op jit(solution)/shard_map/psum | solution.py:303
  845.9 17.1 %collective-permute-start.31 = (f32[1024]{0:T(1024)}, f32[1024]{0:T(1024)}, u32[]{:S(2)}, u32[]{:S(2)}) collective-permute-start(f32[1024]{0:T(1024)} %add.775), channel_id=1, source_target_pairs={{0,2},{2,0},{4,6},{6,4},{1,3},{3,1},{5,7},{7,5},{8,10},{10,8},{12,... | collective-permute-start | bytes 12296 | tf_op jit(solution)/shard_map/ppermute | solution.py:60
  852.7 10.3 collective-permute-start.32
  852.7 10.3 collective-permute-start.33
  921.4 144.6 %all-reduce.48.cloned.1.call-start = ((), (), s32[]{:S(2)}) async-start(), calls=%async_computation.7 | async-start | bytes 4194304 | tf_op jit(solution)/shard_map/psum | solution.py:261
  928.7 84.7 %collective-permute-start.45 = (bf16[256,1152]{1,0:T(8,128)(2,1)S(1)}, bf16[256,1152]{1,0:T(8,128)(2,1)S(1)}, u32[]{:S(2)}, u32[]{:S(2)}) collective-permute-start(bf16[256,1152]{1,0:T(8,128)(2,1)S(1)} %get-tuple-element.180), channel_id=1, source_target_pairs={{0,8},{8,0},{16,24},{24,16},{1,9},{9,1},{17,25},{25,17},{2,10},{10... | collective-permute-start | bytes 1769480 | tf_op jit(solution)/shard_map/ppermute | solution.py:60
  931.3 82.7 %collective-permute-start.46 = (bf16[256,1152]{1,0:T(8,128)(2,1)S(1)}, bf16[256,1152]{1,0:T(8,128)(2,1)S(1)}, u32[]{:S(2)}, u32[]{:S(2)}) collective-permute-start(bf16[256,1152]{1,0:T(8,128)(2,1)S(1)} %get-tuple-element.182), channel_id=1, source_target_pairs={{0,16},{8,24},{16,0},{24,8},{1,17},{9,25},{17,1},{25,9},{2,18},{10... | collective-permute-start | bytes 1769480 | tf_op jit(solution)/shard_map/ppermute | solution.py:60
  931.3 82.7 %collective-permute-start.47 = (bf16[256,1152]{1,0:T(8,128)(2,1)S(1)}, bf16[256,1152]{1,0:T(8,128)(2,1)S(1)}, u32[]{:S(2)}, u32[]{:S(2)}) collective-permute-start(bf16[256,1152]{1,0:T(8,128)(2,1)S(1)} %get-tuple-element.181), channel_id=1, source_target_pairs={{0,24},{8,16},{16,8},{24,0},{1,25},{9,17},{17,9},{25,1},{2,26},{10... | collective-permute-start | bytes 1769480 | tf_op jit(solution)/shard_map/ppermute | solution.py:60
  1001.2 142.6 %all-gather.13.cloned.1.call-start = ((), (), s32[]{:S(2)}) async-start(), calls=%async_computation.10 | async-start | bytes 5308416 | tf_op jit(solution)/shard_map/all_gather | solution.py:525
  1019.5 291.6 %all-reduce.50.cloned.1.call-start = ((), (), s32[]{:S(2)}) async-start(), calls=%async_computation.8 | async-start | bytes 4194304 | tf_op jit(solution)/shard_map/psum | solution.py:303
  1087.4 10.9 collective-permute-start.42
  1150.5 188.8 %reduce-scatter.2.cloned.1.call-start = ((), (), s32[]{:S(2)}) async-start(), calls=%async_computation.4 | async-start | bytes 2359296 | tf_op jit(solution)/shard_map/reduce_scatter | solution.py:490
  1156.1 257.2 %all-gather.17.cloned.1.call-start = ((), (), s32[]{:S(2)}) async-start(), calls=%async_computation.12 | async-start | bytes 5308416 | tf_op jit(solution)/shard_map/all_gather | solution.py:511
  1164.9 93.9 %collective-permute-start.57 = (bf16[256,512]{0,1:T(8,128)(2,1)S(1)}, bf16[256,512]{0,1:T(8,128)(2,1)S(1)}, u32[]{:S(2)}, u32[]{:S(2)}) collective-permute-start(bf16[256,512]{0,1:T(8,128)(2,1)S(1)} %get-tuple-element.206), channel_id=1, source_target_pairs={{0,8},{8,0},{16,24},{24,16},{1,9},{9,1},{17,25},{25,17},{2,10},{10... | collective-permute-start | bytes 786440 | tf_op jit(solution)/shard_map/ppermute | solution.py:60
  1167.7 93.4 %collective-permute-start.58 = (bf16[256,512]{0,1:T(8,128)(2,1)S(1)}, bf16[256,512]{0,1:T(8,128)(2,1)S(1)}, u32[]{:S(2)}, u32[]{:S(2)}) collective-permute-start(bf16[256,512]{0,1:T(8,128)(2,1)S(1)} %get-tuple-element.208), channel_id=1, source_target_pairs={{0,16},{8,24},{16,0},{24,8},{1,17},{9,25},{17,1},{25,9},{2,18},{10... | collective-permute-start | bytes 786440 | tf_op jit(solution)/shard_map/ppermute | solution.py:60
  1171.0 90.2 %collective-permute-start.59 = (bf16[256,512]{0,1:T(8,128)(2,1)S(1)}, bf16[256,512]{0,1:T(8,128)(2,1)S(1)}, u32[]{:S(2)}, u32[]{:S(2)}) collective-permute-start(bf16[256,512]{0,1:T(8,128)(2,1)S(1)} %get-tuple-element.207), channel_id=1, source_target_pairs={{0,24},{8,16},{16,8},{24,0},{1,25},{9,17},{17,9},{25,1},{2,26},{10... | collective-permute-start | bytes 786440 | tf_op jit(solution)/shard_map/ppermute | solution.py:60
  1172.0 109.8 %collective-permute-start.61 = (bf16[144,1024]{1,0:T(8,128)(2,1)}, bf16[144,1024]{1,0:T(8,128)(2,1)}, u32[]{:S(2)}, u32[]{:S(2)}) collective-permute-start(bf16[144,1024]{1,0:T(8,128)(2,1)} %get-tuple-element.200), channel_id=1, source_target_pairs={{0,2},{2,0},{4,6},{6,4},{1,3},{3,1},{5,7},{7,5},{8,10},{10,8},{12,... | collective-permute-start | bytes 884744 | tf_op jit(solution)/shard_map/ppermute | solution.py:60
  1258.8 28.7 %collective-permute-start.62 = (bf16[144,1024]{1,0:T(8,128)(2,1)}, bf16[144,1024]{1,0:T(8,128)(2,1)}, u32[]{:S(2)}, u32[]{:S(2)}) collective-permute-start(bf16[144,1024]{1,0:T(8,128)(2,1)} %get-tuple-element.202), channel_id=1, source_target_pairs={{0,4},{2,6},{4,0},{6,2},{1,5},{3,7},{5,1},{7,3},{8,12},{10,14},{12... | collective-permute-start | bytes 884744 | tf_op jit(solution)/shard_map/ppermute | solution.py:60
  1258.8 28.7 %collective-permute-start.63 = (bf16[144,1024]{1,0:T(8,128)(2,1)}, bf16[144,1024]{1,0:T(8,128)(2,1)}, u32[]{:S(2)}, u32[]{:S(2)}) collective-permute-start(bf16[144,1024]{1,0:T(8,128)(2,1)} %get-tuple-element.201), channel_id=1, source_target_pairs={{0,6},{2,4},{4,2},{6,0},{1,7},{3,5},{5,3},{7,1},{8,14},{10,12},{12... | collective-permute-start | bytes 884744 | tf_op jit(solution)/shard_map/ppermute | solution.py:60
  1292.8 176.2 %all-gather.15.cloned.1.call-start = ((), (), s32[]{:S(2)}) async-start(), calls=%async_computation.11 | async-start | bytes 5308416 | tf_op jit(solution)/shard_map/all_gather | solution.py:525
  1299.6 19.8 %collective-permute-start.51 = (bf16[256,1152]{1,0:T(8,128)(2,1)S(1)}, bf16[256,1152]{1,0:T(8,128)(2,1)S(1)}, u32[]{:S(2)}, u32[]{:S(2)}) collective-permute-start(bf16[256,1152]{1,0:T(8,128)(2,1)S(1)} %get-tuple-element.177), channel_id=1, source_target_pairs={{0,8},{8,0},{16,24},{24,16},{1,9},{9,1},{17,25},{25,17},{2,10},{10... | collective-permute-start | bytes 1769480 | tf_op jit(solution)/shard_map/ppermute | solution.py:60
  1302.2 27.5 %collective-permute-start.52 = (bf16[256,1152]{1,0:T(8,128)(2,1)S(1)}, bf16[256,1152]{1,0:T(8,128)(2,1)S(1)}, u32[]{:S(2)}, u32[]{:S(2)}) collective-permute-start(bf16[256,1152]{1,0:T(8,128)(2,1)S(1)} %get-tuple-element.179), channel_id=1, source_target_pairs={{0,16},{8,24},{16,0},{24,8},{1,17},{9,25},{17,1},{25,9},{2,18},{10... | collective-permute-start | bytes 1769480 | tf_op jit(solution)/shard_map/ppermute | solution.py:60
  1305.1 26.3 %collective-permute-start.53 = (bf16[256,1152]{1,0:T(8,128)(2,1)S(1)}, bf16[256,1152]{1,0:T(8,128)(2,1)S(1)}, u32[]{:S(2)}, u32[]{:S(2)}) collective-permute-start(bf16[256,1152]{1,0:T(8,128)(2,1)S(1)} %get-tuple-element.178), channel_id=1, source_target_pairs={{0,24},{8,16},{16,8},{24,0},{1,25},{9,17},{17,9},{25,1},{2,26},{10... | collective-permute-start | bytes 1769480 | tf_op jit(solution)/shard_map/ppermute | solution.py:60
  1317.3 15.5 %collective-permute-start.54 = (f32[4489]{0:T(1024)}, f32[4489]{0:T(1024)S(1)}, u32[]{:S(2)}, u32[]{:S(2)}) collective-permute-start(f32[4489]{0:T(1024)} %concatenate.192), channel_id=1, source_target_pairs={{0,8},{8,0},{16,24},{24,16},{1,9},{9,1},{17,25},{25,17},{2,10},{10... | collective-permute-start | bytes 53876 | tf_op jit(solution)/shard_map/ppermute | solution.py:60
  1317.9 15.0 collective-permute-start.55
  1319.4 13.5 collective-permute-start.56
  (343 other events, 3561.5 us)
Sparse Core Ops, SparseCore 0:
  255.9 86.3 all-reduce.37
  354.9 129.6 all-reduce.39
  578.0 63.8 all-reduce.41
  657.6 64.4 all-reduce.43
  841.5 56.2 all-gather.10
  921.5 64.1 all-reduce.45
  1001.4 64.5 all-reduce.47
  1068.2 51.6 all-gather.12
  1150.6 145.7 all-reduce.49
  1299.1 36.1 reduce-scatter.1
  1337.5 50.3 all-gather.16
  1389.4 50.5 all-gather.14

commit v3 on v2

v3 whole, which is shorter than its diff:
```python
import math

import jax
import jax.numpy as jnp
from jax import lax
from jax.experimental import pallas as pl
from jax.experimental.pallas import tpu as pltpu
from jax.sharding import Mesh, PartitionSpec as P

QH = 8
KVH = 2
HD = 128
MH = 24
MP = 64
NS = 128
CONV = 4
LAYERS = 2
SEQS = 3
DSSM = 1536
CONVCH = 1792
TP = 8
ZZ = 4
PAR = 2
HEADS = MH // TP
XW = HEADS * MP
CW = XW + 2 * NS
CHUNK = 256
ATTN = 256
DTL = 64

EPSILON = 1e-05
ROPE_BASE = 100000000000.0
MASKED = -1e30
BF = jnp.bfloat16
F32 = jnp.float32
TPA = ("zz", "par")


def dot(a, b):
    return jnp.dot(a, b, preferred_element_type=F32)


def dot_nt(a, b):
    return lax.dot_general(a, b, (((1,), (1,)), ((), ())), preferred_element_type=F32)


def dot_tn(a, b):
    return lax.dot_general(a, b, (((0,), (0,)), ((), ())), preferred_element_type=F32)


def one_hot(index, count):
    return (index[:, None] == jnp.arange(count, dtype=jnp.int32)[None, :]).astype(BF)


def swapped(shard, axis, by):
    size = lax.axis_size(axis)
    return lax.ppermute(shard, axis, [(i, i ^ by) for i in range(size)])


def tp_sum(values):
    values = values + swapped(values, "par", 1)
    others = [swapped(values, "zz", by) for by in range(1, ZZ)]
    for other in others:
        values = values + other
    return values


def gathered_rows(shard, axis):
    size, own = lax.axis_size(axis), lax.axis_index(axis)
    rows = shard.shape[0]
    whole = jnp.zeros((size * rows,) + shard.shape[1:], shard.dtype)
    others = [swapped(shard, axis, by) for by in range(1, size)]
    for by, block in enumerate([shard] + others):
        whole = lax.dynamic_update_slice_in_dim(whole, block, (own ^ by) * rows, 0)
    return whole


def scattered_rows(whole, axis):
    size, own = lax.axis_size(axis), lax.axis_index(axis)
    rows = whole.shape[0] // size
    blocks = [
        lax.dynamic_slice_in_dim(whole, (own ^ by) * rows, rows, 0) for by in range(size)
    ]
    total = blocks[0].astype(F32)
    for by in range(1, size):
        total = total + swapped(blocks[by], axis, by).astype(F32)
    return total


def group_tokens(shard):
    line = [shard] + [swapped(shard, "zz", by) for by in range(1, ZZ)]
    line = jnp.concatenate(line, 0)
    both = jnp.concatenate([line, swapped(line, "par", 1)], 0)
    if lax.axis_size("rep") > 1:
        both = lax.all_gather(both, "rep", axis=0, tiled=True)
    return both


def inv_rms(values):
    return lax.rsqrt(jnp.mean(values * values, axis=-1, keepdims=True) + EPSILON)


def rms_back(grad_y, values, inv, gain):
    scaled = values * inv
    gg = grad_y * gain
    return (gg - scaled * jnp.mean(gg * scaled, axis=-1, keepdims=True)) * inv


def gain_back(grad_y, values, inv):
    return jnp.sum(grad_y.astype(F32) * (values * inv), axis=0)


def iota(shape, dim):
    return lax.broadcasted_iota(jnp.int32, shape, dim)


def exact(a, b):
    return jnp.dot(a, b, preferred_element_type=F32, precision=lax.Precision.HIGHEST)


def halves(vals):
    high = vals.astype(BF)
    return high, (vals - high.astype(F32)).astype(BF)


def fine_left(kind, a, b):
    high, low = halves(a)
    return kind(high, b) + kind(low, b)


def fine_right(kind, a, b):
    high, low = halves(b)
    return kind(a, high) + kind(a, low)


def fine_both(kind, a, b):
    a_high, a_low = halves(a)
    b_high, b_low = halves(b)
    return kind(a_high, b_high) + (kind(a_high, b_low) + kind(a_low, b_high))


def by_head(vals):
    lane = iota((1, XW), 1)
    cols = [vals[:, DTL + h : DTL + h + 1] for h in range(HEADS)]
    out = cols[HEADS - 1]
    for h in range(HEADS - 2, -1, -1):
        out = jnp.where(lane < MP * (h + 1), cols[h], out)
    return out


def head_lanes():
    return (iota((XW, 128), 0) // MP + DTL == iota((XW, 128), 1)).astype(F32)


def head_only(vals, h):
    lane = iota((1, XW), 1)
    return jnp.where((lane >= MP * h) & (lane < MP * (h + 1)), vals, 0.0)


def chunk_terms(buf, tile, meta, seg_row, taps, heads, size):
    shifts = [buf[8 : 8 + size, :]]
    for lag in range(1, CONV):
        shifts.append(buf[8 - lag : 8 - lag + size, :] * meta[:, 2 + lag : 3 + lag])
    pre = taps[CONV : CONV + 1, :] + taps[CONV - 1 : CONV, :] * shifts[0]
    for lag in range(1, CONV):
        pre = pre + taps[CONV - 1 - lag : CONV - lag, :] * shifts[lag]
    sig = jax.nn.sigmoid(pre)
    conv = (pre * sig).astype(BF)
    bm, cm, xs = conv[:, :NS], conv[:, NS : 2 * NS], conv[:, 2 * NS : CW]
    raw = tile + heads[0:1, :]
    dt = jnp.maximum(raw, 0.0) + jnp.log1p(jnp.exp(-jnp.abs(raw)))
    la = -dt * heads[1:2, :]
    row, col = iota((size, size), 0), iota((size, size), 1)
    cum = exact((row >= col).astype(F32), la)
    allowed = (meta[:, 0:1] == seg_row) & (row >= col)
    last = cum[size - 1 : size, :]
    win = jnp.exp(cum) * meta[:, 1:2]
    ramp = jnp.exp(last - cum) * meta[:, 2:3]
    flow = jnp.exp(last) * meta[size - 1 : size, 1:2]
    return dict(
        shifts=shifts, pre=pre, sig=sig, bm=bm, cm=cm, xs=xs, raw=raw, dt=dt, la=la, cum=cum,
        cum_t=cum.T, dt_t=dt.T, allowed=allowed, win=win, ramp=ramp, flow=flow,
        cb=dot_nt(cm, bm), row=row, col=col,
    )


def decay_of(t, h):
    at = DTL + h
    gap = t["cum"][:, at : at + 1] - t["cum_t"][at : at + 1, :]
    return jnp.exp(jnp.where(t["allowed"], gap, MASKED))


def ssd_fwd_kernel(
    p_ref, meta_ref, seg_ref, taps_ref, heads_ref, skip_ref, ssd_ref, gated_ref, sum_ref, st_ref,
    state, buf,
):
    size = p_ref.shape[0]

    @pl.when(pl.program_id(0) == 0)
    def _():
        state[...] = jnp.zeros_like(state)
        buf[...] = jnp.zeros_like(buf)

    st_ref[0] = state[...]
    buf[0:8, :] = buf[size : size + 8, :]
    buf[8 : 8 + size, :] = p_ref[:, :CW].astype(BF).astype(F32)
    tile = p_ref[:, 640:768].astype(BF).astype(F32)
    t = chunk_terms(buf, tile, meta_ref[...], seg_ref[0], taps_ref[...], heads_ref[...], size)
    xs = t["xs"].astype(F32)
    y = fine_right(dot_nt, t["cm"], state[...]) * by_head(t["win"]) + skip_ref[...] * xs
    for h in range(HEADS):
        at = DTL + h
        kern = decay_of(t, h) * t["cb"] * t["dt_t"][at : at + 1, :]
        y = y + fine_left(dot, kern, head_only(xs, h).astype(BF))
    weighted = xs * by_head(t["ramp"] * t["dt"])
    flow = jnp.sum(head_lanes() * t["flow"], axis=1, keepdims=True)
    state[...] = flow * state[...] + fine_left(dot_tn, weighted, t["bm"])
    z = p_ref[:, 512 : 512 + XW].astype(BF).astype(F32)
    gated = y * (z * jax.nn.sigmoid(z))
    ssd_ref[...] = y
    gated_ref[...] = gated
    ones = jnp.ones((8, XW), F32)
    total = lax.dot_general(
        ones, gated * gated, (((1,), (1,)), ((), ())), preferred_element_type=F32,
        precision=lax.Precision.HIGHEST,
    )
    sum_ref[0] = total[0:1, :]


def ssd_bwd_kernel(
    p_ref, prev_ref, meta_ref, seg_ref, ssd_ref, gmix_ref, scale_ref, st_ref, taps_ref, heads_ref,
    skip_ref, gain_ref, out_ref, taps_acc, small_acc, grad, buf, gbuf,
):
    size = p_ref.shape[0]

    @pl.when(pl.program_id(0) == 0)
    def _():
        grad[...] = jnp.zeros_like(grad)
        gbuf[...] = jnp.zeros_like(gbuf)
        taps_acc[...] = jnp.zeros_like(taps_acc)
        small_acc[...] = jnp.zeros_like(small_acc)

    buf[0:8, :] = prev_ref[:, :CW].astype(BF).astype(F32)
    buf[8 : 8 + size, :] = p_ref[:, :CW].astype(BF).astype(F32)
    tile = p_ref[:, 640:768].astype(BF).astype(F32)
    meta, taps, heads, skip = meta_ref[...], taps_ref[...], heads_ref[...], skip_ref[...]
    t = chunk_terms(buf, tile, meta, seg_ref[0], taps, heads, size)
    xs = t["xs"].astype(F32)
    z = p_ref[:, 512 : 512 + XW].astype(BF).astype(F32)
    sz = jax.nn.sigmoid(z)
    silu = z * sz
    ssd = ssd_ref[...]
    inv, mean = scale_ref[:, 0:1], scale_ref[:, 1:2]
    scaled = ssd * silu * inv
    gmix = gmix_ref[:, :XW]
    g_gated = (gmix * gain_ref[...] - scaled * mean) * inv
    gy = g_gated * silu
    gz = g_gated * ssd * sz * (1.0 + z * (1.0 - sz))
    entering = st_ref[0]
    win, ramp, dt = by_head(t["win"]), by_head(t["ramp"]), by_head(t["dt"])
    from_b = fine_right(dot_nt, t["bm"], grad[...])
    gyw = gy * win
    xw = xs * ramp * dt
    dxs = skip * gy + ramp * dt * from_b
    dc = fine_both(dot, gyw, entering)
    db = fine_both(dot, xw, grad[...])
    lanes = head_lanes()
    carried = exact(gyw * fine_right(dot_nt, t["cm"], entering), lanes)
    ramped = exact(xs * from_b * ramp, lanes)
    flow = jnp.sum(lanes * t["flow"], axis=1, keepdims=True)
    passed = jnp.sum(grad[...] * entering, axis=1, keepdims=True) * flow
    d_last = jnp.sum(lanes * passed, axis=0, keepdims=True)
    grad[...] = flow * grad[...] + fine_left(dot_tn, gyw, t["cm"])
    lane = iota((size, 128), 1)
    sub = iota((128, size), 0)
    dcb = jnp.zeros((size, size), F32)
    rows = jnp.zeros((size, 128), F32)
    cols = jnp.zeros((128, size), F32)
    for h in range(HEADS):
        at = DTL + h
        decay = decay_of(t, h)
        dt_row = t["dt_t"][at : at + 1, :]
        weight = decay * dt_row
        gy_h = head_only(gy, h)
        dk = fine_left(dot_nt, gy_h, t["xs"])
        dcb = dcb + dk * weight
        inner = dk * decay * t["cb"]
        rows = jnp.where(lane == at, jnp.sum(inner * dt_row, axis=1, keepdims=True), rows)
        cols = jnp.where(sub == at, jnp.sum(inner, axis=0, keepdims=True), cols)
        dxs = dxs + fine_both(dot_tn, weight * t["cb"], gy_h)
    cols = cols.T
    d_dt = cols + ramped
    after = ramped * t["dt"]
    d_cum = rows + carried - d_dt * t["dt"]
    d_last = d_last + jnp.sum(after, axis=0, keepdims=True)
    d_cum = d_cum + jnp.where(iota((size, 128), 0) == size - 1, d_last, 0.0)
    d_la = exact((t["row"] <= t["col"]).astype(F32), d_cum)
    d_raw = (d_dt - heads[1:2, :] * d_la) * jax.nn.sigmoid(t["raw"])
    dc = dc + fine_left(dot, dcb, t["bm"])
    db = db + fine_left(dot_tn, dcb, t["cm"])
    pre, sig = t["pre"], t["sig"]
    slope = sig * (1.0 + pre * (1.0 - sig))
    gbuf[size : size + 8, :] = gbuf[0:8, :]
    gbuf[0:size, :NS] = db * slope[:, :NS]
    gbuf[0:size, NS : 2 * NS] = dc * slope[:, NS : 2 * NS]
    gbuf[0:size, 2 * NS : CW] = dxs * slope[:, 2 * NS : CW]
    d_pre = gbuf[0:size, :]
    d_in = taps[CONV - 1 : CONV, :] * d_pre
    for lag in range(1, CONV):
        d_in = d_in + taps[CONV - 1 - lag : CONV - lag, :] * (
            gbuf[lag : lag + size, :] * meta[:, 5 + lag : 6 + lag]
        )
    for lag in range(CONV):
        at = CONV - 1 - lag
        taps_acc[at : at + 1, :] += jnp.sum(d_pre * t["shifts"][lag], axis=0, keepdims=True)
    taps_acc[CONV : CONV + 1, :] += jnp.sum(d_pre, axis=0, keepdims=True)
    small_acc[0:1, :XW] += jnp.sum(gmix * scaled, axis=0, keepdims=True)
    small_acc[1:2, :XW] += jnp.sum(gy * xs, axis=0, keepdims=True)
    small_acc[2:3, :128] += jnp.sum(d_raw, axis=0, keepdims=True)
    small_acc[3:4, :128] += jnp.sum(t["la"] * d_la, axis=0, keepdims=True)
    out_ref[:, :CW] = d_in.astype(BF)
    out_ref[:, CW:512] = jnp.zeros((size, 512 - CW), BF)
    out_ref[:, 512 : 512 + XW] = gz.astype(BF)
    out_ref[:, 704:768] = d_raw[:, DTL:].astype(BF)


def full_spec(shape):
    return pl.BlockSpec(shape, lambda i: (0,) * len(shape))


def kernel_params():
    return pltpu.CompilerParams(
        dimension_semantics=("arbitrary",), vmem_limit_bytes=48 * 1024 * 1024
    )


def ssd_forward(p, meta, seg_rows, w):
    rows = p.shape[0]
    size = min(CHUNK, rows)
    chunks = rows // size
    return pl.pallas_call(
        ssd_fwd_kernel,
        grid=(chunks,),
        in_specs=[
            pl.BlockSpec((size, 768), lambda i: (i, 0)),
            pl.BlockSpec((size, 16), lambda i: (i, 0)),
            pl.BlockSpec((1, 1, size), lambda i: (i, 0, 0)),
            full_spec((8, CW)),
            full_spec((8, 128)),
            full_spec((1, XW)),
        ],
        out_specs=[
            pl.BlockSpec((size, XW), lambda i: (i, 0)),
            pl.BlockSpec((size, XW), lambda i: (i, 0)),
            pl.BlockSpec((1, 1, size), lambda i: (i, 0, 0)),
            pl.BlockSpec((1, XW, NS), lambda i: (i, 0, 0)),
        ],
        out_shape=[
            jax.ShapeDtypeStruct((rows, XW), F32),
            jax.ShapeDtypeStruct((rows, XW), F32),
            jax.ShapeDtypeStruct((chunks, 1, size), F32),
            jax.ShapeDtypeStruct((chunks, XW, NS), F32),
        ],
        scratch_shapes=[pltpu.VMEM((XW, NS), F32), pltpu.VMEM((size + 8, CW), F32)],
        compiler_params=kernel_params(),
        cost_estimate=pl.CostEstimate(
            flops=rows * size * 2 * 1024, bytes_accessed=rows * 6000, transcendentals=rows * 1500
        ),
        name="ssd_forward",
    )(p, meta, seg_rows, w["taps"], w["heads"], w["skip"])


def ssd_backward(p, meta, seg_rows, ssd, gmix, scale, states, w):
    rows = p.shape[0]
    size = min(CHUNK, rows)
    chunks = rows // size
    back = lambda i: (chunks - 1 - i, 0)
    back3 = lambda i: (chunks - 1 - i, 0, 0)
    return pl.pallas_call(
        ssd_bwd_kernel,
        grid=(chunks,),
        in_specs=[
            pl.BlockSpec((size, 768), back),
            pl.BlockSpec(
                (8, 768), lambda i: (jnp.maximum((chunks - 1 - i) * (size // 8) - 1, 0), 0)
            ),
            pl.BlockSpec((size, 16), back),
            pl.BlockSpec((1, 1, size), back3),
            pl.BlockSpec((size, XW), back),
            pl.BlockSpec((size, XW + HD), back),
            pl.BlockSpec((size, 2), back),
            pl.BlockSpec((1, XW, NS), back3),
            full_spec((8, CW)),
            full_spec((8, 128)),
            full_spec((1, XW)),
            full_spec((1, XW)),
        ],
        out_specs=[
            pl.BlockSpec((size, 768), back),
            full_spec((8, CW)),
            full_spec((8, 256)),
        ],
        out_shape=[
            jax.ShapeDtypeStruct((rows, 1152), BF),
            jax.ShapeDtypeStruct((8, CW), F32),
            jax.ShapeDtypeStruct((8, 256), F32),
        ],
        scratch_shapes=[
            pltpu.VMEM((XW, NS), F32),
            pltpu.VMEM((size + 8, CW), F32),
            pltpu.VMEM((size + 8, CW), F32),
        ],
        compiler_params=kernel_params(),
        cost_estimate=pl.CostEstimate(
            flops=rows * size * 2 * 3000, bytes_accessed=rows * 9000, transcendentals=rows * 1500
        ),
        name="ssd_backward",
    )(p, p, meta, seg_rows, ssd, gmix, scale, states, w["taps"], w["heads"], w["skip"], w["gain"])


def turn(vals, cosine, sine):
    return vals * cosine + pltpu.roll(vals, HD // 2, 1) * sine


def allowed_keys(meta, seg_all, first):
    size, keys = meta.shape[0], seg_all.shape[1]
    return (meta[:, 0:1] == seg_all) & (iota((size, keys), 0) + first >= iota((size, keys), 1))


def attn_fwd_kernel(
    p_ref, cos_ref, sin_ref, meta_ref, seg_ref, q_ref, k_ref, v_ref, att_ref, log_ref
):
    size = q_ref.shape[0]
    first = pl.program_id(0) * size

    @pl.when(pl.program_id(0) == 0)
    def _():
        k_ref[...] = turn(p_ref[:, HD : 2 * HD], cos_ref[...], sin_ref[...]).astype(BF)
        v_ref[...] = p_ref[:, 2 * HD :].astype(BF)

    at = pl.ds(pl.multiple_of(first, size), size)
    q = turn(p_ref[at, :HD], cos_ref[at, :], sin_ref[at, :]).astype(BF)
    q_ref[...] = q
    scores = dot_nt(q, k_ref[...]) * HD ** (-0.5)
    scores = jnp.where(allowed_keys(meta_ref[...], seg_ref[...], first), scores, MASKED)
    top = jnp.max(scores, axis=1, keepdims=True)
    prob = jnp.exp(scores - top)
    total = jnp.sum(prob, axis=1, keepdims=True)
    att_ref[...] = dot(prob.astype(BF), v_ref[...]) / total
    log_ref[...] = jnp.broadcast_to(top + jnp.log(total), log_ref.shape)


def attn_bwd_kernel(
    held_ref, q_ref, k_ref, v_ref, att_ref, log_ref, g_ref, cos_ref, sin_ref, meta_ref, seg_ref,
    out_ref, gk, gv,
):
    del held_ref
    size = q_ref.shape[0]
    step = pl.program_id(0)
    first = step * size

    @pl.when(step == 0)
    def _():
        gk[...] = jnp.zeros_like(gk)
        gv[...] = jnp.zeros_like(gv)

    at = pl.ds(pl.multiple_of(first, size), size)
    q = q_ref[...]
    scores = dot_nt(q, k_ref[...]) * HD ** (-0.5) - log_ref[:, 0:1]
    keep = allowed_keys(meta_ref[...], seg_ref[...], first)
    prob = jnp.exp(jnp.where(keep, scores, MASKED))
    g = g_ref[:, XW:].astype(BF)
    delta = jnp.sum(g.astype(F32) * att_ref[...], axis=1, keepdims=True)
    gs = (prob * (dot_nt(g, v_ref[...]) - delta)).astype(BF)
    gq = (dot(gs, k_ref[...]) * HD ** (-0.5)).astype(BF).astype(F32)
    out_ref[at, :HD] = turn(gq, cos_ref[at, :], -sin_ref[at, :]).astype(BF)
    gk[...] += dot_tn(gs, q) * HD ** (-0.5)
    gv[...] += dot_tn(prob.astype(BF), g)

    @pl.when(step == pl.num_programs(0) - 1)
    def _():
        gk_low = gk[...].astype(BF).astype(F32)
        out_ref[:, HD : 2 * HD] = turn(gk_low, cos_ref[...], -sin_ref[...]).astype(BF)
        out_ref[:, 2 * HD :] = gv[...].astype(BF)


def attn_forward(p, tables, meta, seg_all):
    rows = p.shape[0]
    size = min(ATTN, rows)
    block = lambda i: (i, 0)
    return pl.pallas_call(
        attn_fwd_kernel,
        grid=(rows // size,),
        in_specs=[
            pl.BlockSpec((rows, 384), lambda i: (0, 2)),
            full_spec((rows, HD)),
            full_spec((rows, HD)),
            pl.BlockSpec((size, 16), block),
            full_spec((1, rows)),
        ],
        out_specs=[
            pl.BlockSpec((size, HD), block),
            full_spec((rows, HD)),
            full_spec((rows, HD)),
            pl.BlockSpec((size, HD), block),
            pl.BlockSpec((size, 8), block),
        ],
        out_shape=[
            jax.ShapeDtypeStruct((rows, HD), BF),
            jax.ShapeDtypeStruct((rows, HD), BF),
            jax.ShapeDtypeStruct((rows, HD), BF),
            jax.ShapeDtypeStruct((rows, HD), F32),
            jax.ShapeDtypeStruct((rows, 8), F32),
        ],
        compiler_params=kernel_params(),
        cost_estimate=pl.CostEstimate(
            flops=rows * rows * 4 * HD, bytes_accessed=rows * 4000, transcendentals=rows * rows
        ),
        name="attn_forward",
    )(p, *tables, meta, seg_all)


def attn_backward(held, q, k, v, att, logs, g_mixed, tables, meta, seg_all):
    rows = q.shape[0]
    size = min(ATTN, rows)
    block = lambda i: (i, 0)
    return pl.pallas_call(
        attn_bwd_kernel,
        grid=(rows // size,),
        in_specs=[
            pl.BlockSpec(memory_space=pl.ANY),
            pl.BlockSpec((size, HD), block),
            full_spec((rows, HD)),
            full_spec((rows, HD)),
            pl.BlockSpec((size, HD), block),
            pl.BlockSpec((size, 8), block),
            pl.BlockSpec((size, XW + HD), block),
            full_spec((rows, HD)),
            full_spec((rows, HD)),
            pl.BlockSpec((size, 16), block),
            full_spec((1, rows)),
        ],
        out_specs=pl.BlockSpec((rows, 384), lambda i: (0, 2)),
        out_shape=jax.ShapeDtypeStruct((rows, 1152), BF),
        scratch_shapes=[pltpu.VMEM((rows, HD), F32), pltpu.VMEM((rows, HD), F32)],
        input_output_aliases={0: 0},
        compiler_params=kernel_params(),
        cost_estimate=pl.CostEstimate(
            flops=rows * rows * 10 * HD, bytes_accessed=rows * 5000, transcendentals=rows * rows
        ),
        name="attn_backward",
    )(held, q, k, v, att, logs, g_mixed, *tables, meta, seg_all)


def columns_kernel(c_ref, *refs):
    in_ref, q_ref, k_ref, v_ref = refs[-4:]
    bc = None
    for t in range(TP):
        c = c_ref[t].astype(F32)
        in_ref[0, :, XW * t : XW * (t + 1)] = c[:, 512 : 512 + XW]
        in_ref[0, :, DSSM + XW * t : DSSM + XW * (t + 1)] = c[:, 2 * NS : CW]
        at = DSSM + CONVCH + HEADS * t
        in_ref[0, :, at : at + HEADS] = c[:, 704 : 704 + HEADS]
        bc = c[:, : 2 * NS] if t == 0 else bc + c[:, : 2 * NS]
        q_ref[0, :, HD * t : HD * (t + 1)] = c[:, 768:896]
        group = TP // KVH
        kv = c[:, 896:1152] if t % group == 0 else kv + c[:, 896:1152]
        if t % group == group - 1:
            at = HD * (t // group)
            k_ref[0, :, at : at + HD] = kv[:, :HD]
            v_ref[0, :, at : at + HD] = kv[:, HD:]
    in_ref[0, :, 2 * DSSM : DSSM + CONVCH] = bc


def rows_kernel(c_ref, *refs):
    gate_ref, up_ref, out_ref, attn_ref, down_ref = refs[-5:]
    ff = gate_ref.shape[2] // PAR
    for par in range(PAR):
        gate_ref[0, :, ff * par : ff * (par + 1)] = c_ref[par, :, :ff].astype(F32)
        up_ref[0, :, ff * par : ff * (par + 1)] = c_ref[par, :, ff : 2 * ff].astype(F32)
        turned = c_ref[par, :, 2 * ff :].astype(F32).T
        out_ref[0, XW * par : XW * (par + 1), :] = turned[:XW]
        attn_ref[0, HD * par : HD * (par + 1), :] = turned[XW : XW + HD]
        down_ref[0, ff * par : ff * (par + 1), :] = turned[XW + HD : XW + HD + ff]


def assembled(kernel, gathered, in_block, grid, blocks, shapes, layer, held):
    any_spec = pl.BlockSpec(memory_space=pl.ANY)
    held = () if held is None else tuple(held)
    place = [
        pl.BlockSpec((1,) + shape, lambda i, by=by: (layer,) + by(i)) for shape, by in blocks
    ]
    return pl.pallas_call(
        kernel,
        grid=(grid,),
        in_specs=[in_block] + [any_spec] * len(held),
        out_specs=place,
        out_shape=[jax.ShapeDtypeStruct((LAYERS,) + shape, F32) for shape in shapes],
        input_output_aliases={1 + i: i for i in range(len(held))},
        compiler_params=kernel_params(),
        cost_estimate=pl.CostEstimate(flops=0, bytes_accessed=12000000, transcendentals=0),
        name="assemble",
    )(gathered, *held)


def column_outputs(gathered, layer, held):
    rows = gathered.shape[1]
    size = 64
    by = lambda i: (i, 0)
    widths = (DSSM + CONVCH + MH, QH * HD, KVH * HD, KVH * HD)
    return assembled(
        columns_kernel,
        gathered,
        pl.BlockSpec((TP, size, gathered.shape[2]), lambda i: (0, i, 0)),
        rows // size,
        [((size, width), by) for width in widths],
        [(rows, width) for width in widths],
        layer,
        held,
    )


def row_outputs(gathered, layer, held, ff):
    rows = gathered.shape[1]
    by = lambda i: (0, i)
    heights = (XW, HD, ff)
    blocks = [((rows, PAR * ff), by)] * 2 + [((PAR * h, rows), by) for h in heights]
    shapes = [(rows, TP * ff)] * 2 + [(PAR * h, ZZ * rows) for h in heights]
    return assembled(
        rows_kernel,
        gathered,
        pl.BlockSpec((PAR, rows, gathered.shape[2]), lambda i: (i, 0, 0)),
        ZZ,
        blocks,
        shapes,
        layer,
        held,
    )


def layer_forward(h, w, meta):
    marks, seg_rows, seg_all, tables = meta
    inv1 = inv_rms(h)
    normed = (h * inv1 * w["norm_gain"]).astype(BF)
    p = dot(normed, w["w1"])
    ssd, gated, squares, states = ssd_forward(p, marks, seg_rows, w)
    square = tp_sum(squares)
    q, k, v, attended, logs = attn_forward(p, tables, marks, seg_all)
    inv_g = lax.rsqrt(square.reshape(-1) / DSSM + EPSILON)[:, None]
    mixer = (gated * inv_g * w["gain"]).astype(BF)
    mixed = jnp.concatenate([mixer, attended.astype(BF)], axis=1)
    mid = h + lax.psum(dot(mixed, w["wr"][: XW + HD]).astype(BF), TPA).astype(F32)
    inv2 = inv_rms(mid)
    normed2 = (mid * inv2 * w["ffn_gain"]).astype(BF)
    gu = dot(normed2, w["w2"])
    ff = gu.shape[1] // 2
    act = (jax.nn.silu(gu[:, :ff]) * gu[:, ff:]).astype(BF)
    kept = dict(
        h=h, inv1=inv1, normed=normed, p=p, ssd=ssd, gated=gated, states=states, inv_g=inv_g,
        q=q, k=k, v=v, attended=attended, logs=logs, mixed=mixed, mid=mid, inv2=inv2,
        normed2=normed2, gu=gu, act=act,
    )
    return mid, act, kept


def layer_backward(gout, w, kept, meta, reduce_rows, pending, finish):
    marks, seg_rows, seg_all, tables = meta
    g_down = gout.astype(BF)
    g_act = dot_nt(g_down, w["wr"][XW + HD :])
    d_down = dot_tn(g_down, kept["act"])
    ff = kept["gu"].shape[1] // 2
    gate, up = kept["gu"][:, :ff], kept["gu"][:, ff:]
    sig = jax.nn.sigmoid(gate)
    g_gate = g_act * up * sig * (1.0 + gate * (1.0 - sig))
    g_up = g_act * gate * sig
    g_gu = jnp.concatenate([g_gate.astype(BF), g_up.astype(BF)], axis=1)
    part_2 = dot_nt(g_gu, w["w2"]).astype(BF)
    g_n2 = lax.psum(part_2, TPA).astype(F32)
    d_ffn_gain = gain_back(part_2, kept["mid"], kept["inv2"])
    d_w2 = dot_tn(kept["normed2"], g_gu)
    g_mid = gout + rms_back(g_n2, kept["mid"], kept["inv2"], w["ffn_gain"])
    g_low = g_mid.astype(BF)
    g_mixed = dot_nt(g_low, w["wr"][: XW + HD])
    d_wr = dot_tn(g_low, kept["mixed"])
    early = reduce_rows(d_w2, d_wr, d_down)
    weighted = g_mixed[:, :XW] * w["gain"] * kept["gated"] * kept["inv_g"]
    mean = tp_sum(jnp.sum(weighted, axis=-1))[:, None] / DSSM
    scale = jnp.concatenate([kept["inv_g"], mean], axis=1)
    held, d_taps, d_small = ssd_backward(
        kept["p"], marks, seg_rows, kept["ssd"], g_mixed, scale, kept["states"], w
    )
    g_pr = attn_backward(
        held, kept["q"], kept["k"], kept["v"], kept["attended"], kept["logs"], g_mixed, tables,
        marks, seg_all,
    )
    g_pr, pending = lax.optimization_barrier((g_pr, pending))
    part_1 = dot_nt(g_pr, w["w1"]).astype(BF)
    if finish is None:
        g_n1 = lax.psum(part_1, TPA).astype(F32)
        g_h = g_mid + rms_back(g_n1, kept["h"], kept["inv1"], w["norm_gain"])
    else:
        g_h = finish(g_pr, g_mid)
    d_w1 = dot_tn(kept["normed"], g_pr)
    d_norm_gain = gain_back(part_1, kept["h"], kept["inv1"])
    d_skip = jnp.sum(d_small[1, :XW].reshape(HEADS, MP), axis=1)
    at = slice(DTL, DTL + HEADS)
    small = (
        d_norm_gain, d_taps[:CONV], d_taps[CONV], d_small[2, at], d_small[3, at], d_skip,
        d_small[0, :XW], d_ffn_gain,
    )
    return g_h, d_w1, early, pending, small


def per_device(
    block_in,
    seq_lengths,
    norm_gain,
    in_proj,
    conv_weight,
    conv_bias,
    dt_bias,
    decay_log,
    skip_gain,
    mixer_gain,
    out_proj,
    query_proj,
    key_proj,
    value_proj,
    attn_proj,
    ffn_gain,
    gate_proj,
    up_proj,
    down_proj,
    out_grad,
):
    fs = lax.axis_size("fsdp")
    reps = lax.axis_size("rep")
    ctx = reps * TP
    own_rows, width = block_in.shape
    rows = ctx * own_rows
    f = lax.axis_index("fsdp")
    rep = lax.axis_index("rep")
    t = lax.axis_index(TPA)
    every = ("rep",) + TPA

    lengths = seq_lengths[0]
    ends = jnp.cumsum(lengths)
    starts = ends - lengths
    line = jnp.arange(rows, dtype=jnp.int32)
    seg = jnp.sum((line[:, None] >= ends[None, :]).astype(jnp.int32), axis=1)
    pos = line - jnp.sum(jnp.where(seg[:, None] == jnp.arange(SEQS)[None, :], starts[None, :], 0), axis=1)
    pieces = lengths // ctx
    p_ends = jnp.cumsum(pieces)
    p_starts = p_ends - pieces

    def placed(piece):
        local = line[: piece.shape[0]] % own_rows
        l_seg = jnp.sum((local[:, None] >= p_ends[None, :]).astype(jnp.int32), axis=1)
        pick = l_seg[:, None] == jnp.arange(SEQS)[None, :]
        moved = starts[None, :] - p_starts[None, :] + piece[:, None] * pieces[None, :]
        return jnp.sum(jnp.where(pick, moved, 0), axis=1) + local

    slot = line // own_rows
    near = (lax.axis_index("zz") ^ (slot % ZZ)) * PAR
    near = near + (lax.axis_index("par") ^ (slot // ZZ % PAR))
    place_rel = placed(slot // TP * TP + near)
    half = HD // 2
    frequency = jnp.exp(-math.log(ROPE_BASE) * jnp.arange(half, dtype=F32) / half)
    angles = pos.astype(F32)[:, None] * frequency[None, :]
    cosine, sine = jnp.cos(angles), jnp.sin(angles)
    tables = (
        jnp.concatenate([cosine, cosine], axis=1),
        jnp.concatenate([-sine, sine], axis=1),
    )
    size = min(CHUNK, rows)
    by_chunk = seg.reshape(-1, size)
    last_seg = by_chunk[:, -1:]
    prev_seg = jnp.concatenate([jnp.full((1, 1), -1, last_seg.dtype), last_seg[:-1]], 0)
    ahead = jnp.concatenate([pos, jnp.zeros((CONV - 1,), pos.dtype)])
    marks = [seg, (by_chunk == prev_seg).reshape(-1), (by_chunk == last_seg).reshape(-1)]
    marks += [pos >= lag for lag in range(1, CONV)]
    marks += [ahead[lag : lag + rows] >= lag for lag in range(1, CONV)]
    marks = jnp.stack([m.astype(F32) for m in marks] + [jnp.zeros((rows,), F32)] * 7, axis=1)
    seg_f = seg.astype(F32)
    meta = (marks, seg_f.reshape(-1, 1, size), seg_f.reshape(1, rows), tables)

    to_seq = one_hot(place_rel, rows).T

    def cut(array, layer, at, count, axis):
        begin = [layer, 0, 0]
        extent = [1] + list(array.shape[1:])
        begin[axis], extent[axis] = at, count
        return lax.dynamic_slice(array, begin, extent)[0]

    ff = gate_proj.shape[2] // TP
    own_kv = HD * (t * KVH // TP)
    depth = in_proj.shape[1]

    def columns_1(layer):
        return jnp.concatenate(
            [
                in_proj[layer, :, 2 * DSSM : DSSM + CONVCH],
                cut(in_proj, layer, DSSM + XW * t, XW, 2),
                jnp.zeros((depth, 64), BF),
                cut(in_proj, layer, XW * t, XW, 2),
                cut(in_proj, layer, DSSM + CONVCH + HEADS * t, HEADS, 2),
                jnp.zeros((depth, 64 - HEADS), BF),
                cut(query_proj, layer, HD * t, HD, 2),
                cut(key_proj, layer, own_kv, HD, 2),
                cut(value_proj, layer, own_kv, HD, 2),
            ],
            1,
        )

    def columns_2(layer):
        return jnp.concatenate(
            [cut(gate_proj, layer, ff * t, ff, 2), cut(up_proj, layer, ff * t, ff, 2)], 1
        )

    par = t % PAR

    def row_chunk(layer):
        whole = jnp.concatenate(
            [
                cut(out_proj, layer, XW * par, XW, 1),
                cut(attn_proj, layer, HD * par, HD, 1),
                cut(down_proj, layer, ff * par, ff, 1),
            ],
            0,
        )
        part = whole.shape[0] // ZZ
        return lax.dynamic_slice_in_dim(whole, lax.axis_index("zz") * part, part, 0)

    forth = []
    for s in range(fs):
        for r in range(reps):
            for c in range(TP):
                src = (s * reps + r) * TP + c
                dst = ((c // PAR) * reps + r) * TP + PAR * s + c % PAR
                forth.append((src, dst))
    back = [(b, a) for a, b in forth]
    axes = ("fsdp",) + every

    smalls = jnp.concatenate(
        [
            norm_gain,
            conv_weight.transpose(0, 2, 1).reshape(LAYERS, -1),
            conv_bias,
            dt_bias,
            decay_log,
            skip_gain,
            mixer_gain,
            ffn_gain,
        ],
        axis=1,
    )
    w1 = [gathered_rows(columns_1(0), "fsdp"), None]
    x_all = group_tokens(block_in)
    small_all = gathered_rows(smalls[None], "fsdp")
    w2 = [None, None]
    wr = [None, None]
    x_all, w1[0], others, own_grad = lax.optimization_barrier(
        (
            x_all,
            w1[0],
            ([row_chunk(i) for i in range(LAYERS)], [columns_2(i) for i in range(LAYERS)], columns_1(1)),
            out_grad,
        )
    )
    wr[0] = gathered_rows(lax.ppermute(others[0][0], axes, forth), "fsdp")
    w2[0] = gathered_rows(others[1][0], "fsdp")
    w1[1] = gathered_rows(others[2], "fsdp")
    wr[1] = gathered_rows(lax.ppermute(others[0][1], axes, forth), "fsdp")
    w2[1] = gathered_rows(others[1][1], "fsdp")
    g_all = group_tokens(own_grad)

    sizes = [
        norm_gain.shape[1],
        CONV * conv_weight.shape[1],
        conv_bias.shape[1],
        dt_bias.shape[1],
        decay_log.shape[1],
        skip_gain.shape[1],
        mixer_gain.shape[1],
        ffn_gain.shape[1],
    ]
    offsets = [sum(sizes[:i]) for i in range(len(sizes) + 1)]

    def own_conv(full):
        return jnp.concatenate(
            [full[..., DSSM:], lax.dynamic_slice_in_dim(full, XW * t, XW, full.ndim - 1)], -1
        )

    weights = []
    for layer in range(LAYERS):
        part = [
            small_all[:, layer, offsets[i] : offsets[i + 1]].astype(F32) for i in range(len(sizes))
        ]
        cw = part[1].reshape(fs, CONV, -1).transpose(1, 0, 2).reshape(CONV, CONVCH)
        full = [p.reshape(-1) for p in part]
        weights.append(
            dict(
                w1=w1[layer],
                w2=w2[layer],
                wr=wr[layer],
                norm_gain=full[0],
                taps=jnp.concatenate(
                    [own_conv(cw), own_conv(full[2])[None], jnp.zeros((3, CW), F32)], 0
                ),
                heads=jnp.zeros((8, 128), F32)
                .at[0, DTL : DTL + HEADS]
                .set(lax.dynamic_slice_in_dim(full[3], HEADS * t, HEADS, 0))
                .at[1, DTL : DTL + HEADS]
                .set(jnp.exp(lax.dynamic_slice_in_dim(full[4], HEADS * t, HEADS, 0))),
                skip=jnp.repeat(lax.dynamic_slice_in_dim(full[5], HEADS * t, HEADS, 0), MP)[None],
                gain=lax.dynamic_slice_in_dim(full[6], XW * t, XW, 0)[None],
                ffn_gain=full[7],
            )
        )

    h = dot(to_seq, x_all)
    saved = []
    for layer in range(LAYERS):
        mid, act, kept = layer_forward(h, weights[layer], meta)
        saved.append(kept)
        if layer < LAYERS - 1:
            h = mid + lax.psum(dot(act, weights[layer]["wr"][XW + HD :]).astype(BF), TPA).astype(F32)

    own_hot = one_hot(placed(jnp.full((own_rows,), rep * TP + t, jnp.int32)), rows)
    rep_place = placed(rep * TP + line[: TP * own_rows] // own_rows)
    rep_hot = one_hot(rep_place, rows)
    act_rep = dot(rep_hot, act).astype(BF)
    down_own = lax.psum_scatter(
        dot(act_rep, weights[-1]["wr"][XW + HD :]).astype(BF), TPA, scatter_dimension=0, tiled=True
    )
    mid_own = jnp.dot(
        own_hot.astype(F32), mid, precision=lax.Precision.HIGHEST, preferred_element_type=F32
    )

    gout = dot(to_seq, g_all)

    def reduce_rows(d_w2, d_wr, d_down):
        d_all = jnp.concatenate([d_w2.astype(BF), d_wr.astype(BF), d_down.astype(BF)], 1)
        part = scattered_rows(d_all, "fsdp").astype(BF)
        kept_cols = d_w2.shape[1]
        moved = lax.ppermute(part[:, kept_cols:], axes, back)
        held = jnp.zeros((part.shape[0], 64), BF)
        part = jnp.concatenate([part[:, :kept_cols], moved, held], 1)
        return part

    def reduce_columns(d_w1, small_grads):
        g_n, g_cw, g_cb, g_db, g_dl, g_sk, g_mg, g_fg = small_grads
        small = jnp.concatenate(
            [g_n, g_cw.reshape(-1), g_cb, g_db, g_dl, g_sk, g_mg, g_fg]
        )
        others = [swapped(small, "fsdp", by) for by in range(1, fs)]
        for other in others:
            small = small + other
        part = scattered_rows(d_w1.astype(BF), "fsdp").astype(BF)
        held = jnp.zeros((part.shape[0] * 64,), BF)
        high = small.astype(BF)
        low = (small - lax.optimization_barrier(high).astype(F32)).astype(BF)
        held = lax.dynamic_update_slice(held, jnp.concatenate([high, low]), (0,)).reshape(-1, 64)
        return jnp.concatenate([part[:, :CW], held, part[:, 512:]], 1)

    def finish(g_pr, g_mid):
        moved = dot(rep_hot, g_pr).astype(BF)
        own = lax.psum_scatter(
            dot_nt(moved, weights[0]["w1"]).astype(BF), TPA, scatter_dimension=0, tiled=True
        ).astype(F32)
        mid = jnp.dot(
            own_hot.astype(F32), g_mid, precision=lax.Precision.HIGHEST, preferred_element_type=F32
        )
        h_own = block_in.astype(F32)
        return mid + rms_back(own, h_own, inv_rms(h_own), weights[0]["norm_gain"])

    gout, d_w1, early, down_own, small_grads = layer_backward(
        gout, weights[1], saved[1], meta, reduce_rows, down_own, None
    )
    block_out = (mid_own + down_own.astype(F32)).astype(BF)
    late = reduce_columns(d_w1, small_grads)
    pending = (lax.all_gather(early, TPA, axis=0), late)
    in_grad, d_w1, early, pending, small_grads = layer_backward(
        gout, weights[0], saved[0], meta, reduce_rows, pending, finish
    )
    in_grad = in_grad.astype(BF)
    rows_1, late = pending
    both = lax.all_gather(jnp.concatenate([late, early], 1), TPA, axis=0)
    split = late.shape[1]
    columns_0 = lax.all_gather(reduce_columns(d_w1, small_grads), TPA, axis=0)
    columns_of = [columns_0, both[:, :, :split]]
    held = row_outputs(rows_1, 1, None, ff)
    o_gate, o_up, o_out, o_attn, o_down = row_outputs(both[:, :, split:], 0, held, ff)
    held = column_outputs(columns_of[1], 1, None)
    o_in, o_q, o_k, o_v = column_outputs(columns_of[0], 0, held)

    own_sizes = [width, CONV * CW, CW, HEADS, HEADS, HEADS, XW, width]
    own_at = [sum(own_sizes[:i]) for i in range(len(own_sizes) + 1)]
    outs_small = [[] for _ in sizes]

    def conv_full(parts):
        parts = parts.astype(F32)
        return jnp.concatenate(
            [
                jnp.moveaxis(parts[..., 2 * NS :], 0, -2).reshape(parts.shape[1:-1] + (DSSM,)),
                jnp.sum(parts[..., : 2 * NS], axis=0),
            ],
            -1,
        )

    for layer in range(LAYERS):
        held = columns_of[layer][:, :, CW:512].astype(F32).reshape(TP, -1)
        held = held[:, : own_at[-1]] + held[:, own_at[-1] : 2 * own_at[-1]]
        parts = [held[:, own_at[i] : own_at[i + 1]] for i in range(len(own_sizes))]
        full = [
            jnp.sum(parts[0].astype(F32), axis=0),
            conv_full(parts[1].reshape(TP, CONV, CW)).T.reshape(-1),
            conv_full(parts[2]),
        ]
        full += [p.astype(F32).reshape(-1) for p in parts[3:7]] + [jnp.sum(parts[7].astype(F32), axis=0)]
        for i, vec in enumerate(full):
            own = vec.shape[0] // fs
            outs_small[i].append(lax.dynamic_slice_in_dim(vec, own * f, own, 0))
    (o_norm, o_cw, o_cb, o_db, o_dl, o_sk, o_mg, o_fg) = [jnp.stack(o) for o in outs_small]
    o_cw = o_cw.reshape(LAYERS, -1, CONV)

    return (
        block_out,
        in_grad,
        o_norm,
        o_in,
        o_cw,
        o_cb,
        o_db,
        o_dl,
        o_sk,
        o_mg,
        o_out,
        o_q,
        o_k,
        o_v,
        o_attn,
        o_fg,
        o_gate,
        o_up,
        o_down,
    )


def solution(mesh):
    fs = mesh.shape["fsdp"]
    inner = Mesh(
        mesh.devices.reshape(fs, mesh.shape["ctx"] // TP, ZZ, PAR), ("fsdp", "rep", "zz", "par")
    )
    tokens = P(("fsdp", "rep", "zz", "par"), None)
    vec = P(None, "fsdp")
    mat = P(None, "fsdp", None)
    kinds = (
        vec, mat, mat, vec, vec, vec, vec, vec, mat, mat, mat, mat, mat, vec, mat, mat, mat
    )
    return jax.shard_map(
        per_device,
        mesh=inner,
        in_specs=(tokens, P("fsdp", None)) + kinds + (tokens,),
        out_specs=(tokens, tokens) + kinds,
        check_vma=False,
    )
```

time: 1570 us -> 1080 us (0.69)
  local copies, waits for them, and re-layouts: 373 us -> 181 us
  other arithmetic: 258 us -> 76.7 us
  starting transfers between devices: 277 us -> 139 us
  Pallas kernels: 0 us -> 94.4 us
  matrix products: 155 us -> 113 us
    ppermute x60 -> x63, starting transfers between devices: 243 us -> 134 us  [swapped(): return lax.ppermute(shard, axis, [(i, i ^ by) for i in range(size)])]
    all_gather x4 -> x3, waiting for transfers between devices: 0.01 us -> 102 us  [the longest x1 88.3 us: per_device(): both = lax.all_gather(jnp.concatenate([late, early], 1), TPA, axis=0)]
    pallas_call x0 -> x12, Pallas kernels: none -> 94.4 us  [the longest x2 38.8 us: ssd_backward(): pl.pallas_call(ssd_bwd_kernel, grid=(chunks,), in_specs=[pl.BlockSpec((si...]
    another operation x25 -> x6, other arithmetic: 60.2 us -> 4.12 us  [the longest x4 29.5 us: ssd_local(): cum = jnp.cumsum(la, axis=1)]
    convert_element_type x29 -> x14, other arithmetic: 54.1 us -> 3.71 us  [the longest x2 1.98 us: reduce_rows(): part = scattered_rows(d_all, 'fsdp').astype(BF)]
    reduce_sum x34 -> x18, other arithmetic: 62.4 us -> 19.2 us  [the longest x3 15.8 us: gain_back(): return jnp.sum(grad_y.astype(F32) * (values * inv), axis=0)]
    slice x52 -> x27, local copies, waits for them, and re-layouts: 55.3 us -> 12.5 us  [the longest x1 8.5 us: per_device(): both[:, :, split:]]
    psum x1, waiting for transfers between devices: 83.6 us -> 42.6 us  [per_device(): lax.psum(dot(act, weights[layer]['wr'][XW + HD:]).astype(BF), TPA)]
  transfers between devices with their start and end apart: 76 -> 78, of which waited for: 18 -> 25; matrix products, arithmetic and copies ran while one was open for 41% -> 25% of each run, Pallas kernels for 0% -> 8%
where the time goes in v3:
time: 1080 us; the launch traced here: 1070 us
  waiting for transfers between devices  446 us (41%)
  local copies, waits for them, and re-layouts  181 us (17%)
  starting transfers between devices  139 us (13%)
  matrix products  113 us (10%)
  Pallas kernels  94.4 us (9%)
  other arithmetic  76.7 us (7%)
  between operations  16.9 us (2%)
    ppermute x63, starting transfers between devices, swapped(): return lax.ppermute(shard, axis, [(i, i ^ by) for i in range(size)])  134 us
    ppermute x63, waiting for transfers between devices, swapped(): return lax.ppermute(shard, axis, [(i, i ^ by) for i in range(size)])  105 us
    all_gather x1, waiting for transfers between devices, per_device(): both = lax.all_gather(jnp.concatenate([late, early], 1), TPA, axis=0)  88.3 us
    psum x2, waiting for transfers between devices, layer_forward(): lax.psum(dot(mixed, w['wr'][:XW + HD]).astype(BF), TPA).astype(F32)  81.1 us
    psum x2, waiting for transfers between devices, layer_backward(): g_n2 = lax.psum(part_2, TPA).astype(F32)  63.2 us
    unnamed x327, local copies, waits for them, and re-layouts  58.5 us
    psum x1, waiting for transfers between devices, layer_backward(): g_n1 = lax.psum(part_1, TPA).astype(F32)  52.6 us
    psum x1, waiting for transfers between devices, per_device(): lax.psum(dot(act, weights[layer]['wr'][XW + HD:]).astype(BF), TPA)  42.6 us
  transfers between devices with their start and end apart: 78, of which 25 were waited for; matrix products, arithmetic and copies ran while one was open for 25% of the time, Pallas kernels for 8%

profile of v3, /device:TPU:0, one launch (start us, length us, event | category | flops | bytes accessed | tf_op | source)
XLA Modules:
  0.0 1067.8 jit_solution(17513520955659474051)
XLA Ops:
  8.9 4.0 collective-permute-start.9
  13.5 4.0 collective-permute-start.2
  48.3 6.1 concatenate.136
  63.2 9.0 concatenate.141
  92.1 8.9 collective-permute-done.4
  107.6 5.1 fusion.99.p_ref.prev_ref
  112.7 9.1 ssd_forward.2
  124.7 6.0 collective-permute-start.13
  131.4 5.1 attn_forward.2
  144.2 6.1 collective-permute-done.15
  152.4 6.0 collective-permute-done.16
  175.8 3.6 collective-permute-start.33
  183.0 10.0 collective-permute-done.32
  199.4 19.0 %collective-permute-start.30 = (bf16[144,1024]{1,0:T(8,128)(2,1)}, bf16[144,1024]{1,0:T(8,128)(2,1)}, u32[]{:S(2)}, u32[]{:S(2)}) collective-permute-start(bf16[144,1024]{1,0:T(8,128)(2,1)} %collective-permute-done.28), channel_id=1, source_target_pairs={{0,16},{8,24},{16,0},{24,8},{1,17},{9,25},{17,1},{25,9},{2,18},{10... | collective-permute-start | bytes 884744 | tf_op jit(solution)/shard_map/ppermute | solution.py:57
  218.5 4.8 collective-permute-start.29
  223.3 33.0 %all-reduce.10.cloned.1.call-done = bf16[1024,1024]{0,1:T(8,128)(2,1)} async-done(((bf16[1024,1024]{0,1:T(8,128)(2,1)}), bf16[1024,1024]{0,1:T(8,128)(2,1)}) %all-reduce.10.cloned.1.call-update) | async-done | bytes 2097168 | tf_op jit(solution)/shard_map/psum | solution.py:652
  256.3 3.7 multiply_reduce_fusion.9
  260.0 3.4 fusion.100
  279.3 9.6 collective-permute-done.23
  289.8 42.6 %all-reduce.12.cloned.1.call-done = bf16[1024,1024]{0,1:T(8,128)(2,1)} async-done(((bf16[1024,1024]{0,1:T(8,128)(2,1)}), bf16[1024,1024]{0,1:T(8,128)(2,1)}) %all-reduce.12.cloned.1.call-update) | async-done | bytes 2097168 | tf_op jit(solution)/shard_map/psum | solution.py:927
  332.4 3.7 multiply_reduce_fusion.8
  336.1 8.2 fusion.101.p_ref.prev_ref
  344.3 9.1 ssd_forward.3
  360.9 5.1 attn_forward.3
  381.2 6.1 fusion.2
  387.4 48.1 %all-reduce.14.cloned.1.call-done = bf16[1024,1024]{0,1:T(8,128)(2,1)} async-done(((bf16[1024,1024]{0,1:T(8,128)(2,1)}), bf16[1024,1024]{0,1:T(8,128)(2,1)}) %all-reduce.14.cloned.1.call-update) | async-done | bytes 2097168 | tf_op jit(solution)/shard_map/psum | solution.py:652
  435.5 3.7 multiply_reduce_fusion.7
  439.3 3.6 fusion.102
  446.2 3.8 convolution_convert_fusion.7
  450.1 4.6 convolution_convert_fusion.8
  454.9 5.4 copy.303
  460.3 54.4 %all-reduce.16.cloned.1.call-done = bf16[1024,1024]{0,1:T(8,128)(2,1)} async-done(((bf16[1024,1024]{0,1:T(8,128)(2,1)}), bf16[1024,1024]{0,1:T(8,128)(2,1)}) %all-reduce.16.cloned.1.call-update) | async-done | bytes 2097168 | tf_op jit(solution)/shard_map/psum | solution.py:678
  514.8 5.5 multiply_reduce_fusion.2
  542.5 19.4 %ssd_backward.2 = (bf16[1024,1152]{1,0:T(8,128)(2,1)}, f32[8,448]{1,0:T(8,128)S(1)}, f32[8,256]{1,0:T(8,128)S(1)}) custom-call(f32[1024,1152]{1,0:T(8,128)} %fusion.101.p_ref.prev_ref, f32[1024,1152]{1,0:T(8,128)} %fusion.101.p_ref.prev_ref, f32[1024,16]{1,0:T(8,128)S(1)} %copy.294.meta_ref, f32[4,1,256]{2,1,0:T(1,128)S(1)} %bitcast.232, ...), custom_call_target="tpu_custom_call" | custom-call | flops 1572864000 | bytes 9216000 | tf_op jit(solution)/shard_map/ssd_backward/pallas_call | solution.py:379
  563.1 6.9 attn_backward.2
  570.0 6.6 convolution_convert_fusion.3
  588.8 52.6 %all-reduce.18.cloned.1.call-done = bf16[1024,1024]{0,1:T(8,128)(2,1)} async-done(((bf16[1024,1024]{0,1:T(8,128)(2,1)}), bf16[1024,1024]{0,1:T(8,128)(2,1)}) %all-reduce.18.cloned.1.call-update) | async-done | bytes 2097168 | tf_op jit(solution)/shard_map/psum | solution.py:699
  641.4 4.9 multiply_reduce_fusion.3
  653.6 3.8 convolution_convert_fusion.6
  661.3 6.1 convolution_convert_fusion.1
  668.7 29.6 %collective-permute-start.51 = (bf16[256,1152]{1,0:T(8,128)(2,1)}, bf16[256,1152]{1,0:T(8,128)(2,1)S(1)}, u32[]{:S(2)}, u32[]{:S(2)}) collective-permute-start(bf16[256,1152]{1,0:T(8,128)(2,1)} %get-tuple-element.333), channel_id=1, source_target_pairs={{0,8},{8,0},{16,24},{24,16},{1,9},{9,1},{17,25},{25,17},{2,10},{10... | collective-permute-start | bytes 1769480 | tf_op jit(solution)/shard_map/ppermute | solution.py:57
  705.3 7.5 collective-permute-done.51
  714.8 6.6 collective-permute-done.53
  727.5 8.8 all-reduce.20.cloned.1.call-done
  736.3 5.5 multiply_reduce_fusion
  764.8 19.4 %ssd_backward.3 = (bf16[1024,1152]{1,0:T(8,128)(2,1)}, f32[8,448]{1,0:T(8,128)S(1)}, f32[8,256]{1,0:T(8,128)S(1)}) custom-call(f32[1024,1152]{1,0:T(8,128)} %fusion.99.p_ref.prev_ref, f32[1024,1152]{1,0:T(8,128)} %fusion.99.p_ref.prev_ref, f32[1024,16]{1,0:T(8,128)S(1)} %copy.294.meta_ref, f32[4,1,256]{2,1,0:T(1,128)S(1)} %bitcast.234, ...), custom_call_target="tpu_custom_call" | custom-call | flops 1572864000 | bytes 9216000 | tf_op jit(solution)/shard_map/ssd_backward/pallas_call | solution.py:379
  785.4 6.6 attn_backward.3
  792.0 6.8 copy.318
  798.8 8.7 convolution_convert_fusion.2
  809.6 5.8 multiply_reduce_fusion.1
  819.0 5.9 convolution_convert_fusion
  830.0 12.9 %collective-permute-done.57 = bf16[256,1152]{1,0:T(8,128)(2,1)} collective-permute-done((bf16[256,1152]{1,0:T(8,128)(2,1)}, bf16[256,1152]{1,0:T(8,128)(2,1)}, u32[]{:S(2)}, u32[]{:S(2)}) %collective-permute-start.57) | collective-permute-done | bytes 589856 | tf_op jit(solution)/shard_map/ppermute | solution.py:57
  842.8 11.1 %collective-permute-done.59 = bf16[256,1152]{1,0:T(8,128)(2,1)} collective-permute-done((bf16[256,1152]{1,0:T(8,128)(2,1)}, bf16[256,1152]{1,0:T(8,128)(2,1)}, u32[]{:S(2)}, u32[]{:S(2)}) %collective-permute-start.59) | collective-permute-done | bytes 589856 | tf_op jit(solution)/shard_map/ppermute | solution.py:57
  858.2 3.1 convolution_convert_fusion.15
  869.5 12.1 %collective-permute-done.63 = bf16[256,1088]{0,1:T(8,128)(2,1)S(1)} collective-permute-done((bf16[256,1088]{0,1:T(8,128)(2,1)S(1)}, bf16[256,1088]{0,1:T(8,128)(2,1)S(1)}, u32[]{:S(2)}, u32[]{:S(2)}) %collective-permute-start.63) | collective-permute-done | bytes 557088 | tf_op jit(solution)/shard_map/ppermute | solution.py:57
  881.6 6.9 collective-permute-done.65
  894.0 5.5 fusion.10
  901.8 3.8 assemble.6
  906.8 5.5 fusion.11
  912.3 13.2 %all-gather.9.cloned.1.call-done = bf16[2048,1152]{1,0:T(8,128)(2,1)} async-done(((bf16[256,1152]{1,0:T(8,128)(2,1)}), bf16[2048,1152]{1,0:T(8,128)(2,1)}) %all-gather.9.cloned.1.call-update) | async-done | bytes 4718608 | tf_op jit(solution)/shard_map/all_gather | solution.py:990
  930.0 88.3 %all-gather.11.cloned.1.call-done = bf16[2048,2304]{1,0:T(8,128)(2,1)} async-done(((bf16[256,2304]{1,0:T(8,128)(2,1)}), bf16[2048,2304]{1,0:T(8,128)(2,1)}) %all-gather.11.cloned.1.call-update) | async-done | bytes 9437200 | tf_op jit(solution)/shard_map/all_gather | solution.py:988
  1019.6 8.5 fusion.106
  1042.0 7.9 copy.329
  1057.0 3.8 assemble.7
  (790 shorter events, 296.4 us)
Async XLA Ops:
  7.2 249.1 %all-reduce.10.cloned.1.call-start = ((), (), s32[]{:S(2)}) async-start(), calls=%async_computation.2 | async-start | bytes 4194304 | tf_op jit(solution)/shard_map/psum | solution.py:652
  8.9 68.4 %collective-permute-start.9 = (bf16[1,2,3154]{2,1,0:T(2,128)(2,1)S(1)}, bf16[1,2,3154]{2,1,0:T(2,128)(2,1)}, u32[]{:S(2)}, u32[]{:S(2)}) collective-permute-start(bf16[1,2,3154]{2,1,0:T(2,128)(2,1)S(1)} %bitcast.252), channel_id=1, source_target_pairs={{0,24},{8,16},{16,8},{24,0},{1,25},{9,17},{17,9},{25,1},{2,26},{10... | collective-permute-start | bytes 37856 | tf_op jit(solution)/shard_map/ppermute | solution.py:57
  12.9 60.8 %collective-permute-start.8 = (bf16[1,2,3154]{2,1,0:T(2,128)(2,1)S(1)}, bf16[1,2,3154]{2,1,0:T(2,128)(2,1)}, u32[]{:S(2)}, u32[]{:S(2)}) collective-permute-start(bf16[1,2,3154]{2,1,0:T(2,128)(2,1)S(1)} %bitcast.253), channel_id=1, source_target_pairs={{0,16},{8,24},{16,0},{24,8},{1,17},{9,25},{17,1},{25,9},{2,18},{10... | collective-permute-start | bytes 37856 | tf_op jit(solution)/shard_map/ppermute | solution.py:57
  13.4 58.8 %collective-permute-start.7 = (bf16[1,2,3154]{2,1,0:T(2,128)(2,1)S(1)}, bf16[1,2,3154]{2,1,0:T(2,128)(2,1)}, u32[]{:S(2)}, u32[]{:S(2)}) collective-permute-start(bf16[1,2,3154]{2,1,0:T(2,128)(2,1)S(1)} %bitcast.254), channel_id=1, source_target_pairs={{0,8},{8,0},{16,24},{24,16},{1,9},{9,1},{17,25},{25,17},{2,10},{10... | collective-permute-start | bytes 37856 | tf_op jit(solution)/shard_map/ppermute | solution.py:57
  13.5 72.8 %collective-permute-start.2 = (bf16[128,1024]{1,0:T(8,128)(2,1)}, bf16[128,1024]{1,0:T(8,128)(2,1)}, u32[]{:S(2)}, u32[]{:S(2)}) collective-permute-start(bf16[128,1024]{1,0:T(8,128)(2,1)} %param.28), channel_id=1, source_target_pairs={{0,6},{2,4},{4,2},{6,0},{1,7},{3,5},{5,3},{7,1},{8,14},{10,12},{12... | collective-permute-start | bytes 786440 | tf_op jit(solution)/shard_map/ppermute | solution.py:57
  17.5 69.1 %collective-permute-start.1 = (bf16[128,1024]{1,0:T(8,128)(2,1)}, bf16[128,1024]{1,0:T(8,128)(2,1)}, u32[]{:S(2)}, u32[]{:S(2)}) collective-permute-start(bf16[128,1024]{1,0:T(8,128)(2,1)} %param.28), channel_id=1, source_target_pairs={{0,4},{2,6},{4,0},{6,2},{1,5},{3,7},{5,1},{7,3},{8,12},{10,14},{12... | collective-permute-start | bytes 786440 | tf_op jit(solution)/shard_map/ppermute | solution.py:57
  72.1 14.5 %collective-permute-start = (bf16[128,1024]{1,0:T(8,128)(2,1)S(1)}, bf16[128,1024]{1,0:T(8,128)(2,1)S(1)}, u32[]{:S(2)}, u32[]{:S(2)}) collective-permute-start(bf16[128,1024]{1,0:T(8,128)(2,1)S(1)} %copy-done.70), channel_id=1, source_target_pairs={{0,2},{2,0},{4,6},{6,4},{1,3},{3,1},{5,7},{7,5},{8,10},{10,8},{12,... | collective-permute-start | bytes 786440 | tf_op jit(solution)/shard_map/ppermute | solution.py:57
  73.6 28.7 %collective-permute-start.6 = (bf16[256,1152]{0,1:T(8,128)(2,1)S(1)}, bf16[256,1152]{0,1:T(8,128)(2,1)S(1)}, u32[]{:S(2)}, u32[]{:S(2)}) collective-permute-start(bf16[256,1152]{0,1:T(8,128)(2,1)S(1)} %concatenate.136), channel_id=1, source_target_pairs={{0,24},{8,16},{16,8},{24,0},{1,25},{9,17},{17,9},{25,1},{2,26},{10... | collective-permute-start | bytes 1769480 | tf_op jit(solution)/shard_map/ppermute | solution.py:57
  77.3 23.8 %collective-permute-start.4 = (bf16[256,1152]{0,1:T(8,128)(2,1)S(1)}, bf16[256,1152]{0,1:T(8,128)(2,1)}, u32[]{:S(2)}, u32[]{:S(2)}) collective-permute-start(bf16[256,1152]{0,1:T(8,128)(2,1)S(1)} %concatenate.136), channel_id=1, source_target_pairs={{0,8},{8,0},{16,24},{24,16},{1,9},{9,1},{17,25},{25,17},{2,10},{10... | collective-permute-start | bytes 1769480 | tf_op jit(solution)/shard_map/ppermute | solution.py:57
  86.3 16.0 %collective-permute-start.5 = (bf16[256,1152]{0,1:T(8,128)(2,1)S(1)}, bf16[256,1152]{0,1:T(8,128)(2,1)S(1)}, u32[]{:S(2)}, u32[]{:S(2)}) collective-permute-start(bf16[256,1152]{0,1:T(8,128)(2,1)S(1)} %concatenate.136), channel_id=1, source_target_pairs={{0,16},{8,24},{16,0},{24,8},{1,17},{9,25},{17,1},{25,9},{2,18},{10... | collective-permute-start | bytes 1769480 | tf_op jit(solution)/shard_map/ppermute | solution.py:57
  88.0 14.4 %collective-permute-start.3 = (bf16[512,1024]{1,0:T(8,128)(2,1)S(1)}, bf16[512,1024]{1,0:T(8,128)(2,1)S(1)}, u32[]{:S(2)}, u32[]{:S(2)}) collective-permute-start(bf16[512,1024]{1,0:T(8,128)(2,1)S(1)} %pad_maximum_fusion.2), channel_id=1, source_target_pairs={{0,1},{1,0},{2,3},{3,2},{4,5},{5,4},{6,7},{7,6},{8,9},{9,8},{10,11... | collective-permute-start | bytes 3145736 | tf_op jit(solution)/shard_map/ppermute | solution.py:57
  102.5 78.5 %collective-permute-start.20 = (bf16[256,512]{1,0:T(8,128)(2,1)}, bf16[256,512]{1,0:T(8,128)(2,1)}, u32[]{:S(2)}, u32[]{:S(2)}) collective-permute-start(bf16[256,512]{1,0:T(8,128)(2,1)} %pad_maximum_fusion.19), channel_id=1, source_target_pairs={{0,24},{8,16},{16,8},{24,0},{1,25},{9,17},{17,9},{25,1},{2,26},{10... | collective-permute-start | bytes 786440 | tf_op jit(solution)/shard_map/ppermute | solution.py:57
  104.0 35.6 %collective-permute-start.14 = (bf16[144,1024]{1,0:T(8,128)(2,1)S(1)}, bf16[144,1024]{1,0:T(8,128)(2,1)S(1)}, u32[]{:S(2)}, u32[]{:S(2)}) collective-permute-start(bf16[144,1024]{1,0:T(8,128)(2,1)S(1)} %copy-done.107), channel_id=1, source_target_pairs={{0,0},{1,1},{2,8},{3,9},{4,16},{5,17},{6,24},{7,25},{8,2},{9,3},{1... | collective-permute-start | bytes 884744 | tf_op jit(solution)/shard_map/ppermute | solution.py:870
  124.7 11.9 %collective-permute-start.13 = (f32[4,1,256]{2,1,0:T(1,128)S(1)}, f32[4,1,256]{2,1,0:T(1,128)S(1)}, u32[]{:S(2)}, u32[]{:S(2)}) collective-permute-start(f32[4,1,256]{2,1,0:T(1,128)S(1)} %add.590), channel_id=1, source_target_pairs={{0,6},{2,4},{4,2},{6,0},{1,7},{3,5},{5,3},{7,1},{8,14},{10,12},{12... | collective-permute-start | bytes 12296 | tf_op jit(solution)/shard_map/ppermute | solution.py:57
  130.8 8.8 collective-permute-start.12
  130.8 8.8 collective-permute-start.11
  136.6 39.1 %collective-permute-start.19 = (bf16[256,512]{1,0:T(8,128)(2,1)}, bf16[256,512]{1,0:T(8,128)(2,1)}, u32[]{:S(2)}, u32[]{:S(2)}) collective-permute-start(bf16[256,512]{1,0:T(8,128)(2,1)} %pad_maximum_fusion.19), channel_id=1, source_target_pairs={{0,16},{8,24},{16,0},{24,8},{1,17},{9,25},{17,1},{25,9},{2,18},{10... | collective-permute-start | bytes 786440 | tf_op jit(solution)/shard_map/ppermute | solution.py:57
  139.6 18.8 %collective-permute-start.16 = (bf16[144,1024]{1,0:T(8,128)(2,1)S(1)}, bf16[144,1024]{1,0:T(8,128)(2,1)S(1)}, u32[]{:S(2)}, u32[]{:S(2)}) collective-permute-start(bf16[144,1024]{1,0:T(8,128)(2,1)S(1)} %collective-permute-done.14), channel_id=1, source_target_pairs={{0,16},{8,24},{16,0},{24,8},{1,17},{9,25},{17,1},{25,9},{2,18},{10... | collective-permute-start | bytes 884744 | tf_op jit(solution)/shard_map/ppermute | solution.py:57
  139.7 10.6 collective-permute-start.15
  142.6 18.5 %collective-permute-start.17 = (bf16[144,1024]{1,0:T(8,128)(2,1)S(1)}, bf16[144,1024]{1,0:T(8,128)(2,1)S(1)}, u32[]{:S(2)}, u32[]{:S(2)}) collective-permute-start(bf16[144,1024]{1,0:T(8,128)(2,1)S(1)} %collective-permute-done.14), channel_id=1, source_target_pairs={{0,24},{8,16},{16,8},{24,0},{1,25},{9,17},{17,9},{25,1},{2,26},{10... | collective-permute-start | bytes 884744 | tf_op jit(solution)/shard_map/ppermute | solution.py:57
  150.3 23.3 %collective-permute-start.18 = (bf16[256,512]{1,0:T(8,128)(2,1)}, bf16[256,512]{1,0:T(8,128)(2,1)}, u32[]{:S(2)}, u32[]{:S(2)}) collective-permute-start(bf16[256,512]{1,0:T(8,128)(2,1)} %pad_maximum_fusion.19), channel_id=1, source_target_pairs={{0,8},{8,0},{16,24},{24,16},{1,9},{9,1},{17,25},{25,17},{2,10},{10... | collective-permute-start | bytes 786440 | tf_op jit(solution)/shard_map/ppermute | solution.py:57
  158.3 38.9 %collective-permute-start.34 = (bf16[128,1024]{1,0:T(8,128)(2,1)}, bf16[128,1024]{1,0:T(8,128)(2,1)}, u32[]{:S(2)}, u32[]{:S(2)}) collective-permute-start(bf16[128,1024]{1,0:T(8,128)(2,1)} %param.47), channel_id=1, source_target_pairs={{0,6},{2,4},{4,2},{6,0},{1,7},{3,5},{5,3},{7,1},{8,14},{10,12},{12... | collective-permute-start | bytes 786440 | tf_op jit(solution)/shard_map/ppermute | solution.py:57
  161.1 216.2 %collective-permute-start.38 = (bf16[256,512]{1,0:T(8,128)(2,1)S(1)}, bf16[256,512]{1,0:T(8,128)(2,1)}, u32[]{:S(2)}, u32[]{:S(2)}) collective-permute-start(bf16[256,512]{1,0:T(8,128)(2,1)S(1)} %copy-done.98), channel_id=1, source_target_pairs={{0,24},{8,16},{16,8},{24,0},{1,25},{9,17},{17,9},{25,1},{2,26},{10... | collective-permute-start | bytes 786440 | tf_op jit(solution)/shard_map/ppermute | solution.py:57
  165.4 167.0 %all-reduce.12.cloned.1.call-start = ((), (), s32[]{:S(2)}) async-start(), calls=%async_computation.3 | async-start | bytes 4194304 | tf_op jit(solution)/shard_map/psum | solution.py:927
  173.6 19.4 %collective-permute-start.32 = (bf16[128,1024]{1,0:T(8,128)(2,1)}, bf16[128,1024]{1,0:T(8,128)(2,1)S(1)}, u32[]{:S(2)}, u32[]{:S(2)}) collective-permute-start(bf16[128,1024]{1,0:T(8,128)(2,1)} %param.47), channel_id=1, source_target_pairs={{0,2},{2,0},{4,6},{6,4},{1,3},{3,1},{5,7},{7,5},{8,10},{10,8},{12,... | collective-permute-start | bytes 786440 | tf_op jit(solution)/shard_map/ppermute | solution.py:57
  175.8 19.5 %collective-permute-start.33 = (bf16[128,1024]{1,0:T(8,128)(2,1)}, bf16[128,1024]{1,0:T(8,128)(2,1)S(1)}, u32[]{:S(2)}, u32[]{:S(2)}) collective-permute-start(bf16[128,1024]{1,0:T(8,128)(2,1)} %param.47), channel_id=1, source_target_pairs={{0,4},{2,6},{4,0},{6,2},{1,5},{3,7},{5,1},{7,3},{8,12},{10,14},{12... | collective-permute-start | bytes 786440 | tf_op jit(solution)/shard_map/ppermute | solution.py:57
  181.0 96.4 %collective-permute-start.22 = (bf16[256,1152]{0,1:T(8,128)(2,1)}, bf16[256,1152]{0,1:T(8,128)(2,1)}, u32[]{:S(2)}, u32[]{:S(2)}) collective-permute-start(bf16[256,1152]{0,1:T(8,128)(2,1)} %concatenate.141), channel_id=1, source_target_pairs={{0,16},{8,24},{16,0},{24,8},{1,17},{9,25},{17,1},{25,9},{2,18},{10... | collective-permute-start | bytes 1769480 | tf_op jit(solution)/shard_map/ppermute | solution.py:57
  195.3 78.7 %collective-permute-start.21 = (bf16[256,1152]{0,1:T(8,128)(2,1)}, bf16[256,1152]{0,1:T(8,128)(2,1)}, u32[]{:S(2)}, u32[]{:S(2)}) collective-permute-start(bf16[256,1152]{0,1:T(8,128)(2,1)} %concatenate.141), channel_id=1, source_target_pairs={{0,8},{8,0},{16,24},{24,16},{1,9},{9,1},{17,25},{25,17},{2,10},{10... | collective-permute-start | bytes 1769480 | tf_op jit(solution)/shard_map/ppermute | solution.py:57
  199.4 72.0 %collective-permute-start.30 = (bf16[144,1024]{1,0:T(8,128)(2,1)}, bf16[144,1024]{1,0:T(8,128)(2,1)}, u32[]{:S(2)}, u32[]{:S(2)}) collective-permute-start(bf16[144,1024]{1,0:T(8,128)(2,1)} %collective-permute-done.28), channel_id=1, source_target_pairs={{0,16},{8,24},{16,0},{24,8},{1,17},{9,25},{17,1},{25,9},{2,18},{10... | collective-permute-start | bytes 884744 | tf_op jit(solution)/shard_map/ppermute | solution.py:57
  218.5 50.4 %collective-permute-start.29 = (bf16[144,1024]{1,0:T(8,128)(2,1)}, bf16[144,1024]{1,0:T(8,128)(2,1)}, u32[]{:S(2)}, u32[]{:S(2)}) collective-permute-start(bf16[144,1024]{1,0:T(8,128)(2,1)} %collective-permute-done.28), channel_id=1, source_target_pairs={{0,8},{8,0},{16,24},{24,16},{1,9},{9,1},{17,25},{25,17},{2,10},{10... | collective-permute-start | bytes 884744 | tf_op jit(solution)/shard_map/ppermute | solution.py:57
  267.7 167.8 %all-reduce.14.cloned.1.call-start = ((), (), s32[]{:S(2)}) async-start(), calls=%async_computation.4 | async-start | bytes 4194304 | tf_op jit(solution)/shard_map/psum | solution.py:652
  268.9 106.7 %collective-permute-start.37 = (bf16[256,512]{1,0:T(8,128)(2,1)S(1)}, bf16[256,512]{1,0:T(8,128)(2,1)}, u32[]{:S(2)}, u32[]{:S(2)}) collective-permute-start(bf16[256,512]{1,0:T(8,128)(2,1)S(1)} %copy-done.98), channel_id=1, source_target_pairs={{0,16},{8,24},{16,0},{24,8},{1,17},{9,25},{17,1},{25,9},{2,18},{10... | collective-permute-start | bytes 786440 | tf_op jit(solution)/shard_map/ppermute | solution.py:57
  271.4 17.5 %collective-permute-start.23 = (bf16[256,1152]{0,1:T(8,128)(2,1)}, bf16[256,1152]{0,1:T(8,128)(2,1)S(1)}, u32[]{:S(2)}, u32[]{:S(2)}) collective-permute-start(bf16[256,1152]{0,1:T(8,128)(2,1)} %concatenate.141), channel_id=1, source_target_pairs={{0,24},{8,16},{16,8},{24,0},{1,25},{9,17},{17,9},{25,1},{2,26},{10... | collective-permute-start | bytes 1769480 | tf_op jit(solution)/shard_map/ppermute | solution.py:57
  274.0 81.2 %collective-permute-start.31 = (bf16[144,1024]{1,0:T(8,128)(2,1)}, bf16[144,1024]{1,0:T(8,128)(2,1)}, u32[]{:S(2)}, u32[]{:S(2)}) collective-permute-start(bf16[144,1024]{1,0:T(8,128)(2,1)} %collective-permute-done.28), channel_id=1, source_target_pairs={{0,24},{8,16},{16,8},{24,0},{1,25},{9,17},{17,9},{25,1},{2,26},{10... | collective-permute-start | bytes 884744 | tf_op jit(solution)/shard_map/ppermute | solution.py:57
  356.4 9.7 collective-permute-start.27
  358.6 9.1 collective-permute-start.26
  367.6 11.3 %collective-permute-start.35 = (bf16[512,1024]{1,0:T(8,128)(2,1)}, bf16[512,1024]{1,0:T(8,128)(2,1)}, u32[]{:S(2)}, u32[]{:S(2)}) collective-permute-start(bf16[512,1024]{1,0:T(8,128)(2,1)} %pad_maximum_fusion.3), channel_id=1, source_target_pairs={{0,1},{1,0},{2,3},{3,2},{4,5},{5,4},{6,7},{7,6},{8,9},{9,8},{10,11... | collective-permute-start | bytes 3145736 | tf_op jit(solution)/shard_map/ppermute | solution.py:57
  371.5 143.3 %all-reduce.16.cloned.1.call-start = ((), (), s32[]{:S(2)}) async-start(), calls=%async_computation.5 | async-start | bytes 4194304 | tf_op jit(solution)/shard_map/psum | solution.py:678
  450.0 120.0 %reduce-scatter.3.cloned.1.call-start = ((), (), s32[]{:S(2)}) async-start(), calls=%async_computation.6 | async-start | bytes 2359296 | tf_op jit(solution)/shard_map/reduce_scatter | solution.py:933
  454.7 186.7 %all-reduce.18.cloned.1.call-start = ((), (), s32[]{:S(2)}) async-start(), calls=%async_computation.7 | async-start | bytes 4194304 | tf_op jit(solution)/shard_map/psum | solution.py:699
  576.7 159.5 %all-reduce.20.cloned.1.call-start = ((), (), s32[]{:S(2)}) async-start(), calls=%async_computation.8 | async-start | bytes 4194304 | tf_op jit(solution)/shard_map/psum | solution.py:678
  585.3 72.2 %collective-permute-start.47 = (bf16[256,1088]{0,1:T(8,128)(2,1)}, bf16[256,1088]{0,1:T(8,128)(2,1)S(1)}, u32[]{:S(2)}, u32[]{:S(2)}) collective-permute-start(bf16[256,1088]{0,1:T(8,128)(2,1)} %get-tuple-element.339), channel_id=1, source_target_pairs={{0,8},{8,0},{16,24},{24,16},{1,9},{9,1},{17,25},{25,17},{2,10},{10... | collective-permute-start | bytes 1671176 | tf_op jit(solution)/shard_map/ppermute | solution.py:57
  586.9 70.7 %collective-permute-start.49 = (bf16[256,1088]{0,1:T(8,128)(2,1)}, bf16[256,1088]{0,1:T(8,128)(2,1)}, u32[]{:S(2)}, u32[]{:S(2)}) collective-permute-start(bf16[256,1088]{0,1:T(8,128)(2,1)} %get-tuple-element.340), channel_id=1, source_target_pairs={{0,24},{8,16},{16,8},{24,0},{1,25},{9,17},{17,9},{25,1},{2,26},{10... | collective-permute-start | bytes 1671176 | tf_op jit(solution)/shard_map/ppermute | solution.py:57
  588.3 69.2 %collective-permute-start.48 = (bf16[256,1088]{0,1:T(8,128)(2,1)S(1)}, bf16[256,1088]{0,1:T(8,128)(2,1)}, u32[]{:S(2)}, u32[]{:S(2)}) collective-permute-start(bf16[256,1088]{0,1:T(8,128)(2,1)S(1)} %get-tuple-element.341), channel_id=1, source_target_pairs={{0,16},{8,24},{16,0},{24,8},{1,17},{9,25},{17,1},{25,9},{2,18},{10... | collective-permute-start | bytes 1671176 | tf_op jit(solution)/shard_map/ppermute | solution.py:57
  657.4 134.6 %all-gather.7.cloned.1.call-start = ((), (), s32[]{:S(2)}) async-start(), calls=%async_computation.10 | async-start | bytes 5308416 | tf_op jit(solution)/shard_map/all_gather | solution.py:982
  660.9 244.8 %reduce-scatter.5.cloned.1.call-start = ((), (), s32[]{:S(2)}) async-start(), calls=%async_computation.9 | async-start | bytes 2359296 | tf_op jit(solution)/shard_map/reduce_scatter | solution.py:968
  668.7 44.1 %collective-permute-start.51 = (bf16[256,1152]{1,0:T(8,128)(2,1)}, bf16[256,1152]{1,0:T(8,128)(2,1)S(1)}, u32[]{:S(2)}, u32[]{:S(2)}) collective-permute-start(bf16[256,1152]{1,0:T(8,128)(2,1)} %get-tuple-element.333), channel_id=1, source_target_pairs={{0,8},{8,0},{16,24},{24,16},{1,9},{9,1},{17,25},{25,17},{2,10},{10... | collective-permute-start | bytes 1769480 | tf_op jit(solution)/shard_map/ppermute | solution.py:57
  698.4 23.1 %collective-permute-start.53 = (bf16[256,1152]{1,0:T(8,128)(2,1)}, bf16[256,1152]{1,0:T(8,128)(2,1)}, u32[]{:S(2)}, u32[]{:S(2)}) collective-permute-start(bf16[256,1152]{1,0:T(8,128)(2,1)} %get-tuple-element.334), channel_id=1, source_target_pairs={{0,24},{8,16},{16,8},{24,0},{1,25},{9,17},{17,9},{25,1},{2,26},{10... | collective-permute-start | bytes 1769480 | tf_op jit(solution)/shard_map/ppermute | solution.py:57
  698.4 25.3 %collective-permute-start.52 = (bf16[256,1152]{1,0:T(8,128)(2,1)S(1)}, bf16[256,1152]{1,0:T(8,128)(2,1)}, u32[]{:S(2)}, u32[]{:S(2)}) collective-permute-start(bf16[256,1152]{1,0:T(8,128)(2,1)S(1)} %get-tuple-element.335), channel_id=1, source_target_pairs={{0,16},{8,24},{16,0},{24,8},{1,17},{9,25},{17,1},{25,9},{2,18},{10... | collective-permute-start | bytes 1769480 | tf_op jit(solution)/shard_map/ppermute | solution.py:57
  701.9 24.9 %collective-permute-start.56 = (f32[4489]{0:T(1024)S(1)}, f32[4489]{0:T(1024)S(1)}, u32[]{:S(2)}, u32[]{:S(2)}) collective-permute-start(f32[4489]{0:T(1024)S(1)} %concatenate.163), channel_id=1, source_target_pairs={{0,24},{8,16},{16,8},{24,0},{1,25},{9,17},{17,9},{25,1},{2,26},{10... | collective-permute-start | bytes 53876 | tf_op jit(solution)/shard_map/ppermute | solution.py:57
  703.3 23.5 %collective-permute-start.55 = (f32[4489]{0:T(1024)S(1)}, f32[4489]{0:T(1024)S(1)}, u32[]{:S(2)}, u32[]{:S(2)}) collective-permute-start(f32[4489]{0:T(1024)S(1)} %concatenate.163), channel_id=1, source_target_pairs={{0,16},{8,24},{16,0},{24,8},{1,17},{9,25},{17,1},{25,9},{2,18},{10... | collective-permute-start | bytes 53876 | tf_op jit(solution)/shard_map/ppermute | solution.py:57
  712.8 14.0 %collective-permute-start.54 = (f32[4489]{0:T(1024)S(1)}, f32[4489]{0:T(1024)S(1)}, u32[]{:S(2)}, u32[]{:S(2)}) collective-permute-start(f32[4489]{0:T(1024)S(1)} %concatenate.163), channel_id=1, source_target_pairs={{0,8},{8,0},{16,24},{24,16},{1,9},{9,1},{17,25},{25,17},{2,10},{10... | collective-permute-start | bytes 53876 | tf_op jit(solution)/shard_map/ppermute | solution.py:57
  749.3 8.7 collective-permute-start.46
  807.6 117.9 %all-gather.9.cloned.1.call-start = ((), (), s32[]{:S(2)}) async-start(), calls=%async_computation.11 | async-start | bytes 5308416 | tf_op jit(solution)/shard_map/all_gather | solution.py:990
  815.5 13.7 %collective-permute-start.62 = (f32[4489]{0:T(1024)S(1)}, f32[4489]{0:T(1024)S(1)}, u32[]{:S(2)}, u32[]{:S(2)}) collective-permute-start(f32[4489]{0:T(1024)S(1)} %concatenate.166), channel_id=1, source_target_pairs={{0,24},{8,16},{16,8},{24,0},{1,25},{9,17},{17,9},{25,1},{2,26},{10... | collective-permute-start | bytes 53876 | tf_op jit(solution)/shard_map/ppermute | solution.py:57
  817.9 11.8 %collective-permute-start.61 = (f32[4489]{0:T(1024)S(1)}, f32[4489]{0:T(1024)S(1)}, u32[]{:S(2)}, u32[]{:S(2)}) collective-permute-start(f32[4489]{0:T(1024)S(1)} %concatenate.166), channel_id=1, source_target_pairs={{0,16},{8,24},{16,0},{24,8},{1,17},{9,25},{17,1},{25,9},{2,18},{10... | collective-permute-start | bytes 53876 | tf_op jit(solution)/shard_map/ppermute | solution.py:57
  818.5 11.3 %collective-permute-start.60 = (f32[4489]{0:T(1024)S(1)}, f32[4489]{0:T(1024)S(1)}, u32[]{:S(2)}, u32[]{:S(2)}) collective-permute-start(f32[4489]{0:T(1024)S(1)} %concatenate.166), channel_id=1, source_target_pairs={{0,8},{8,0},{16,24},{24,16},{1,9},{9,1},{17,25},{25,17},{2,10},{10... | collective-permute-start | bytes 53876 | tf_op jit(solution)/shard_map/ppermute | solution.py:57
  826.2 16.6 %collective-permute-start.57 = (bf16[256,1152]{1,0:T(8,128)(2,1)}, bf16[256,1152]{1,0:T(8,128)(2,1)}, u32[]{:S(2)}, u32[]{:S(2)}) collective-permute-start(bf16[256,1152]{1,0:T(8,128)(2,1)} %get-tuple-element.330), channel_id=1, source_target_pairs={{0,8},{8,0},{16,24},{24,16},{1,9},{9,1},{17,25},{25,17},{2,10},{10... | collective-permute-start | bytes 1769480 | tf_op jit(solution)/shard_map/ppermute | solution.py:57
  827.7 26.2 %collective-permute-start.59 = (bf16[256,1152]{1,0:T(8,128)(2,1)}, bf16[256,1152]{1,0:T(8,128)(2,1)}, u32[]{:S(2)}, u32[]{:S(2)}) collective-permute-start(bf16[256,1152]{1,0:T(8,128)(2,1)} %get-tuple-element.331), channel_id=1, source_target_pairs={{0,24},{8,16},{16,8},{24,0},{1,25},{9,17},{17,9},{25,1},{2,26},{10... | collective-permute-start | bytes 1769480 | tf_op jit(solution)/shard_map/ppermute | solution.py:57
  829.2 26.1 %collective-permute-start.58 = (bf16[256,1152]{1,0:T(8,128)(2,1)}, bf16[256,1152]{1,0:T(8,128)(2,1)}, u32[]{:S(2)}, u32[]{:S(2)}) collective-permute-start(bf16[256,1152]{1,0:T(8,128)(2,1)} %get-tuple-element.332), channel_id=1, source_target_pairs={{0,16},{8,24},{16,0},{24,8},{1,17},{9,25},{17,1},{25,9},{2,18},{10... | collective-permute-start | bytes 1769480 | tf_op jit(solution)/shard_map/ppermute | solution.py:57
  858.2 160.1 %all-gather.11.cloned.1.call-start = ((), (), s32[]{:S(2)}) async-start(), calls=%async_computation.12 | async-start | bytes 10616832 | tf_op jit(solution)/shard_map/all_gather | solution.py:988
  866.0 15.6 %collective-permute-start.63 = (bf16[256,1088]{0,1:T(8,128)(2,1)S(1)}, bf16[256,1088]{0,1:T(8,128)(2,1)S(1)}, u32[]{:S(2)}, u32[]{:S(2)}) collective-permute-start(bf16[256,1088]{0,1:T(8,128)(2,1)S(1)} %get-tuple-element.336), channel_id=1, source_target_pairs={{0,8},{8,0},{16,24},{24,16},{1,9},{9,1},{17,25},{25,17},{2,10},{10... | collective-permute-start | bytes 1671176 | tf_op jit(solution)/shard_map/ppermute | solution.py:57
  867.4 21.1 %collective-permute-start.65 = (bf16[256,1088]{0,1:T(8,128)(2,1)S(1)}, bf16[256,1088]{0,1:T(8,128)(2,1)S(1)}, u32[]{:S(2)}, u32[]{:S(2)}) collective-permute-start(bf16[256,1088]{0,1:T(8,128)(2,1)S(1)} %get-tuple-element.337), channel_id=1, source_target_pairs={{0,24},{8,16},{16,8},{24,0},{1,25},{9,17},{17,9},{25,1},{2,26},{10... | collective-permute-start | bytes 1671176 | tf_op jit(solution)/shard_map/ppermute | solution.py:57
  867.8 22.1 %collective-permute-start.64 = (bf16[256,1088]{0,1:T(8,128)(2,1)S(1)}, bf16[256,1088]{0,1:T(8,128)(2,1)S(1)}, u32[]{:S(2)}, u32[]{:S(2)}) collective-permute-start(bf16[256,1088]{0,1:T(8,128)(2,1)S(1)} %get-tuple-element.338), channel_id=1, source_target_pairs={{0,16},{8,24},{16,0},{24,8},{1,17},{9,25},{17,1},{25,9},{2,18},{10... | collective-permute-start | bytes 1671176 | tf_op jit(solution)/shard_map/ppermute | solution.py:57
  (168 other events, 2890.7 us)
Sparse Core Ops, SparseCore 0:
  165.5 90.6 all-reduce.9
  267.8 64.5 all-reduce.11
  371.6 63.8 all-reduce.13
  450.2 64.5 all-reduce.15
  517.5 35.4 reduce-scatter.2
  576.8 64.5 all-reduce.17
  657.6 78.6 all-reduce.19
  737.8 51.9 all-gather.6
  807.7 36.4 reduce-scatter.4
  858.3 67.1 all-gather.8
  927.2 91.1 all-gather.10
